TPU v7x, 32 devices: a whole 2x2x4 slice. The times are simulated.
32 devices in a mesh: dp: 8 (over z, core), expert: 4 (over y, x).
Axes of the slice: x: 2, y: 2, z: 4, core: 2. Of those that a mesh axis runs over, the one named last changes fastest.
Arguments:
- tokens: bfloat16 [4096, 2048], P(('dp', 'expert'))
- targets: bfloat16 [4096, 2048], P(('dp', 'expert'))
- routes: int32 [4096, 8], P(('dp', 'expert')), may hold values from 0 to 15, all different within a row; in each aligned block of 128 rows (0 to 127, 128 to 255, ...) at most 64 rows name the same one
- route_logits: float32 [4096, 8], P(('dp', 'expert')), may hold values from -3 to 3
- slot_order: int32 [4096, 8], P(('dp', 'expert')), may hold values from 0 to 7, each once within a row
- seq_ids: int32 [4096], P(('dp', 'expert')), may hold values from 0 to 63, as said below
- w_gate: bfloat16 [16, 2048, 384], P('expert')
- w_up: bfloat16 [16, 2048, 384], P('expert')
- w_down: bfloat16 [2048, 16, 384], P('dp', 'expert')
Outputs:
- mixed: bfloat16 [4096, 2048], P(('dp', 'expert'))
- seq_loss: float32 [64], replicated
- dual_weight: float32 [64], replicated
- grad_down: float32 [2048, 16, 384], P('dp', 'expert')
Inputs may be any that keep to these rules, and one draw needn't show every extreme that they name: `routes`: in each aligned block of 128 rows (the rows of one device) every expert is named by exactly 64 rows; the 8 numbers of a row differ. `slot_order`: each row is a permutation of 0 to 7. `seq_ids`: sequence numbers never fall along the tokens, and every number names one or more tokens.
All inputs are finite; a program needn't handle non-finite values.
Results may differ from a plain program's by a relative error of at most 0.0046.
Values may be sent and summed in bfloat16 or wider, within the bound.
No kernel may reach another device: no remote copies, remote signals or barrier semaphores. Data moves between devices by JAX's collectives and lax.ppermute only.
A program may use at most 64 MiB of HBM per device.

v0:
```python
import jax
import jax.numpy as jnp
from jax import lax
from jax.sharding import PartitionSpec as P

NSEQ = 64
BISECT_STEPS = 40


radius_factor = 2.0


def unchanged(single_value):
    return single_value


def dual_search(seq_loss, pair_total, one_total):
    sum_total = one_total(jnp.sum(seq_loss))

    def advance(step_index, bounds):
        lower, upper = bounds
        middle = 0.5 * (lower + upper)
        excess = jnp.maximum(seq_loss - middle, 0.0)
        square_sum, plain_sum = pair_total((jnp.sum(excess * excess), jnp.sum(excess)))
        is_above = NSEQ * square_sum - radius_factor * plain_sum * plain_sum >= 0.0
        return (jnp.where(is_above, lower, middle), jnp.where(is_above, middle, upper))

    lower, upper = lax.fori_loop(0, BISECT_STEPS, advance, (-sum_total, sum_total))
    excess = jnp.maximum(seq_loss - 0.5 * (lower + upper), 0.0)
    return excess / one_total(jnp.sum(excess))


def route_gates(route_logits, slot_order):
    top_k = slot_order.shape[1]
    columns = lax.broadcasted_iota(jnp.int32, (1, 1, top_k), 2)
    picked = jnp.sum(
        jnp.where(slot_order[:, :, None] == columns, route_logits[:, None, :], 0.0), axis=2
    )
    raised = jnp.exp(picked)
    return raised / jnp.sum(raised, axis=1, keepdims=True)


def by_expert(blocks, groups):
    exp_dev = blocks.shape[0] // groups
    tail_shape = blocks.shape[1:]
    split_view = blocks.reshape((groups, exp_dev) + tail_shape)
    moved_view = jnp.swapaxes(split_view, 0, 1)
    return moved_view.reshape((exp_dev, groups * tail_shape[0]) + tail_shape[1:])


def by_source(local_rows, groups):
    exp_dev = local_rows.shape[0]
    capacity = local_rows.shape[1] // groups
    tail_shape = local_rows.shape[2:]
    split_view = local_rows.reshape((exp_dev, groups, capacity) + tail_shape)
    return jnp.swapaxes(split_view, 0, 1).reshape((exp_dev * groups, capacity) + tail_shape)


def local(tokens, targets, routes, route_logits, slot_order, seq_ids, w_gate, w_up, w_down):
    tok_rows, feat_width = tokens.shape
    top_k = routes.shape[1]
    groups = lax.axis_size("expert")
    exp_dev = w_gate.shape[0]
    experts = exp_dev * groups
    slot_count = tok_rows * top_k
    capacity = slot_count // experts
    grad_scale = float(tok_rows * lax.axis_size("dp") * groups // 8)
    flat_route = routes.reshape(slot_count)
    expert_hot = (flat_route[:, None] == lax.broadcasted_iota(jnp.int32, (1, experts), 1)).astype(
        jnp.int32
    )
    slot_rank = jnp.sum((jnp.cumsum(expert_hot, axis=0) - 1) * expert_hot, axis=1)
    slot_index = flat_route * capacity + slot_rank
    inverse = (
        jnp.zeros((slot_count,), jnp.int32).at[slot_index].set(lax.iota(jnp.int32, slot_count))
    )
    source_row = inverse // top_k
    gate_probs = route_gates(route_logits, slot_order)
    send_rows = tokens[source_row].reshape(experts, capacity, feat_width)
    arrived = lax.all_to_all(send_rows, "expert", split_axis=0, concat_axis=0, tiled=True)
    local_rows = by_expert(arrived, groups)
    gate_proj = jnp.einsum("erd,edh->erh", local_rows, w_gate, preferred_element_type=jnp.float32)
    up_proj = jnp.einsum("erd,edh->erh", local_rows, w_up, preferred_element_type=jnp.float32)
    hidden = (jax.nn.silu(gate_proj) * up_proj).astype(jnp.bfloat16)
    expert_out = jnp.einsum(
        "erh,neh->ern",
        hidden,
        lax.all_gather(w_down, "dp", axis=0, tiled=True),
        preferred_element_type=jnp.float32,
    ).astype(jnp.bfloat16)
    returned = lax.all_to_all(
        by_source(expert_out, groups), "expert", split_axis=0, concat_axis=0, tiled=True
    )
    per_slot = returned.reshape(slot_count, feat_width)[slot_index].reshape(
        tok_rows, top_k, feat_width
    )
    combined = jnp.sum(gate_probs[:, :, None] * per_slot.astype(jnp.float32), axis=1)
    error = combined - targets.astype(jnp.float32)
    error_low = error.astype(jnp.bfloat16)
    sent_error = lax.all_to_all(
        error_low[source_row].reshape(experts, capacity, feat_width),
        "expert",
        split_axis=0,
        concat_axis=0,
        tiled=True,
    )
    seq_hot = seq_ids[:, None] == lax.broadcasted_iota(jnp.int32, (1, NSEQ), 1)
    partial_sq = jnp.sum(jnp.where(seq_hot, jnp.sum(error * error, axis=1)[:, None], 0.0), axis=0)
    counts = jnp.sum(seq_hot.astype(jnp.float32), axis=0)
    seq_sq, seq_len = lax.psum((partial_sq, counts), ("dp", "expert"))
    seq_loss = seq_sq / (seq_len * feat_width)
    dual_weight = dual_search(seq_loss, unchanged, unchanged)
    seq_rate = dual_weight / seq_len
    scaled_gates = grad_scale * gate_probs
    token_rate = jnp.sum(jnp.where(seq_hot, seq_rate[None, :], 0.0), axis=1)
    flat_weight = (scaled_gates * token_rate[:, None]).reshape(slot_count)
    slot_weight = lax.all_to_all(
        flat_weight[inverse].reshape(experts, capacity),
        "expert",
        split_axis=0,
        concat_axis=0,
        tiled=True,
    )
    weight_local = by_expert(slot_weight, groups)
    error_local = by_expert(sent_error, groups)
    scaled = (weight_local[:, :, None] * hidden).astype(jnp.bfloat16)
    grad_down = lax.psum_scatter(
        jnp.einsum("ern,erh->neh", error_local, scaled, preferred_element_type=jnp.float32),
        "dp",
        scatter_dimension=0,
        tiled=True,
    )
    return (combined.astype(jnp.bfloat16), seq_loss, dual_weight, grad_down)


def solution(mesh):
    return jax.shard_map(
        local,
        mesh=mesh,
        in_specs=(
            P(("dp", "expert"), None),
            P(("dp", "expert"), None),
            P(("dp", "expert"), None),
            P(("dp", "expert"), None),
            P(("dp", "expert"), None),
            P(("dp", "expert")),
            P("expert", None, None),
            P("expert", None, None),
            P("dp", "expert", None),
        ),
        out_specs=(P(("dp", "expert"), None), P(), P(), P("dp", "expert", None)),
        check_vma=False,
    )
```

profile of v0, /device:TPU:0, one launch (start us, length us, event | category | flops | bytes accessed | tf_op | source)
XLA Modules:
  0.0 593.1 jit_solution(3862143301892139008)
XLA Ops:
  7.2 2.2 copy.54
  9.4 0.8 copy.49
  10.4 0.7 broadcast_multiply_fusion.1
  11.3 4.5 reduce-window.6
  16.3 4.3 scatter_custom_fusion
  20.6 6.1 %gather_fusion = bf16[1024,2048]{1,0:T(8,128)(2,1)} fusion(bf16[128,2048]{1,0:T(8,128)(2,1)S(1)} %copy-done, s32[1024]{0:T(1024)S(1)} %get-tuple-element.65), kind=kCustom, calls=%fused_computation | custom fusion | bytes 8392704 | tf_op jit(solution)/shard_map/gather | solution.py:79
  26.7 53.4 %all_to_all.24 = bf16[16,64,2048]{2,1,0:T(8,128)(2,1)S(1)} all-to-all(bf16[16,64,2048]{2,1,0:T(8,128)(2,1)} %bitcast.47), channel_id=1, replica_groups=mesh['dp'=8,'expert'=4] {'expert'}, dimensions={0} | all-to-all | bytes 8388608 | tf_op jit(solution)/shard_map/all_to_all | solution.py:80
  80.7 1.0 slice-done.1
  81.7 2.4 fusion.15
  84.2 2.5 multiply_convert_fusion.1
  86.7 5.2 convolution_convert_fusion
  91.9 2.5 copy.55
  94.4 5.2 all-to-all-start.1
  99.8 45.7 %all-to-all-done.1 = bf16[16,64,2048]{2,1,0:T(8,128)(2,1)} async-done(((bf16[16,64,2048]{2,1,0:T(8,128)(2,1)}), bf16[16,64,2048]{2,1,0:T(8,128)(2,1)}, u32[]{:S(2)}, u32[]{:S(2)}) %all-to-all-start.1) | async-done | bytes 4194336 | tf_op jit(solution)/shard_map/all_to_all | solution.py:91
  145.5 11.6 %gather_fusion.1 = bf16[1024,2048]{1,0:T(8,128)(2,1)} fusion(bf16[1024,2048]{1,0:T(8,128)(2,1)} %bitcast.11, s32[1024]{0:T(1024)S(1)} %broadcast_clamp_fusion), kind=kCustom, calls=%fused_computation.1 | custom fusion | bytes 8392704 | tf_op jit(solution)/shard_map/gather | solution.py:94
  157.1 6.6 %fusion.1 = f32[128,2048]{1,0:T(8,128)S(1)} fusion(bf16[1024,2048]{1,0:T(8,128)(2,1)} %gather_fusion.1, f32[128,8]{1,0:T(8,128)S(1)} %copy.47), kind=kLoop, calls=%fused_computation.9 | loop fusion | flops 6029312 | bytes 5246976 | tf_op jit(solution)/shard_map/reduce_sum | solution.py:97
  163.7 1.0 fusion.3
  164.8 39.9 %all-reduce = (f32[64]{0:T(128)S(1)}, f32[64]{0:T(128)S(1)}) all-reduce(f32[64]{0:T(128)S(1)} %get-tuple-element.48, f32[64]{0:T(128)S(1)} %get-tuple-element.47), channel_id=1, replica_groups=mesh['dp'=8,'expert'=4] {'dp','expert'}, use_global_device_ids=true, to_apply=%region_9.10 | all-reduce | flops 128 | bytes 1024 | tf_op jit(solution)/shard_map/psum | solution.py:110
  204.7 0.6 fusion.14
  205.9 170.7 %while.12 = (s32[]{:T(128)}, f32[]{:T(128)}, f32[]{:T(128)}, f32[64]{0:T(128)S(1)}, s32[]{:T(128)}, /*index=5*/f32[]{:T(128)}, f32[]{:T(128)}, f32[]{:T(128)}, f32[]{:T(128)}) while((s32[]{:T(128)}, f32[]{:T(128)}, f32[]{:T(128)}, f32[64]{0:T(128)S(1)}, s32[]{:T(128)}, /*index=5*/f32[]{:T(128)}, f32[]{:T(128)}, f32[]{:T(128)}, ...), condition=%wide.region_16.17_spmd, body=%wide.region_13.16_spmd.sunk | while | flops 329 | bytes 468 | solution.py:28
  377.9 1.2 multiply_divide_fusion
  379.4 4.5 gather_fusion.2
  384.0 0.7 reshape.181
  384.7 4.4 all-to-all-start.2
  389.1 6.0 %gather_fusion.3 = bf16[1024,2048]{1,0:T(8,128)(2,1)} fusion(bf16[128,2048]{1,0:T(8,128)(2,1)S(1)} %get-tuple-element.61, s32[1024]{0:T(1024)S(1)} %get-tuple-element.65), kind=kCustom, calls=%fused_computation.3 | custom fusion | bytes 8392704 | tf_op jit(solution)/shard_map/gather | solution.py:101
  395.1 4.9 all-to-all-start.3
  400.5 0.7 reduce
  401.4 44.8 %all-to-all-done.3 = bf16[16,64,2048]{2,1,0:T(8,128)(2,1)} async-done(((bf16[16,64,2048]{2,1,0:T(8,128)(2,1)}), bf16[16,64,2048]{2,1,0:T(8,128)(2,1)}, u32[]{:S(2)}, u32[]{:S(2)}) %all-to-all-start.3) | async-done | bytes 4194336 | tf_op jit(solution)/shard_map/all_to_all | solution.py:100
  446.2 2.5 copy.58
  448.7 6.5 %convolution_bitcast_fusion = f32[2048,4,384]{0,2,1:T(8,128)} fusion(bf16[4,256,2048]{2,1,0:T(8,128)(2,1)S(1)} %bitcast.46, bf16[4,256,384]{2,1,0:T(8,128)(2,1)S(1)} %multiply_convert_fusion.1, f32[4,256]{1,0:T(4,128)S(1)} %mul.106), kind=kOutput, calls=%fused_computation.10 | convolution fusion | flops 1611792384 | bytes 17567744 | tf_op jit(solution)/shard_map/ern,erh->neh/dot_general | solution.py:128
  455.3 128.5 %reduce-scatter.2.cloned.1.call-done = f32[256,4,384]{0,2,1:T(8,128)} async-done(((f32[2048,4,384]{0,2,1:T(8,128)}), f32[256,4,384]{0,2,1:T(8,128)}) %reduce-scatter.2.cloned.1.call-update) | async-done | bytes 1572880 | tf_op jit(solution)/shard_map/reduce_scatter | solution.py:127
  583.7 2.6 copy.60
  (102 shorter events, 27.6 us)
Async XLA Ops:
  7.2 13.5 %copy-start = (bf16[128,2048]{1,0:T(8,128)(2,1)S(1)}, bf16[128,2048]{1,0:T(8,128)(2,1)}, u32[]{:S(2)}) copy-start(bf16[128,2048]{1,0:T(8,128)(2,1)} %param.11) | copy-start | bytes 1572868
  7.2 79.5 %all-gather.2.cloned.1.call-start = ((), (), s32[]{:S(2)}) async-start(), calls=%async_computation.5 | async-start | bytes 7077888 | tf_op jit(solution)/shard_map/all_gather | solution.py:88
  26.7 54.0 %slice-start = ((s8[6291456]{0:T(1024)(128)(4,1)}), s8[4194304]{0:T(1024)(128)(4,1)S(1)}, s32[]{:S(2)}) async-start(s8[6291456]{0:T(1024)(128)(4,1)} %bitcast.59), calls=%async_computation.7 | async-start | bytes 8388608
  80.1 1.6 slice-start.1
  80.1 4.0 slice-start.2
  81.7 2.4 slice-start.3
  94.4 5.2 copy-start.4
  94.4 5.2 copy-start.5
  94.4 51.1 %all-to-all-start.1 = ((bf16[16,64,2048]{2,1,0:T(8,128)(2,1)}), bf16[16,64,2048]{2,1,0:T(8,128)(2,1)}, u32[]{:S(2)}, u32[]{:S(2)}) async-start(bf16[16,64,2048]{2,1,0:T(8,128)(2,1)} %bitcast.48), calls=%async_computation.1 | async-start | bytes 8388608 | tf_op jit(solution)/shard_map/all_to_all | solution.py:91
  157.1 6.6 %copy-start.2 = (bf16[128,2048]{1,0:T(8,128)(2,1)S(1)}, bf16[128,2048]{1,0:T(8,128)(2,1)}, u32[]{:S(2)}) copy-start(bf16[128,2048]{1,0:T(8,128)(2,1)} %param.12) | copy-start | bytes 1572868
  157.1 7.6 %copy-start.6 = (s32[128]{0:T(128)S(1)}, s32[128]{0:T(128)}, u32[]{:S(2)}) copy-start(s32[128]{0:T(128)} %param.16) | copy-start | bytes 1540
  376.7 18.4 %copy-start.3 = (f32[64]{0:T(128)}, f32[64]{0:T(128)S(1)}, u32[]{:S(2)}) copy-start(f32[64]{0:T(128)S(1)} %get-tuple-element.136) | copy-start | bytes 772
  384.7 10.4 %all-to-all-start.2 = ((f32[4,1,256]{2,1,0:T(1,128)}), f32[4,1,256]{2,1,0:T(1,128)S(1)}, u32[]{:S(2)}, u32[]{:S(2)}) async-start(f32[4,1,256]{2,1,0:T(1,128)} %reshape.181), calls=%async_computation.2 | async-start | bytes 8192 | tf_op jit(solution)/shard_map/all_to_all | solution.py:117
  395.1 51.1 %all-to-all-start.3 = ((bf16[16,64,2048]{2,1,0:T(8,128)(2,1)}), bf16[16,64,2048]{2,1,0:T(8,128)(2,1)}, u32[]{:S(2)}, u32[]{:S(2)}) async-start(bf16[16,64,2048]{2,1,0:T(8,128)(2,1)} %bitcast.45), calls=%async_computation.3 | async-start | bytes 8388608 | tf_op jit(solution)/shard_map/all_to_all | solution.py:100
  400.0 183.8 %reduce-scatter.2.cloned.1.call-start = ((), (), s32[]{:S(2)}) async-start(), calls=%async_computation.6 | async-start | bytes 14155776 | tf_op jit(solution)/shard_map/reduce_scatter | solution.py:127
  455.3 131.0 %copy-start.1 = (bf16[128,2048]{1,0:T(8,128)(2,1)S(1)}, bf16[128,2048]{1,0:T(8,128)(2,1)}, u32[]{:S(2)}) copy-start(bf16[128,2048]{1,0:T(8,128)(2,1)} %param.11) | copy-start | bytes 1572868
Sparse Core Ops, SparseCore 0:
  10.2 67.4 all-gather.1
  455.4 128.2 reduce-scatter.1
where the time goes:
time: 596 us; the launch traced here: 593 us
  waiting for transfers between devices  219 us (37%)
  loops' own time  147 us (25%)
  blocking collectives  93.3 us (16%)
  local copies, waits for them, and re-layouts  47 us (8%)
  other arithmetic  40.3 us (7%)
  matrix products  16.6 us (3%)
  between operations  15.6 us (3%)
  starting transfers between devices  14.5 us (2%)
    another operation x1, loops' own time, dual_search(): lax.fori_loop(0, BISECT_STEPS, advance, (-sum_total, sum_total))  147 us
    reduce_scatter x1, waiting for transfers between devices, local(): lax.psum_scatter(jnp.einsum('ern,erh->neh', error_local, scaled, preferre...  128 us
    all_to_all x1, blocking collectives, local(): lax.all_to_all(send_rows, 'expert', split_axis=0, concat_axis=0, tiled=True)  53.4 us
    all_to_all x1, waiting for transfers between devices, local(): lax.all_to_all(by_source(expert_out, groups), 'expert', split_axis=0, con...  45.7 us
    all_to_all x1, waiting for transfers between devices, local(): lax.all_to_all(error_low[source_row].reshape(experts, capacity, feat_widt...  44.8 us
    psum x1, blocking collectives, local(): seq_sq, seq_len = lax.psum((partial_sq, counts), ('dp', 'expert'))  39.9 us
    reduce_sum x40, other arithmetic, advance(): jnp.sum(excess)  24.1 us
  transfers between devices with their start and end apart: 5, of which 3 were waited for; matrix products, arithmetic and copies ran while one was open for 5% of the time, Pallas kernels for 0%

commit v1 on v0

--- a/solution.py
+++ b/solution.py
@@ -1,6 +1,10 @@
+import functools
+
 import jax
 import jax.numpy as jnp
 from jax import lax
+from jax.experimental import pallas as pl
+from jax.experimental.pallas import tpu as pltpu
 from jax.sharding import PartitionSpec as P
 
 NSEQ = 64
@@ -56,7 +60,7 @@
     return jnp.swapaxes(split_view, 0, 1).reshape((exp_dev * groups, capacity) + tail_shape)
 
 
-def local(tokens, targets, routes, route_logits, slot_order, seq_ids, w_gate, w_up, w_down):
+def row_plan(tokens, targets, routes, route_logits, slot_order, seq_ids, w_gate, w_up, w_down):
     tok_rows, feat_width = tokens.shape
     top_k = routes.shape[1]
     groups = lax.axis_size("expert")
@@ -131,6 +135,562 @@
         tiled=True,
     )
     return (combined.astype(jnp.bfloat16), seq_loss, dual_weight, grad_down)
+
+
+LANES = 128
+FLOAT = jnp.float32
+HALF = jnp.bfloat16
+INFO = 16
+SEQ_LINE = 8
+
+
+def swap(block, axis, mask):
+    size = lax.axis_size(axis)
+    return lax.ppermute(block, axis, [(s, s ^ mask) for s in range(size)])
+
+
+def tree_sum(terms):
+    while len(terms) > 1:
+        rest = terms[len(terms) // 2 * 2 :]
+        terms = [a + b for a, b in zip(terms[::2], terms[1::2])] + rest
+    return terms[0]
+
+
+def dot_nt(a, b):
+    return lax.dot_general(a, b, (((1,), (1,)), ((), ())), preferred_element_type=FLOAT)
+
+
+def dot_nn(a, b):
+    return jnp.dot(a, b, preferred_element_type=FLOAT)
+
+
+def cost():
+    return pl.CostEstimate(flops=1, bytes_accessed=1, transcendentals=0)
+
+
+def params(mib=60):
+    return pltpu.CompilerParams(vmem_limit_bytes=mib << 20)
+
+
+def col_to_row(col):
+    count = col.shape[0]
+    diagonal = lax.broadcasted_iota(jnp.int32, (count, LANES), 0) == lax.broadcasted_iota(
+        jnp.int32, (count, LANES), 1
+    )
+    return jnp.sum(jnp.where(diagonal, col, 0.0), axis=0, keepdims=True)
+
+
+def row_to_col(row, count):
+    diagonal = lax.broadcasted_iota(jnp.int32, (count, LANES), 0) == lax.broadcasted_iota(
+        jnp.int32, (count, LANES), 1
+    )
+    return jnp.sum(jnp.where(diagonal, row, 0.0), axis=1, keepdims=True)
+
+
+def in_vmem(count=1):
+    return [pl.BlockSpec(memory_space=pltpu.VMEM)] * count
+
+
+def pack_tokens_kernel(experts, tokens, routes, logits, order, seq, out):
+    top_k, rows = routes.shape
+    names, slots, scores = routes[...], order[...], logits[...]
+    picked = jnp.zeros((top_k, rows), FLOAT)
+    for k in range(top_k):
+        picked += jnp.where(slots == k, scores[k : k + 1, :], 0.0)
+    raised = jnp.exp(picked)
+    gates = raised / jnp.sum(raised, axis=0, keepdims=True)
+    expert = lax.broadcasted_iota(jnp.int32, (experts, rows), 0)
+    named = jnp.zeros((experts, rows), FLOAT)
+    prob = jnp.zeros((experts, rows), FLOAT)
+    for k in range(top_k):
+        hit = names[k : k + 1, :] == expert
+        named += jnp.where(hit, 1.0, 0.0)
+        prob += jnp.where(hit, gates[k : k + 1, :], 0.0)
+    before = lax.broadcasted_iota(jnp.int32, (rows, rows), 0) < lax.broadcasted_iota(
+        jnp.int32, (rows, rows), 1
+    )
+    rank = dot_nn(named.astype(HALF), jnp.where(before, 1.0, 0.0).astype(HALF))
+    place = jnp.where(named > 0.5, rank, -1.0).astype(HALF)
+    number = jnp.broadcast_to(seq[...].astype(FLOAT), (experts, rows)).astype(HALF)
+    out[0:rows, :] = tokens[...]
+    out[rows:, :] = jnp.zeros((experts, out.shape[1]), HALF)
+    for b, piece in enumerate([place, *exact_pieces(prob), number]):
+        out[rows:, b * rows : (b + 1) * rows] = piece
+
+
+def exact_pieces(value):
+    pieces = []
+    for _ in range(3):
+        pieces.append(value.astype(HALF))
+        value = value - pieces[-1].astype(FLOAT)
+    return pieces
+
+
+def pack_tokens(tokens, routes, route_logits, slot_order, seq_ids, experts):
+    rows, width = tokens.shape
+    return pl.pallas_call(
+        functools.partial(pack_tokens_kernel, experts),
+        in_specs=in_vmem(5),
+        out_specs=pl.BlockSpec(memory_space=pltpu.VMEM),
+        out_shape=jax.ShapeDtypeStruct((rows + experts, width), HALF),
+        cost_estimate=cost(),
+        compiler_params=params(),
+        name="pack_tokens",
+    )(tokens, routes.T, route_logits.T, slot_order.T, seq_ids.reshape(1, rows))
+
+
+def hidden_kernel(experts, capacity, own, x_side, y_side, upper, lower, *refs):
+    w_gate, w_up, out, joined, info, picked, probs, both, arrived = refs
+    exp_dev, _, units = w_gate.shape
+    for e in range(exp_dev):
+        pltpu.make_async_copy(w_gate.at[e], both.at[e, :, pl.ds(0, units)], arrived.at[e]).start()
+        pltpu.make_async_copy(w_up.at[e], both.at[e, :, pl.ds(units, units)], arrived.at[e]).start()
+    joined[0 : upper.shape[0], :] = upper[...]
+    joined[joined.shape[0] - lower.shape[0] :, :] = lower[...]
+    tokens = [own, x_side, y_side, joined]
+    total = len(tokens) * capacity
+    rows = own.shape[0] - experts
+    first = lax.axis_index("expert") * exp_dev
+    slot = lax.broadcasted_iota(jnp.int32, (capacity, rows), 0).astype(FLOAT)
+    lane = lax.broadcasted_iota(jnp.int32, (INFO, rows), 1).astype(FLOAT).astype(HALF)
+    line = lax.broadcasted_iota(jnp.int32, (INFO, total), 0)
+    expert = lax.broadcasted_iota(jnp.int32, (experts, rows), 0)
+    info[...] = jnp.zeros(info.shape, FLOAT)
+    origins = [[] for _ in range(exp_dev)]
+    for m, block in enumerate(tokens):
+        place, high, middle, low, number = (
+            block[rows:, b * rows : (b + 1) * rows].astype(FLOAT) for b in range(5)
+        )
+        prob = high + middle + low
+        info[SEQ_LINE + m : SEQ_LINE + m + 1, 0:rows] = number[0:1, :]
+        picks = []
+        for e in range(exp_dev):
+            mine = expert == first + e
+            own_place = jnp.sum(jnp.where(mine, place, 0.0), axis=0, keepdims=True)
+            own_prob = jnp.sum(jnp.where(mine, prob, 0.0), axis=0, keepdims=True)
+            pick = jnp.where(own_place == slot, 1.0, 0.0)
+            probs[e, m * capacity : (m + 1) * capacity, :] = jnp.broadcast_to(
+                jnp.sum(pick * own_prob, axis=1, keepdims=True), (capacity, LANES)
+            )
+            picks.append(pick.astype(HALF))
+            origins[e].append(picks[-1])
+        rows_m = dot_nn(jnp.concatenate(picks, axis=0), block[0:rows, :]).astype(HALF)
+        for e in range(exp_dev):
+            picked[e, m * capacity : (m + 1) * capacity, :] = rows_m[
+                e * capacity : (e + 1) * capacity, :
+            ]
+    for e in range(exp_dev):
+        origin = dot_nt(lane, jnp.concatenate(origins[e], axis=0))
+        info[:, 0:total] = jnp.where(line == e, origin, info[:, 0:total])
+    out[exp_dev * total :, :] = info[...].astype(HALF)
+
+    def one_expert(e, carry):
+        chosen = picked[e]
+        pltpu.make_async_copy(both.at[e], both.at[e], arrived.at[e]).wait()
+        product = dot_nn(chosen, both[e])
+        gate, up = product[:, :units], product[:, units:]
+        hidden = (gate / (1.0 + jnp.exp(-gate)) * up).astype(HALF)
+        scaled = (probs[e, :, 0:1] * hidden.astype(FLOAT)).astype(HALF)
+        out[pl.ds(pl.multiple_of(e * total, total), total), :] = scaled
+        return carry
+
+    lax.fori_loop(0, exp_dev, one_expert, 0)
+
+
+def hidden_rows(tokens, w_gate, w_up, experts, capacity):
+    lines, width = tokens[0].shape
+    exp_dev, _, units = w_gate.shape
+    total = 4 * capacity
+    return pl.pallas_call(
+        functools.partial(hidden_kernel, experts, capacity),
+        in_specs=in_vmem(5) + [pl.BlockSpec(memory_space=pl.ANY)] * 2,
+        out_specs=pl.BlockSpec(memory_space=pltpu.VMEM),
+        out_shape=jax.ShapeDtypeStruct((exp_dev * total + INFO, units), HALF),
+        scratch_shapes=[
+            pltpu.VMEM((lines, width), HALF),
+            pltpu.VMEM((INFO, units), FLOAT),
+            pltpu.VMEM((exp_dev, total, width), HALF),
+            pltpu.VMEM((exp_dev, total, LANES), FLOAT),
+            pltpu.VMEM((exp_dev, width, 2 * units), HALF),
+            pltpu.SemaphoreType.DMA((exp_dev,)),
+        ],
+        cost_estimate=cost(),
+        compiler_params=params(),
+        name="hidden_rows",
+    )(*tokens, w_gate, w_up)
+
+
+def row_places(info, e, total, capacity, rows, sources):
+    shift = (lax.broadcasted_iota(jnp.int32, (1, total), 1) // capacity * rows).astype(FLOAT)
+    token = lax.broadcasted_iota(jnp.int32, (sources * rows, total), 0).astype(FLOAT)
+    return jnp.where(token == info[e : e + 1, 0:total] + shift, 1.0, 0.0).astype(HALF)
+
+
+def project_kernel(exp_dev, capacity, rows, sources, slots, *refs):
+    blocks, (w_down, seqs), refs = refs[:slots], refs[slots : slots + 2], refs[slots + 2 :]
+    partials, (packed, outs, places, arrived) = refs[:sources], refs[sources:]
+    units = w_down.shape[1] // exp_dev
+    total = sources * capacity
+    for s in range(slots):
+        pltpu.make_async_copy(blocks[s], packed.at[s], arrived.at[s]).start()
+
+    def one_slot(s, carry):
+        pltpu.make_async_copy(packed.at[s], packed.at[s], arrived.at[s]).wait()
+        info = packed[s, exp_dev * total :, :].astype(FLOAT)
+        seqs[s] = info[SEQ_LINE:, 0:rows]
+        for e in range(exp_dev):
+            here = slice(e * total, (e + 1) * total)
+            outs[:, here] = dot_nt(
+                w_down[:, e * units : (e + 1) * units], packed[s, here, :]
+            ).astype(HALF)
+            places[:, here] = row_places(info, e, total, capacity, rows, sources)
+        part = dot_nt(outs[...], places[...]).astype(HALF)
+        for k in range(sources):
+            partials[k][s] = part[:, k * rows : (k + 1) * rows]
+        return carry
+
+    lax.fori_loop(0, slots, one_slot, 0)
+
+
+def project(blocks, w_down, exp_dev, capacity, rows, sources):
+    slots = len(blocks)
+    feats = w_down.shape[0]
+    total = exp_dev * sources * capacity
+    out = pl.pallas_call(
+        functools.partial(project_kernel, exp_dev, capacity, rows, sources, slots),
+        in_specs=[pl.BlockSpec(memory_space=pl.ANY)] * slots + in_vmem(1),
+        out_specs=in_vmem(1 + sources),
+        out_shape=[jax.ShapeDtypeStruct((slots, 8, rows), FLOAT)]
+        + [jax.ShapeDtypeStruct((slots, feats, rows), HALF)] * sources,
+        scratch_shapes=[
+            pltpu.VMEM((slots,) + blocks[0].shape, HALF),
+            pltpu.VMEM((feats, total), HALF),
+            pltpu.VMEM((sources * rows, total), HALF),
+            pltpu.SemaphoreType.DMA((slots,)),
+        ],
+        cost_estimate=cost(),
+        compiler_params=params(),
+        name="project",
+    )(*blocks, w_down)
+    return out[0], out[1:]
+
+
+def spread_kernel(exp_dev, capacity, rows, sources, *refs):
+    slots = len(refs) - 5
+    blocks, (spread, packed, held, arrived, done) = refs[:slots], refs[slots:]
+    units = packed.shape[2]
+    total = sources * capacity
+    for s in range(slots):
+        pltpu.make_async_copy(blocks[s], packed.at[s], arrived.at[s]).start()
+
+    def one_slot(s, carry):
+        pltpu.make_async_copy(packed.at[s], packed.at[s], arrived.at[s]).wait()
+        info = packed[s, exp_dev * total :, :].astype(FLOAT)
+        for e in range(exp_dev):
+            place = row_places(info, e, total, capacity, rows, sources)
+            rows_e = packed[s, e * total : (e + 1) * total, :]
+            held[s, :, e * units : (e + 1) * units] = dot_nn(place, rows_e).astype(HALF)
+        pltpu.make_async_copy(held.at[s], spread.at[s], done.at[s]).start()
+        return carry
+
+    lax.fori_loop(0, slots, one_slot, 0)
+    for s in range(slots):
+        pltpu.make_async_copy(held.at[s], spread.at[s], done.at[s]).wait()
+
+
+def spread_rows(blocks, exp_dev, capacity, rows, sources):
+    slots = len(blocks)
+    shape = (slots, sources * rows, exp_dev * blocks[0].shape[1])
+    return pl.pallas_call(
+        functools.partial(spread_kernel, exp_dev, capacity, rows, sources),
+        in_specs=[pl.BlockSpec(memory_space=pl.ANY)] * slots,
+        out_specs=pl.BlockSpec(memory_space=pl.ANY),
+        out_shape=jax.ShapeDtypeStruct(shape, HALF),
+        scratch_shapes=[
+            pltpu.VMEM((slots,) + blocks[0].shape, HALF),
+            pltpu.VMEM(shape, HALF),
+            pltpu.SemaphoreType.DMA((slots,)),
+            pltpu.SemaphoreType.DMA((slots,)),
+        ],
+        cost_estimate=cost(),
+        compiler_params=params(),
+        name="spread_rows",
+    )(*blocks)
+
+
+def residual_kernel(first, batches, sources, *refs):
+    parts, refs = refs[: sources * len(batches)], refs[sources * len(batches) :]
+    seqs, (targets, *refs) = refs[: len(batches)], refs[len(batches) :]
+    if first:
+        before, earlier, *refs = refs
+    combined, errors, squares = refs
+    feats, rows = targets.shape[1:]
+    me = lax.axis_index("dp")
+    number = lax.broadcasted_iota(jnp.int32, (NSEQ, rows), 0).astype(FLOAT)
+    squared = jnp.zeros((NSEQ, rows), FLOAT)
+    if first:
+        for s in range(first):
+            combined[me ^ s] = earlier[s]
+    slot = 0
+    for b, slots in enumerate(batches):
+        here = parts[b * sources : (b + 1) * sources]
+        for s in range(slots):
+            total = tree_sum([part[s].astype(FLOAT) for part in here])
+            combined[me ^ (first + slot) if first else slot] = total.astype(HALF)
+            error = total - targets[me ^ (first + slot)].astype(FLOAT)
+            errors[slot * feats : (slot + 1) * feats, :] = error.astype(HALF)
+            per_token = jnp.sum(error * error, axis=0, keepdims=True)
+            squared += jnp.where(seqs[b][s, 0:1, :] == number, per_token, 0.0)
+            slot += 1
+    sums = jnp.broadcast_to(col_to_row(jnp.sum(squared, axis=1, keepdims=True)), (8, LANES))
+    squares[...] = sums + before[...] if first else sums
+
+
+def residual(first, parts, seqs, targets, before, earlier):
+    feats, rows = targets.shape[1:]
+    batches = tuple(batch[0].shape[0] for batch in parts)
+    sources = len(parts[0])
+    slots = sum(batches)
+    extra = [before, earlier] if first else []
+    return pl.pallas_call(
+        functools.partial(residual_kernel, first, batches, sources),
+        in_specs=in_vmem((sources + 1) * len(batches) + 1 + len(extra)),
+        out_specs=in_vmem(3),
+        out_shape=[
+            jax.ShapeDtypeStruct((first + slots, feats, rows), HALF),
+            jax.ShapeDtypeStruct((slots * feats, rows), HALF),
+            jax.ShapeDtypeStruct((8, LANES), FLOAT),
+        ],
+        cost_estimate=cost(),
+        compiler_params=params(),
+        name="residual",
+    )(*[part for batch in parts for part in batch], *seqs, targets, *extra)
+
+
+def gradient_kernel(scale, feat_width, exp_dev, terms, batches, parts, sources, *refs):
+    squares, refs = refs[:terms], refs[terms:]
+    count, groups = len(batches), sum(batches)
+    spreads, seqs, refs = refs[:count], refs[count : 2 * count], refs[2 * count :]
+    errors, refs = refs[: sources * len(parts)], refs[sources * len(parts) :]
+    grad, seq_loss, dual_weight, held, error, lines, weighted, total, rates, arrived = refs
+    feats = grad.shape[0]
+    rows = error.shape[2] // sources
+    slot = 0
+    for b, slots in enumerate(parts):
+        for s in range(slots):
+            for m in range(sources):
+                pltpu.make_async_copy(
+                    errors[b * sources + m].at[pl.ds(s * feats, feats), :],
+                    error.at[slot, :, pl.ds(m * rows, rows)],
+                    arrived.at[0, slot],
+                ).start()
+            slot += 1
+    slot = 0
+    for seq, spread, slots in zip(seqs, spreads, batches):
+        for s in range(slots):
+            lines[slot] = seq[s]
+            pltpu.make_async_copy(spread.at[s], held.at[slot], arrived.at[1, slot]).start()
+            slot += 1
+    number = lax.broadcasted_iota(jnp.int32, (NSEQ, rows), 0).astype(FLOAT)
+
+    def count_slot(s, found):
+        for m in range(sources):
+            found += jnp.where(lines[s, m : m + 1, :] == number, 1.0, 0.0)
+        return found
+
+    found = lax.fori_loop(0, groups, count_slot, jnp.zeros((NSEQ, rows), FLOAT))
+    seq_len = jnp.sum(found, axis=1, keepdims=True)
+    summed = tree_sum([part[0:1, :] for part in squares])
+    loss = row_to_col(summed, NSEQ) / (seq_len * feat_width)
+    loss = jnp.broadcast_to(loss, (NSEQ, LANES))
+    weight = dual_search_rows(loss)
+    rates[...] = scale * (weight / seq_len)
+    seq_loss[...] = col_to_row(loss)[:, 0:NSEQ]
+    dual_weight[...] = col_to_row(weight)[:, 0:NSEQ]
+    total[...] = jnp.zeros(total.shape, FLOAT)
+    for s in range(groups):
+        pltpu.make_async_copy(error.at[s], error.at[s], arrived.at[0, s]).wait()
+
+    def weigh(s, turn):
+        for m in range(sources):
+            here = slice(m * rows, (m + 1) * rows)
+            hit = jnp.where(lines[s, m : m + 1, :] == number, rates[...], 0.0)
+            rate = jnp.sum(hit, axis=0, keepdims=True)
+            weighted[turn, :, here] = (rate * error[s, :, here].astype(FLOAT)).astype(HALF)
+
+    def add_slot(s, carry):
+        pltpu.make_async_copy(held.at[s], held.at[s], arrived.at[1, s]).wait()
+        product = dot_nn(weighted[s % 2], held[s])
+        weigh(jnp.minimum(s + 1, groups - 1), (s + 1) % 2)
+        total[...] += product
+        return carry
+
+    weigh(0, 0)
+    lax.fori_loop(0, groups, add_slot, 0)
+    units = grad.shape[2]
+    for e in range(exp_dev):
+        grad[:, e, :] = total[:, e * units : (e + 1) * units]
+
+
+def dual_search_rows(loss):
+    bound = jnp.sum(loss, axis=0, keepdims=True)
+
+    def advance(step_index, bounds):
+        lower, upper = bounds
+        middle = 0.5 * (lower + upper)
+        excess = jnp.maximum(loss - middle, 0.0)
+        square_sum = jnp.sum(excess * excess, axis=0, keepdims=True)
+        plain_sum = jnp.sum(excess, axis=0, keepdims=True)
+        is_above = NSEQ * square_sum - radius_factor * plain_sum * plain_sum >= 0.0
+        return (jnp.where(is_above, lower, middle), jnp.where(is_above, middle, upper))
+
+    lower, upper = lax.fori_loop(
+        0, BISECT_STEPS, advance, (-bound, bound), unroll=8
+    )
+    excess = jnp.maximum(loss - 0.5 * (lower + upper), 0.0)
+    return excess / jnp.sum(excess, axis=0, keepdims=True)
+
+
+def gradient(squares, spreads, seqs, errors, batches, parts, sources, scale, feat_width, exp_dev):
+    rows = errors[0].shape[1]
+    feats = errors[0].shape[0] // parts[0]
+    group_rows, flat = spreads[0].shape[1:]
+    units = flat // exp_dev
+    groups = sum(batches)
+    return pl.pallas_call(
+        functools.partial(
+            gradient_kernel, scale, feat_width, exp_dev, len(squares), batches, parts, sources
+        ),
+        in_specs=in_vmem(len(squares))
+        + [pl.BlockSpec(memory_space=pl.ANY)] * len(spreads)
+        + in_vmem(len(seqs))
+        + [pl.BlockSpec(memory_space=pl.ANY)] * len(errors),
+        out_specs=in_vmem(3),
+        out_shape=[
+            jax.ShapeDtypeStruct((feats, exp_dev, units), FLOAT),
+            jax.ShapeDtypeStruct((1, NSEQ), FLOAT),
+            jax.ShapeDtypeStruct((1, NSEQ), FLOAT),
+        ],
+        scratch_shapes=[
+            pltpu.VMEM((groups, group_rows, flat), HALF),
+            pltpu.VMEM((groups, feats, group_rows), HALF),
+            pltpu.VMEM((groups, 8, rows), FLOAT),
+            pltpu.VMEM((2, feats, group_rows), HALF),
+            pltpu.VMEM((feats, flat), FLOAT),
+            pltpu.VMEM((NSEQ, rows), FLOAT),
+            pltpu.SemaphoreType.DMA((2, groups)),
+        ],
+        cost_estimate=cost(),
+        compiler_params=params(),
+        name="gradient",
+    )(*squares, *spreads, *seqs, *errors)
+
+
+def z_near(block):
+    return {2: swap(block, "dp", 2), 4: swap(block, "dp", 4)}
+
+
+def z_far(blocks):
+    return swap(blocks[4], "dp", 2)
+
+
+def feature_plan(tokens, targets, routes, route_logits, slot_order, seq_ids, w_gate, w_up, w_down):
+    rows, feat_width = tokens.shape
+    groups, sources = lax.axis_size("dp"), lax.axis_size("expert")
+    exp_dev, _, units = w_gate.shape
+    experts = exp_dev * sources
+    capacity = rows * routes.shape[1] // experts
+    feats = feat_width // groups
+    scale = float(rows * groups * sources // 8)
+    far = range(1, sources)
+    tie = lax.optimization_barrier
+
+    own_tokens = pack_tokens(tokens, routes, route_logits, slot_order, seq_ids, experts)
+    x_tokens, y_tokens = swap(own_tokens, "expert", 1), swap(own_tokens, "expert", 2)
+    half = (rows + experts + 31) // 32 * 16
+    diagonal = [swap(y_tokens[:half], "expert", 1), swap(x_tokens[-half:], "expert", 2)]
+    turned, own_tokens = tie((targets.T, own_tokens))
+    own_targets = lax.all_to_all(
+        turned.reshape(groups, feats, rows), "dp", split_axis=0, concat_axis=0, tiled=True
+    )
+    x_tokens, y_tokens, diagonal, own_targets = tie((x_tokens, y_tokens, diagonal, own_targets))
+    packed = hidden_rows(
+        [own_tokens, x_tokens, y_tokens, *diagonal], w_gate, w_up, experts, capacity
+    )
+    blocks = {0: packed, **z_near(packed)}
+    flat_down = w_down.reshape(feats, exp_dev * units)
+
+    def expert_parts(first, slots):
+        for s in range(first, first + slots, 2):
+            blocks[s + 1] = swap(blocks[s], "dp", 1)
+        here = [blocks[s] for s in range(first, first + slots)]
+        seq, parts = project(here, flat_down, exp_dev, capacity, rows, sources)
+        parts = [parts[0]] + [swap(parts[m], "expert", m) for m in far]
+        spread = spread_rows(here, exp_dev, capacity, rows, sources)
+        parts, spread = tie((parts, spread))
+        return spread, seq, parts
+
+    def far_errors(error):
+        return [swap(error, "expert", m) for m in far]
+
+    batches = (2, groups - 4, 2)
+    spread_0, seq_0, parts_0 = expert_parts(0, batches[0])
+    mixed_0, error_0, squares_0 = residual(0, [parts_0], [seq_0], own_targets, None, None)
+    errors_0 = far_errors(error_0)
+    blocks, errors_0 = tie((blocks, errors_0))
+    blocks[6] = z_far(blocks)
+
+    spread_1, seq_1, parts_1 = expert_parts(2, batches[1])
+    spread_2, seq_2, parts_2 = expert_parts(groups - 2, batches[2])
+    mixed, error_1, squares = residual(
+        2, [parts_1, parts_2], [seq_1, seq_2], own_targets, squares_0, mixed_0
+    )
+    far_squares = [swap(squares, "expert", m) for m in far]
+    error_1, far_squares = tie((error_1, far_squares))
+    errors_1 = far_errors(error_1)
+    squares = tree_sum([squares] + far_squares)
+    squares = squares + swap(squares, "dp", 1)
+    all_squares = [squares] + [swap(squares, "dp", m) for m in range(2, groups, 2)]
+    mixed = lax.all_to_all(mixed, "dp", split_axis=0, concat_axis=0, tiled=True)
+    grad_down, seq_loss, dual_weight = gradient(
+        all_squares,
+        [spread_0, spread_1, spread_2],
+        [seq_0, seq_1, seq_2],
+        [error_0, *errors_0, error_1, *errors_1],
+        batches,
+        (batches[0], batches[1] + batches[2]),
+        sources,
+        scale,
+        feat_width,
+        exp_dev,
+    )
+    return (
+        mixed.reshape(feat_width, rows).T,
+        seq_loss.reshape(NSEQ),
+        dual_weight.reshape(NSEQ),
+        grad_down,
+    )
+
+
+def local(tokens, targets, routes, route_logits, slot_order, seq_ids, w_gate, w_up, w_down):
+    args = (tokens, targets, routes, route_logits, slot_order, seq_ids, w_gate, w_up, w_down)
+    groups, sources = lax.axis_size("dp"), lax.axis_size("expert")
+    units = w_gate.shape[2]
+    exp_dev = w_gate.shape[0]
+    rows, feat_width = tokens.shape
+    capacity = rows * routes.shape[1] // (exp_dev * sources)
+    whole_tiles = (
+        feat_width % (groups * LANES) == 0
+        and rows == LANES
+        and units % LANES == 0
+        and sources * capacity <= units
+        and capacity % 16 == 0
+        and exp_dev <= SEQ_LINE
+        and exp_dev * sources == INFO
+        and sources == 4
+        and groups == 8
+    )
+    return (feature_plan if whole_tiles else row_plan)(*args)
 
 
 def solution(mesh):

time: 596 us -> 174 us (0.29)
  waiting for transfers between devices: 219 us -> 56.9 us
  loops' own time: 147 us -> 0 us
  blocking collectives: 93.3 us -> 0 us
  Pallas kernels: 0 us -> 54.3 us
  other arithmetic: 40.3 us -> 0.68 us
  local copies, waits for them, and re-layouts: 47 us -> 10.5 us
  starting transfers between devices: 14.5 us -> 50 us
  matrix products: 16.6 us -> 0 us
  between operations: 15.6 us -> 1.02 us
    another operation x1 -> x0, loops' own time: 147 us -> none  [dual_search(): lax.fori_loop(0, BISECT_STEPS, advance, (-sum_total, sum_total))]
    reduce_scatter x1 -> x0, waiting for transfers between devices: 128 us -> none  [local(): lax.psum_scatter(jnp.einsum('ern,erh->neh', error_local, scaled, preferre...]
    all_to_all x3 -> x2, waiting for transfers between devices: 90.6 us -> 0.01 us  [the longest x1 0.01 us: feature_plan(): lax.all_to_all(turned.reshape(groups, feats, rows), 'dp', split_axis=0, c...]
    ppermute x0 -> x33, waiting for transfers between devices: none -> 56.9 us  [swap(): return lax.ppermute(block, axis, [(s, s ^ mask) for s in range(size)])]
    pallas_call x0 -> x11, Pallas kernels: none -> 54.3 us  [the longest x3 15.5 us: project(): pl.pallas_call(functools.partial(project_kernel, exp_dev, capacity, rows,...]
    all_to_all x1 -> x0, blocking collectives: 53.4 us -> none  [local(): lax.all_to_all(send_rows, 'expert', split_axis=0, concat_axis=0, tiled=True)]
    ppermute x0 -> x33, starting transfers between devices: none -> 40.4 us  [swap(): return lax.ppermute(block, axis, [(s, s ^ mask) for s in range(size)])]
    psum x1 -> x0, blocking collectives: 39.9 us -> none  [local(): seq_sq, seq_len = lax.psum((partial_sq, counts), ('dp', 'expert'))]
  transfers between devices with their start and end apart: 5 -> 35, of which waited for: 3 -> 13; matrix products, arithmetic and copies ran while one was open for 5% -> 2% of each run, Pallas kernels for 0% -> 23%
where the time goes in v1:
time: 174 us; the launch traced here: 173 us
  waiting for transfers between devices  56.9 us (33%)
  Pallas kernels  54.3 us (31%)
  starting transfers between devices  50 us (29%)
  local copies, waits for them, and re-layouts  10.5 us (6%)
    ppermute x33, waiting for transfers between devices, swap(): return lax.ppermute(block, axis, [(s, s ^ mask) for s in range(size)])  56.9 us
    ppermute x33, starting transfers between devices, swap(): return lax.ppermute(block, axis, [(s, s ^ mask) for s in range(size)])  40.4 us
    pallas_call x3, Pallas kernels, project(): pl.pallas_call(functools.partial(project_kernel, exp_dev, capacity, rows,...  15.5 us
    pallas_call x3, Pallas kernels, spread_rows(): pl.pallas_call(functools.partial(spread_kernel, exp_dev, capacity, rows,...  13 us
    pallas_call x1, Pallas kernels, gradient(): pl.pallas_call(functools.partial(gradient_kernel, scale, feat_width, exp_...  9.73 us
    pallas_call x1, Pallas kernels, hidden_rows(): pl.pallas_call(functools.partial(hidden_kernel, experts, capacity), in_sp...  8.95 us
    unnamed x63, local copies, waits for them, and re-layouts  7.38 us
    pallas_call x2, Pallas kernels, residual(): pl.pallas_call(functools.partial(residual_kernel, first, batches, sources...  5.05 us
  transfers between devices with their start and end apart: 35, of which 13 were waited for; matrix products, arithmetic and copies ran while one was open for 2% of the time, Pallas kernels for 23%

profile of v1, /device:TPU:0, one launch (start us, length us, event | category | flops | bytes accessed | tf_op | source)
XLA Modules:
  0.0 173.4 jit_solution(5471090530402313213)
XLA Ops:
  0.6 2.1 %pack_tokens.1.own = bf16[144,2048]{1,0:T(8,128)(2,1)} custom-call(bf16[128,2048]{1,0:T(8,128)(2,1)} %tokens.1, s32[8,128]{1,0:T(8,128)} %bitcast.19, f32[8,128]{1,0:T(8,128)} %bitcast.20, s32[8,128]{1,0:T(8,128)} %bitcast.21, s32[1,128]{1,0:T(1,128)} %bitcast.22), custom_call_target="tpu_custom_call" | custom-call | flops 1 | bytes 1 | tf_op jit(solution)/shard_map/pack_tokens/pallas_call | solution.py:231
  2.7 2.9 %collective-permute-start = (bf16[144,2048]{1,0:T(8,128)(2,1)}, bf16[144,2048]{1,0:T(8,128)(2,1)S(1)}, u32[]{:S(2)}, u32[]{:S(2)}) collective-permute-start(bf16[144,2048]{1,0:T(8,128)(2,1)} %pack_tokens.1.own), channel_id=1, source_target_pairs={{0,1},{1,0},{2,3},{3,2},{4,5},{5,4},{6,7},{7,6},{8,9},{9,8},{10,11... | collective-permute-start | bytes 1769480 | tf_op jit(solution)/shard_map/ppermute | solution.py:149
  7.2 2.0 %copy.13 = bf16[2048,128]{1,0:T(8,128)(2,1)} copy(bf16[2048,128]{0,1:T(8,128)(2,1)} %bitcast.17) | data formatting | bytes 1048576 | tf_op jit(solution)/shard_map/optimization_barrier | solution.py:612
  9.2 4.9 %all-to-all-start = ((bf16[8,256,128]{2,1,0:T(8,128)(2,1)}), bf16[8,256,128]{2,1,0:T(8,128)(2,1)S(1)}, u32[]{:S(2)}, u32[]{:S(2)}) async-start(bf16[8,256,128]{2,1,0:T(8,128)(2,1)} %bitcast.5), calls=%async_computation | async-start | bytes 1048576 | tf_op jit(solution)/shard_map/all_to_all | solution.py:613
  14.1 6.6 %collective-permute-done.1.y_side = bf16[144,2048]{1,0:T(8,128)(2,1)S(1)} collective-permute-done((bf16[144,2048]{1,0:T(8,128)(2,1)}, bf16[144,2048]{1,0:T(8,128)(2,1)S(1)}, u32[]{:S(2)}, u32[]{:S(2)}) %collective-permute-start.1) | collective-permute-done | bytes 589856 | tf_op jit(solution)/shard_map/ppermute | solution.py:149
  21.1 1.8 %collective-permute-start.3 = (bf16[80,2048]{1,0:T(8,128)(2,1)S(1)}, bf16[80,2048]{1,0:T(8,128)(2,1)S(1)}, u32[]{:S(2)}, u32[]{:S(2)}) collective-permute-start(bf16[80,2048]{1,0:T(8,128)(2,1)S(1)} %slice.9), channel_id=1, source_target_pairs={{0,2},{1,3},{2,0},{3,1},{4,6},{5,7},{6,4},{7,5},{8,10},{9,11},{10,... | collective-permute-start | bytes 983048 | tf_op jit(solution)/shard_map/ppermute | solution.py:149
  22.9 6.1 %collective-permute-done.2.upper = bf16[80,2048]{1,0:T(8,128)(2,1)S(1)} collective-permute-done((bf16[80,2048]{1,0:T(8,128)(2,1)S(1)}, bf16[80,2048]{1,0:T(8,128)(2,1)S(1)}, u32[]{:S(2)}, u32[]{:S(2)}) %collective-permute-start.2) | collective-permute-done | bytes 327712 | tf_op jit(solution)/shard_map/ppermute | solution.py:149
  30.2 9.0 %hidden_rows.1.refs_0_ = bf16[1040,384]{1,0:T(8,128)(2,1)} custom-call(bf16[144,2048]{1,0:T(8,128)(2,1)} %pack_tokens.1.own, bf16[144,2048]{1,0:T(8,128)(2,1)} %copy-done.7, bf16[144,2048]{1,0:T(8,128)(2,1)} %copy-done.8, bf16[80,2048]{1,0:T(8,128)(2,1)} %copy-done.13, bf16[80,2048]{1,0:T(8,128)(2,1)} %copy-done.14, bf16[4,2048,384]{2,1,0:T(8,128)(2,1)} %refs_0_.1, ...), custom_call_target="tpu_custom_call" | custom-call | flops 1 | bytes 1 | tf_op jit(solution)/shard_map/hidden_rows/pallas_call | solution.py:304
  40.8 2.6 %collective-permute-start.6 = (bf16[1040,384]{1,0:T(8,128)(2,1)}, bf16[1040,384]{1,0:T(8,128)(2,1)S(1)}, u32[]{:S(2)}, u32[]{:S(2)}) collective-permute-start(bf16[1040,384]{1,0:T(8,128)(2,1)} %hidden_rows.1.refs_0_), channel_id=1, source_target_pairs={{0,16},{4,20},{8,24},{12,28},{16,0},{20,4},{24,8},{28,12},{1,17},{... | collective-permute-start | bytes 2396168 | tf_op jit(solution)/shard_map/ppermute | solution.py:149
  45.3 4.6 %project.3 = (f32[2,8,128]{2,1,0:T(8,128)}, bf16[2,256,128]{2,1,0:T(8,128)(2,1)}, bf16[2,256,128]{2,1,0:T(8,128)(2,1)}, bf16[2,256,128]{2,1,0:T(8,128)(2,1)}, bf16[2,256,128]{2,1,0:T(8,128)(2,1)}) custom-call(bf16[1040,384]{1,0:T(8,128)(2,1)} %hidden_rows.1.refs_0_, bf16[1040,384]{1,0:T(8,128)(2,1)} %copy-done.3, bf16[256,1536]{1,0:T(8,128)(2,1)} %bitcast.12), custom_call_target="tpu_custom_call" | custom-call | flops 1 | bytes 1 | tf_op jit(solution)/shard_map/project/pallas_call | solution.py:359
  49.9 1.6 collective-permute-start.7
  53.5 3.8 %spread_rows.3.refs_4_ = bf16[2,512,1536]{2,1,0:T(8,128)(2,1)} custom-call(bf16[1040,384]{1,0:T(8,128)(2,1)} %hidden_rows.1.refs_0_, bf16[1040,384]{1,0:T(8,128)(2,1)} %copy-done.3), custom_call_target="tpu_custom_call" | custom-call | flops 1 | bytes 1 | tf_op jit(solution)/shard_map/spread_rows/pallas_call | solution.py:404
  57.2 2.2 %collective-permute-done.8.refs_2_ = bf16[2,256,128]{2,1,0:T(8,128)(2,1)S(1)} collective-permute-done((bf16[2,256,128]{2,1,0:T(8,128)(2,1)}, bf16[2,256,128]{2,1,0:T(8,128)(2,1)S(1)}, u32[]{:S(2)}, u32[]{:S(2)}) %collective-permute-start.8) | collective-permute-done | bytes 131104 | tf_op jit(solution)/shard_map/ppermute | solution.py:149
  60.2 2.2 %residual.2 = (bf16[2,256,128]{2,1,0:T(8,128)(2,1)}, bf16[512,128]{1,0:T(8,128)(2,1)}, f32[8,128]{1,0:T(8,128)}) custom-call(bf16[2,256,128]{2,1,0:T(8,128)(2,1)} %get-tuple-element.69.refs_0_, bf16[2,256,128]{2,1,0:T(8,128)(2,1)} %copy-done.24, bf16[2,256,128]{2,1,0:T(8,128)(2,1)} %copy-done.25, bf16[2,256,128]{2,1,0:T(8,128)(2,1)} %copy-done.26, ...), custom_call_target="tpu_custom_call" | custom-call | flops 1 | bytes 1 | tf_op jit(solution)/shard_map/residual/pallas_call | solution.py:455
  65.9 10.8 %collective-permute-done.5.refs_0_ = bf16[1040,384]{1,0:T(8,128)(2,1)S(1)} collective-permute-done((bf16[1040,384]{1,0:T(8,128)(2,1)}, bf16[1040,384]{1,0:T(8,128)(2,1)S(1)}, u32[]{:S(2)}, u32[]{:S(2)}) %collective-permute-start.5) | collective-permute-done | bytes 798752 | tf_op jit(solution)/shard_map/ppermute | solution.py:149
  76.7 2.3 %collective-permute-done.6.refs_2_ = bf16[1040,384]{1,0:T(8,128)(2,1)S(1)} collective-permute-done((bf16[1040,384]{1,0:T(8,128)(2,1)}, bf16[1040,384]{1,0:T(8,128)(2,1)S(1)}, u32[]{:S(2)}, u32[]{:S(2)}) %collective-permute-start.6) | collective-permute-done | bytes 798752 | tf_op jit(solution)/shard_map/ppermute | solution.py:149
  80.0 17.1 %collective-permute-done.18.refs_0_ = bf16[1040,384]{1,0:T(8,128)(2,1)S(1)} collective-permute-done((bf16[1040,384]{1,0:T(8,128)(2,1)S(1)}, bf16[1040,384]{1,0:T(8,128)(2,1)S(1)}, u32[]{:S(2)}, u32[]{:S(2)}) %collective-permute-start.18) | collective-permute-done | bytes 798752 | tf_op jit(solution)/shard_map/ppermute | solution.py:149
  98.0 6.3 %project.4 = (f32[4,8,128]{2,1,0:T(8,128)}, bf16[4,256,128]{2,1,0:T(8,128)(2,1)}, bf16[4,256,128]{2,1,0:T(8,128)(2,1)}, bf16[4,256,128]{2,1,0:T(8,128)(2,1)}, bf16[4,256,128]{2,1,0:T(8,128)(2,1)}) custom-call(bf16[1040,384]{1,0:T(8,128)(2,1)} %copy-done.4, bf16[1040,384]{1,0:T(8,128)(2,1)} %copy-done.6, bf16[1040,384]{1,0:T(8,128)(2,1)} %copy-done.5, ...), custom_call_target="tpu_custom_call" | custom-call | flops 1 | bytes 1 | tf_op jit(solution)/shard_map/project/pallas_call | solution.py:359
  104.3 1.6 collective-permute-start.15
  108.8 4.6 %project.5 = (f32[2,8,128]{2,1,0:T(8,128)}, bf16[2,256,128]{2,1,0:T(8,128)(2,1)}, bf16[2,256,128]{2,1,0:T(8,128)(2,1)}, bf16[2,256,128]{2,1,0:T(8,128)(2,1)}, bf16[2,256,128]{2,1,0:T(8,128)(2,1)}) custom-call(bf16[1040,384]{1,0:T(8,128)(2,1)} %copy-done.1, bf16[1040,384]{1,0:T(8,128)(2,1)} %copy-done.2, bf16[256,1536]{1,0:T(8,128)(2,1)} %bitcast.14), custom_call_target="tpu_custom_call" | custom-call | flops 1 | bytes 1 | tf_op jit(solution)/shard_map/project/pallas_call | solution.py:359
  116.9 5.2 %spread_rows.4.refs_5_ = bf16[4,512,1536]{2,1,0:T(8,128)(2,1)} custom-call(bf16[1040,384]{1,0:T(8,128)(2,1)} %copy-done.4, bf16[1040,384]{1,0:T(8,128)(2,1)} %copy-done.6, bf16[1040,384]{1,0:T(8,128)(2,1)} %copy-done.5, bf16[1040,384]{1,0:T(8,128)(2,1)} %collective-permute-done.14.refs_3_), custom_call_target="tpu_custom_call" | custom-call | flops 1 | bytes 1 | tf_op jit(solution)/shard_map/spread_rows/pallas_call | solution.py:404
  122.2 4.0 %spread_rows.5.refs_6_ = bf16[2,512,1536]{2,1,0:T(8,128)(2,1)} custom-call(bf16[1040,384]{1,0:T(8,128)(2,1)} %copy-done.1, bf16[1040,384]{1,0:T(8,128)(2,1)} %copy-done.2), custom_call_target="tpu_custom_call" | custom-call | flops 1 | bytes 1 | tf_op jit(solution)/shard_map/spread_rows/pallas_call | solution.py:404
  127.0 2.9 %residual.3 = (bf16[8,256,128]{2,1,0:T(8,128)(2,1)}, bf16[1536,128]{1,0:T(8,128)(2,1)}, f32[8,128]{1,0:T(8,128)}) custom-call(bf16[4,256,128]{2,1,0:T(8,128)(2,1)} %get-tuple-element.82.refs_0_, bf16[4,256,128]{2,1,0:T(8,128)(2,1)} %copy-done.15, bf16[4,256,128]{2,1,0:T(8,128)(2,1)} %copy-done.16, bf16[4,256,128]{2,1,0:T(8,128)(2,1)} %copy-done.17, ...), custom_call_target="tpu_custom_call" | custom-call | flops 1 | bytes 1 | tf_op jit(solution)/shard_map/residual/pallas_call | solution.py:455
  129.9 4.8 %all-to-all-start.1 = ((bf16[8,256,128]{2,1,0:T(8,128)(2,1)}), bf16[8,256,128]{2,1,0:T(8,128)(2,1)S(1)}, u32[]{:S(2)}, u32[]{:S(2)}) async-start(bf16[8,256,128]{2,1,0:T(8,128)(2,1)} %get-tuple-element.98), calls=%async_computation.1 | async-start | bytes 1048576 | tf_op jit(solution)/shard_map/all_to_all | solution.py:654
  140.0 2.4 %collective-permute-done.25 = f32[8,128]{1,0:T(8,128)S(1)} collective-permute-done((f32[8,128]{1,0:T(8,128)}, f32[8,128]{1,0:T(8,128)S(1)}, u32[]{:S(2)}, u32[]{:S(2)}) %collective-permute-start.25) | collective-permute-done | bytes 4128 | tf_op jit(solution)/shard_map/ppermute | solution.py:149
  143.4 2.4 %collective-permute-start.32 = (bf16[1536,128]{1,0:T(8,128)(2,1)}, bf16[1536,128]{1,0:T(8,128)(2,1)S(1)}, u32[]{:S(2)}, u32[]{:S(2)}) collective-permute-start(bf16[1536,128]{1,0:T(8,128)(2,1)} %get-tuple-element.110.refs_14_), channel_id=1, source_target_pairs={{0,3},{1,2},{2,1},{3,0},{4,7},{5,6},{6,5},{7,4},{8,11},{9,10},{10,... | collective-permute-start | bytes 1179656 | tf_op jit(solution)/shard_map/ppermute | solution.py:149
  147.7 2.0 %collective-permute-start.27 = (f32[8,128]{1,0:T(8,128)S(1)}, f32[8,128]{1,0:T(8,128)S(1)}, u32[]{:S(2)}, u32[]{:S(2)}) collective-permute-start(f32[8,128]{1,0:T(8,128)S(1)} %add.15.refs_0_), channel_id=1, source_target_pairs={{0,8},{4,12},{8,0},{12,4},{16,24},{20,28},{24,16},{28,20},{1,9},{5... | collective-permute-start | bytes 12296 | tf_op jit(solution)/shard_map/ppermute | solution.py:149
  149.8 2.4 %collective-permute-start.28 = (f32[8,128]{1,0:T(8,128)S(1)}, f32[8,128]{1,0:T(8,128)S(1)}, u32[]{:S(2)}, u32[]{:S(2)}) collective-permute-start(f32[8,128]{1,0:T(8,128)S(1)} %add.15.refs_0_), channel_id=1, source_target_pairs={{0,16},{4,20},{8,24},{12,28},{16,0},{20,4},{24,8},{28,12},{1,17},{... | collective-permute-start | bytes 12296 | tf_op jit(solution)/shard_map/ppermute | solution.py:149
  152.1 3.0 %collective-permute-start.29 = (f32[8,128]{1,0:T(8,128)S(1)}, f32[8,128]{1,0:T(8,128)S(1)}, u32[]{:S(2)}, u32[]{:S(2)}) collective-permute-start(f32[8,128]{1,0:T(8,128)S(1)} %add.15.refs_0_), channel_id=1, source_target_pairs={{0,24},{4,28},{8,16},{12,20},{16,8},{20,12},{24,0},{28,4},{1,25},{... | collective-permute-start | bytes 12296 | tf_op jit(solution)/shard_map/ppermute | solution.py:149
  155.2 2.4 %collective-permute-done.29.refs_3_ = f32[8,128]{1,0:T(8,128)S(1)} collective-permute-done((f32[8,128]{1,0:T(8,128)S(1)}, f32[8,128]{1,0:T(8,128)S(1)}, u32[]{:S(2)}, u32[]{:S(2)}) %collective-permute-start.29) | collective-permute-done | bytes 4128 | tf_op jit(solution)/shard_map/ppermute | solution.py:149
  157.5 3.6 %collective-permute-done.31.refs_16_ = bf16[1536,128]{1,0:T(8,128)(2,1)S(1)} collective-permute-done((bf16[1536,128]{1,0:T(8,128)(2,1)}, bf16[1536,128]{1,0:T(8,128)(2,1)S(1)}, u32[]{:S(2)}, u32[]{:S(2)}) %collective-permute-start.31) | collective-permute-done | bytes 393248 | tf_op jit(solution)/shard_map/ppermute | solution.py:149
  162.6 9.7 %gradient.1 = (f32[256,4,384]{2,1,0:T(4,128)}, f32[1,64]{1,0:T(1,128)}, f32[1,64]{1,0:T(1,128)}) custom-call(f32[8,128]{1,0:T(8,128)} %copy-done.27, f32[8,128]{1,0:T(8,128)} %copy-done.28, f32[8,128]{1,0:T(8,128)} %copy-done.29, f32[8,128]{1,0:T(8,128)} %copy-done.30, bf16[2,512,1536]{2,1,0:T(8,128)(2,1)} %spread_rows.3.refs_4_, ...), custom_call_target="tpu_custom_call" | custom-call | flops 1 | bytes 1 | tf_op jit(solution)/shard_map/gradient/pallas_call | solution.py:560
  (118 shorter events, 32.7 us)
Async XLA Ops:
  2.7 18.4 %collective-permute-start = (bf16[144,2048]{1,0:T(8,128)(2,1)}, bf16[144,2048]{1,0:T(8,128)(2,1)S(1)}, u32[]{:S(2)}, u32[]{:S(2)}) collective-permute-start(bf16[144,2048]{1,0:T(8,128)(2,1)} %pack_tokens.1.own), channel_id=1, source_target_pairs={{0,1},{1,0},{2,3},{3,2},{4,5},{5,4},{6,7},{7,6},{8,9},{9,8},{10,11... | collective-permute-start | bytes 1769480 | tf_op jit(solution)/shard_map/ppermute | solution.py:149
  5.6 15.0 %collective-permute-start.1 = (bf16[144,2048]{1,0:T(8,128)(2,1)}, bf16[144,2048]{1,0:T(8,128)(2,1)S(1)}, u32[]{:S(2)}, u32[]{:S(2)}) collective-permute-start(bf16[144,2048]{1,0:T(8,128)(2,1)} %pack_tokens.1.own), channel_id=1, source_target_pairs={{0,2},{1,3},{2,0},{3,1},{4,6},{5,7},{6,4},{7,5},{8,10},{9,11},{10,... | collective-permute-start | bytes 1769480 | tf_op jit(solution)/shard_map/ppermute | solution.py:149
  9.2 20.3 %all-to-all-start = ((bf16[8,256,128]{2,1,0:T(8,128)(2,1)}), bf16[8,256,128]{2,1,0:T(8,128)(2,1)S(1)}, u32[]{:S(2)}, u32[]{:S(2)}) async-start(bf16[8,256,128]{2,1,0:T(8,128)(2,1)} %bitcast.5), calls=%async_computation | async-start | bytes 1048576 | tf_op jit(solution)/shard_map/all_to_all | solution.py:613
  20.7 8.3 %collective-permute-start.2 = (bf16[80,2048]{1,0:T(8,128)(2,1)S(1)}, bf16[80,2048]{1,0:T(8,128)(2,1)S(1)}, u32[]{:S(2)}, u32[]{:S(2)}) collective-permute-start(bf16[80,2048]{1,0:T(8,128)(2,1)S(1)} %slice.8), channel_id=1, source_target_pairs={{0,1},{1,0},{2,3},{3,2},{4,5},{5,4},{6,7},{7,6},{8,9},{9,8},{10,11... | collective-permute-start | bytes 983048 | tf_op jit(solution)/shard_map/ppermute | solution.py:149
  21.1 8.4 %collective-permute-start.3 = (bf16[80,2048]{1,0:T(8,128)(2,1)S(1)}, bf16[80,2048]{1,0:T(8,128)(2,1)S(1)}, u32[]{:S(2)}, u32[]{:S(2)}) collective-permute-start(bf16[80,2048]{1,0:T(8,128)(2,1)S(1)} %slice.9), channel_id=1, source_target_pairs={{0,2},{1,3},{2,0},{3,1},{4,6},{5,7},{6,4},{7,5},{8,10},{9,11},{10,... | collective-permute-start | bytes 983048 | tf_op jit(solution)/shard_map/ppermute | solution.py:149
  39.2 5.2 %collective-permute-start.4 = (bf16[1040,384]{1,0:T(8,128)(2,1)}, bf16[1040,384]{1,0:T(8,128)(2,1)S(1)}, u32[]{:S(2)}, u32[]{:S(2)}) collective-permute-start(bf16[1040,384]{1,0:T(8,128)(2,1)} %hidden_rows.1.refs_0_), channel_id=1, source_target_pairs={{0,4},{4,0},{8,12},{12,8},{16,20},{20,16},{24,28},{28,24},{1,5},{5... | collective-permute-start | bytes 2396168 | tf_op jit(solution)/shard_map/ppermute | solution.py:149
  39.3 37.4 %collective-permute-start.5 = (bf16[1040,384]{1,0:T(8,128)(2,1)}, bf16[1040,384]{1,0:T(8,128)(2,1)S(1)}, u32[]{:S(2)}, u32[]{:S(2)}) collective-permute-start(bf16[1040,384]{1,0:T(8,128)(2,1)} %hidden_rows.1.refs_0_), channel_id=1, source_target_pairs={{0,8},{4,12},{8,0},{12,4},{16,24},{20,28},{24,16},{28,20},{1,9},{5... | collective-permute-start | bytes 2396168 | tf_op jit(solution)/shard_map/ppermute | solution.py:149
  40.8 38.2 %collective-permute-start.6 = (bf16[1040,384]{1,0:T(8,128)(2,1)}, bf16[1040,384]{1,0:T(8,128)(2,1)S(1)}, u32[]{:S(2)}, u32[]{:S(2)}) collective-permute-start(bf16[1040,384]{1,0:T(8,128)(2,1)} %hidden_rows.1.refs_0_), channel_id=1, source_target_pairs={{0,16},{4,20},{8,24},{12,28},{16,0},{20,4},{24,8},{28,12},{1,17},{... | collective-permute-start | bytes 2396168 | tf_op jit(solution)/shard_map/ppermute | solution.py:149
  49.9 7.3 %collective-permute-start.7 = (bf16[2,256,128]{2,1,0:T(8,128)(2,1)}, bf16[2,256,128]{2,1,0:T(8,128)(2,1)S(1)}, u32[]{:S(2)}, u32[]{:S(2)}) collective-permute-start(bf16[2,256,128]{2,1,0:T(8,128)(2,1)} %get-tuple-element.66), channel_id=1, source_target_pairs={{0,1},{1,0},{2,3},{3,2},{4,5},{5,4},{6,7},{7,6},{8,9},{9,8},{10,11... | collective-permute-start | bytes 393224 | tf_op jit(solution)/shard_map/ppermute | solution.py:149
  51.5 8.0 %collective-permute-start.8 = (bf16[2,256,128]{2,1,0:T(8,128)(2,1)}, bf16[2,256,128]{2,1,0:T(8,128)(2,1)S(1)}, u32[]{:S(2)}, u32[]{:S(2)}) collective-permute-start(bf16[2,256,128]{2,1,0:T(8,128)(2,1)} %get-tuple-element.67), channel_id=1, source_target_pairs={{0,2},{1,3},{2,0},{3,1},{4,6},{5,7},{6,4},{7,5},{8,10},{9,11},{10,... | collective-permute-start | bytes 393224 | tf_op jit(solution)/shard_map/ppermute | solution.py:149
  53.0 6.5 %collective-permute-start.9 = (bf16[2,256,128]{2,1,0:T(8,128)(2,1)}, bf16[2,256,128]{2,1,0:T(8,128)(2,1)S(1)}, u32[]{:S(2)}, u32[]{:S(2)}) collective-permute-start(bf16[2,256,128]{2,1,0:T(8,128)(2,1)} %get-tuple-element.68), channel_id=1, source_target_pairs={{0,3},{1,2},{2,1},{3,0},{4,7},{5,6},{6,5},{7,4},{8,11},{9,10},{10,... | collective-permute-start | bytes 393224 | tf_op jit(solution)/shard_map/ppermute | solution.py:149
  62.4 16.6 %collective-permute-start.10 = (bf16[512,128]{1,0:T(8,128)(2,1)}, bf16[512,128]{1,0:T(8,128)(2,1)S(1)}, u32[]{:S(2)}, u32[]{:S(2)}) collective-permute-start(bf16[512,128]{1,0:T(8,128)(2,1)} %get-tuple-element.75.refs_10_), channel_id=1, source_target_pairs={{0,1},{1,0},{2,3},{3,2},{4,5},{5,4},{6,7},{7,6},{8,9},{9,8},{10,11... | collective-permute-start | bytes 393224 | tf_op jit(solution)/shard_map/ppermute | solution.py:149
  63.6 15.4 %collective-permute-start.11 = (bf16[512,128]{1,0:T(8,128)(2,1)}, bf16[512,128]{1,0:T(8,128)(2,1)S(1)}, u32[]{:S(2)}, u32[]{:S(2)}) collective-permute-start(bf16[512,128]{1,0:T(8,128)(2,1)} %get-tuple-element.75.refs_10_), channel_id=1, source_target_pairs={{0,2},{1,3},{2,0},{3,1},{4,6},{5,7},{6,4},{7,5},{8,10},{9,11},{10,... | collective-permute-start | bytes 393224 | tf_op jit(solution)/shard_map/ppermute | solution.py:149
  64.4 14.5 %collective-permute-start.12 = (bf16[512,128]{1,0:T(8,128)(2,1)}, bf16[512,128]{1,0:T(8,128)(2,1)S(1)}, u32[]{:S(2)}, u32[]{:S(2)}) collective-permute-start(bf16[512,128]{1,0:T(8,128)(2,1)} %get-tuple-element.75.refs_10_), channel_id=1, source_target_pairs={{0,3},{1,2},{2,1},{3,0},{4,7},{5,6},{6,5},{7,4},{8,11},{9,10},{10,... | collective-permute-start | bytes 393224 | tf_op jit(solution)/shard_map/ppermute | solution.py:149
  79.0 18.1 %collective-permute-start.18 = (bf16[1040,384]{1,0:T(8,128)(2,1)S(1)}, bf16[1040,384]{1,0:T(8,128)(2,1)S(1)}, u32[]{:S(2)}, u32[]{:S(2)}) collective-permute-start(bf16[1040,384]{1,0:T(8,128)(2,1)S(1)} %collective-permute-done.6.refs_2_), channel_id=1, source_target_pairs={{0,8},{4,12},{8,0},{12,4},{16,24},{20,28},{24,16},{28,20},{1,9},{5... | collective-permute-start | bytes 2396168 | tf_op jit(solution)/shard_map/ppermute | solution.py:149
  79.5 17.6 %collective-permute-start.13 = (bf16[1040,384]{1,0:T(8,128)(2,1)S(1)}, bf16[1040,384]{1,0:T(8,128)(2,1)S(1)}, u32[]{:S(2)}, u32[]{:S(2)}) collective-permute-start(bf16[1040,384]{1,0:T(8,128)(2,1)S(1)} %collective-permute-done.5.refs_0_), channel_id=1, source_target_pairs={{0,4},{4,0},{8,12},{12,8},{16,20},{20,16},{24,28},{28,24},{1,5},{5... | collective-permute-start | bytes 2396168 | tf_op jit(solution)/shard_map/ppermute | solution.py:149
  79.5 18.5 %collective-permute-start.14 = (bf16[1040,384]{1,0:T(8,128)(2,1)S(1)}, bf16[1040,384]{1,0:T(8,128)(2,1)}, u32[]{:S(2)}, u32[]{:S(2)}) collective-permute-start(bf16[1040,384]{1,0:T(8,128)(2,1)S(1)} %collective-permute-done.6.refs_2_), channel_id=1, source_target_pairs={{0,4},{4,0},{8,12},{12,8},{16,20},{20,16},{24,28},{28,24},{1,5},{5... | collective-permute-start | bytes 2396168 | tf_op jit(solution)/shard_map/ppermute | solution.py:149
  97.1 10.8 %collective-permute-start.19 = (bf16[1040,384]{1,0:T(8,128)(2,1)S(1)}, bf16[1040,384]{1,0:T(8,128)(2,1)S(1)}, u32[]{:S(2)}, u32[]{:S(2)}) collective-permute-start(bf16[1040,384]{1,0:T(8,128)(2,1)S(1)} %collective-permute-done.18.refs_0_), channel_id=1, source_target_pairs={{0,4},{4,0},{8,12},{12,8},{16,20},{20,16},{24,28},{28,24},{1,5},{5... | collective-permute-start | bytes 2396168 | tf_op jit(solution)/shard_map/ppermute | solution.py:149
  104.3 12.1 %collective-permute-start.15 = (bf16[4,256,128]{2,1,0:T(8,128)(2,1)}, bf16[4,256,128]{2,1,0:T(8,128)(2,1)S(1)}, u32[]{:S(2)}, u32[]{:S(2)}) collective-permute-start(bf16[4,256,128]{2,1,0:T(8,128)(2,1)} %get-tuple-element.79), channel_id=1, source_target_pairs={{0,1},{1,0},{2,3},{3,2},{4,5},{5,4},{6,7},{7,6},{8,9},{9,8},{10,11... | collective-permute-start | bytes 786440 | tf_op jit(solution)/shard_map/ppermute | solution.py:149
  105.9 16.3 %collective-permute-start.16 = (bf16[4,256,128]{2,1,0:T(8,128)(2,1)}, bf16[4,256,128]{2,1,0:T(8,128)(2,1)S(1)}, u32[]{:S(2)}, u32[]{:S(2)}) collective-permute-start(bf16[4,256,128]{2,1,0:T(8,128)(2,1)} %get-tuple-element.80), channel_id=1, source_target_pairs={{0,2},{1,3},{2,0},{3,1},{4,6},{5,7},{6,4},{7,5},{8,10},{9,11},{10,... | collective-permute-start | bytes 786440 | tf_op jit(solution)/shard_map/ppermute | solution.py:149
  107.4 14.8 %collective-permute-start.17 = (bf16[4,256,128]{2,1,0:T(8,128)(2,1)}, bf16[4,256,128]{2,1,0:T(8,128)(2,1)S(1)}, u32[]{:S(2)}, u32[]{:S(2)}) collective-permute-start(bf16[4,256,128]{2,1,0:T(8,128)(2,1)} %get-tuple-element.81), channel_id=1, source_target_pairs={{0,3},{1,2},{2,1},{3,0},{4,7},{5,6},{6,5},{7,4},{8,11},{9,10},{10,... | collective-permute-start | bytes 786440 | tf_op jit(solution)/shard_map/ppermute | solution.py:149
  113.4 12.9 %collective-permute-start.20 = (bf16[2,256,128]{2,1,0:T(8,128)(2,1)}, bf16[2,256,128]{2,1,0:T(8,128)(2,1)S(1)}, u32[]{:S(2)}, u32[]{:S(2)}) collective-permute-start(bf16[2,256,128]{2,1,0:T(8,128)(2,1)} %get-tuple-element.87), channel_id=1, source_target_pairs={{0,1},{1,0},{2,3},{3,2},{4,5},{5,4},{6,7},{7,6},{8,9},{9,8},{10,11... | collective-permute-start | bytes 393224 | tf_op jit(solution)/shard_map/ppermute | solution.py:149
  114.9 11.3 %collective-permute-start.21 = (bf16[2,256,128]{2,1,0:T(8,128)(2,1)}, bf16[2,256,128]{2,1,0:T(8,128)(2,1)S(1)}, u32[]{:S(2)}, u32[]{:S(2)}) collective-permute-start(bf16[2,256,128]{2,1,0:T(8,128)(2,1)} %get-tuple-element.88), channel_id=1, source_target_pairs={{0,2},{1,3},{2,0},{3,1},{4,6},{5,7},{6,4},{7,5},{8,10},{9,11},{10,... | collective-permute-start | bytes 393224 | tf_op jit(solution)/shard_map/ppermute | solution.py:149
  116.4 9.8 %collective-permute-start.22 = (bf16[2,256,128]{2,1,0:T(8,128)(2,1)}, bf16[2,256,128]{2,1,0:T(8,128)(2,1)S(1)}, u32[]{:S(2)}, u32[]{:S(2)}) collective-permute-start(bf16[2,256,128]{2,1,0:T(8,128)(2,1)} %get-tuple-element.89), channel_id=1, source_target_pairs={{0,3},{1,2},{2,1},{3,0},{4,7},{5,6},{6,5},{7,4},{8,11},{9,10},{10,... | collective-permute-start | bytes 393224 | tf_op jit(solution)/shard_map/ppermute | solution.py:149
  129.9 42.5 %all-to-all-start.1 = ((bf16[8,256,128]{2,1,0:T(8,128)(2,1)}), bf16[8,256,128]{2,1,0:T(8,128)(2,1)S(1)}, u32[]{:S(2)}, u32[]{:S(2)}) async-start(bf16[8,256,128]{2,1,0:T(8,128)(2,1)} %get-tuple-element.98), calls=%async_computation.1 | async-start | bytes 1048576 | tf_op jit(solution)/shard_map/all_to_all | solution.py:654
  137.7 4.7 %collective-permute-start.25 = (f32[8,128]{1,0:T(8,128)}, f32[8,128]{1,0:T(8,128)S(1)}, u32[]{:S(2)}, u32[]{:S(2)}) collective-permute-start(f32[8,128]{1,0:T(8,128)} %get-tuple-element.99), channel_id=1, source_target_pairs={{0,3},{1,2},{2,1},{3,0},{4,7},{5,6},{6,5},{7,4},{8,11},{9,10},{10,... | collective-permute-start | bytes 12296 | tf_op jit(solution)/shard_map/ppermute | solution.py:149
  142.4 15.1 %collective-permute-start.30 = (bf16[1536,128]{1,0:T(8,128)(2,1)}, bf16[1536,128]{1,0:T(8,128)(2,1)S(1)}, u32[]{:S(2)}, u32[]{:S(2)}) collective-permute-start(bf16[1536,128]{1,0:T(8,128)(2,1)} %get-tuple-element.110.refs_14_), channel_id=1, source_target_pairs={{0,1},{1,0},{2,3},{3,2},{4,5},{5,4},{6,7},{7,6},{8,9},{9,8},{10,11... | collective-permute-start | bytes 1179656 | tf_op jit(solution)/shard_map/ppermute | solution.py:149
  142.9 18.2 %collective-permute-start.31 = (bf16[1536,128]{1,0:T(8,128)(2,1)}, bf16[1536,128]{1,0:T(8,128)(2,1)S(1)}, u32[]{:S(2)}, u32[]{:S(2)}) collective-permute-start(bf16[1536,128]{1,0:T(8,128)(2,1)} %get-tuple-element.110.refs_14_), channel_id=1, source_target_pairs={{0,2},{1,3},{2,0},{3,1},{4,6},{5,7},{6,4},{7,5},{8,10},{9,11},{10,... | collective-permute-start | bytes 1179656 | tf_op jit(solution)/shard_map/ppermute | solution.py:149
  143.4 17.7 %collective-permute-start.32 = (bf16[1536,128]{1,0:T(8,128)(2,1)}, bf16[1536,128]{1,0:T(8,128)(2,1)S(1)}, u32[]{:S(2)}, u32[]{:S(2)}) collective-permute-start(bf16[1536,128]{1,0:T(8,128)(2,1)} %get-tuple-element.110.refs_14_), channel_id=1, source_target_pairs={{0,3},{1,2},{2,1},{3,0},{4,7},{5,6},{6,5},{7,4},{8,11},{9,10},{10,... | collective-permute-start | bytes 1179656 | tf_op jit(solution)/shard_map/ppermute | solution.py:149
  147.7 4.4 %collective-permute-start.27 = (f32[8,128]{1,0:T(8,128)S(1)}, f32[8,128]{1,0:T(8,128)S(1)}, u32[]{:S(2)}, u32[]{:S(2)}) collective-permute-start(f32[8,128]{1,0:T(8,128)S(1)} %add.15.refs_0_), channel_id=1, source_target_pairs={{0,8},{4,12},{8,0},{12,4},{16,24},{20,28},{24,16},{28,20},{1,9},{5... | collective-permute-start | bytes 12296 | tf_op jit(solution)/shard_map/ppermute | solution.py:149
  149.8 5.4 %collective-permute-start.28 = (f32[8,128]{1,0:T(8,128)S(1)}, f32[8,128]{1,0:T(8,128)S(1)}, u32[]{:S(2)}, u32[]{:S(2)}) collective-permute-start(f32[8,128]{1,0:T(8,128)S(1)} %add.15.refs_0_), channel_id=1, source_target_pairs={{0,16},{4,20},{8,24},{12,28},{16,0},{20,4},{24,8},{28,12},{1,17},{... | collective-permute-start | bytes 12296 | tf_op jit(solution)/shard_map/ppermute | solution.py:149
  152.1 5.4 %collective-permute-start.29 = (f32[8,128]{1,0:T(8,128)S(1)}, f32[8,128]{1,0:T(8,128)S(1)}, u32[]{:S(2)}, u32[]{:S(2)}) collective-permute-start(f32[8,128]{1,0:T(8,128)S(1)} %add.15.refs_0_), channel_id=1, source_target_pairs={{0,24},{4,28},{8,16},{12,20},{16,8},{20,12},{24,0},{28,4},{1,25},{... | collective-permute-start | bytes 12296 | tf_op jit(solution)/shard_map/ppermute | solution.py:149
  (34 other events, 420.1 us)

commit v2 on v1

--- a/solution.py
+++ b/solution.py
@@ -315,7 +315,7 @@
             pltpu.SemaphoreType.DMA((exp_dev,)),
         ],
         cost_estimate=cost(),
-        compiler_params=params(),
+        compiler_params=params(36),
         name="hidden_rows",
     )(*tokens, w_gate, w_up)
 
@@ -331,8 +331,11 @@
     partials, (packed, outs, places, arrived) = refs[:sources], refs[sources:]
     units = w_down.shape[1] // exp_dev
     total = sources * capacity
-    for s in range(slots):
-        pltpu.make_async_copy(blocks[s], packed.at[s], arrived.at[s]).start()
+    fetches = [
+        pltpu.make_async_copy(blocks[s], packed.at[s], arrived.at[s]) for s in range(slots)
+    ]
+    for copy in fetches:
+        copy.start()
 
     def one_slot(s, carry):
         pltpu.make_async_copy(packed.at[s], packed.at[s], arrived.at[s]).wait()
@@ -369,7 +372,7 @@
             pltpu.SemaphoreType.DMA((slots,)),
         ],
         cost_estimate=cost(),
-        compiler_params=params(),
+        compiler_params=params(16),
         name="project",
     )(*blocks, w_down)
     return out[0], out[1:]
@@ -380,8 +383,11 @@
     blocks, (spread, packed, held, arrived, done) = refs[:slots], refs[slots:]
     units = packed.shape[2]
     total = sources * capacity
-    for s in range(slots):
-        pltpu.make_async_copy(blocks[s], packed.at[s], arrived.at[s]).start()
+    fetches = [
+        pltpu.make_async_copy(blocks[s], packed.at[s], arrived.at[s]) for s in range(slots)
+    ]
+    for copy in fetches:
+        copy.start()
 
     def one_slot(s, carry):
         pltpu.make_async_copy(packed.at[s], packed.at[s], arrived.at[s]).wait()
@@ -413,7 +419,7 @@
             pltpu.SemaphoreType.DMA((slots,)),
         ],
         cost_estimate=cost(),
-        compiler_params=params(),
+        compiler_params=params(24),
         name="spread_rows",
     )(*blocks)
 
@@ -422,21 +428,24 @@
     parts, refs = refs[: sources * len(batches)], refs[sources * len(batches) :]
     seqs, (targets, *refs) = refs[: len(batches)], refs[len(batches) :]
     if first:
-        before, earlier, *refs = refs
-    combined, errors, squares = refs
+        before, refs = refs[0], refs[1:]
+    combined, errors, squares = refs[-3:]
     feats, rows = targets.shape[1:]
     me = lax.axis_index("dp")
     number = lax.broadcasted_iota(jnp.int32, (NSEQ, rows), 0).astype(FLOAT)
     squared = jnp.zeros((NSEQ, rows), FLOAT)
-    if first:
-        for s in range(first):
-            combined[me ^ s] = earlier[s]
+    slot = 0
+    for block in refs[:-3]:
+        for s in range(block.shape[0]):
+            combined[me ^ slot] = block[s]
+            slot += 1
+    ordered = len(refs) > 3
     slot = 0
     for b, slots in enumerate(batches):
         here = parts[b * sources : (b + 1) * sources]
         for s in range(slots):
             total = tree_sum([part[s].astype(FLOAT) for part in here])
-            combined[me ^ (first + slot) if first else slot] = total.astype(HALF)
+            combined[me ^ (first + slot) if ordered else slot] = total.astype(HALF)
             error = total - targets[me ^ (first + slot)].astype(FLOAT)
             errors[slot * feats : (slot + 1) * feats, :] = error.astype(HALF)
             per_token = jnp.sum(error * error, axis=0, keepdims=True)
@@ -451,18 +460,18 @@
     batches = tuple(batch[0].shape[0] for batch in parts)
     sources = len(parts[0])
     slots = sum(batches)
-    extra = [before, earlier] if first else []
+    extra = [before, *earlier] if first else []
     return pl.pallas_call(
         functools.partial(residual_kernel, first, batches, sources),
         in_specs=in_vmem((sources + 1) * len(batches) + 1 + len(extra)),
         out_specs=in_vmem(3),
         out_shape=[
-            jax.ShapeDtypeStruct((first + slots, feats, rows), HALF),
+            jax.ShapeDtypeStruct((slots + first * (len(earlier) > 0), feats, rows), HALF),
             jax.ShapeDtypeStruct((slots * feats, rows), HALF),
             jax.ShapeDtypeStruct((8, LANES), FLOAT),
         ],
         cost_estimate=cost(),
-        compiler_params=params(),
+        compiler_params=params(16),
         name="residual",
     )(*[part for batch in parts for part in batch], *seqs, targets, *extra)
 
@@ -489,7 +498,11 @@
     for seq, spread, slots in zip(seqs, spreads, batches):
         for s in range(slots):
             lines[slot] = seq[s]
-            pltpu.make_async_copy(spread.at[s], held.at[slot], arrived.at[1, slot]).start()
+            pltpu.make_async_copy(
+                spread.at[s],
+                held.at[slot // 2, pl.ds(slot % 2 * sources * rows, sources * rows)],
+                arrived.at[1, slot // 2],
+            ).start()
             slot += 1
     number = lax.broadcasted_iota(jnp.int32, (NSEQ, rows), 0).astype(FLOAT)
 
@@ -511,22 +524,26 @@
     for s in range(groups):
         pltpu.make_async_copy(error.at[s], error.at[s], arrived.at[0, s]).wait()
 
-    def weigh(s, turn):
-        for m in range(sources):
-            here = slice(m * rows, (m + 1) * rows)
-            hit = jnp.where(lines[s, m : m + 1, :] == number, rates[...], 0.0)
-            rate = jnp.sum(hit, axis=0, keepdims=True)
-            weighted[turn, :, here] = (rate * error[s, :, here].astype(FLOAT)).astype(HALF)
-
-    def add_slot(s, carry):
-        pltpu.make_async_copy(held.at[s], held.at[s], arrived.at[1, s]).wait()
-        product = dot_nn(weighted[s % 2], held[s])
-        weigh(jnp.minimum(s + 1, groups - 1), (s + 1) % 2)
+    def weigh(pair, turn):
+        for k in range(2):
+            for m in range(sources):
+                here = slice(m * rows, (m + 1) * rows)
+                there = slice((k * sources + m) * rows, (k * sources + m + 1) * rows)
+                hit = jnp.where(lines[2 * pair + k, m : m + 1, :] == number, rates[...], 0.0)
+                rate = jnp.sum(hit, axis=0, keepdims=True)
+                weighted[turn, :, there] = (
+                    rate * error[2 * pair + k, :, here].astype(FLOAT)
+                ).astype(HALF)
+
+    def add_pair(pair, carry):
+        pltpu.make_async_copy(held.at[pair], held.at[pair], arrived.at[1, pair]).wait()
+        product = dot_nn(weighted[pair % 2], held[pair])
+        weigh(jnp.minimum(pair + 1, groups // 2 - 1), (pair + 1) % 2)
         total[...] += product
         return carry
 
     weigh(0, 0)
-    lax.fori_loop(0, groups, add_slot, 0)
+    lax.fori_loop(0, groups // 2, add_pair, 0)
     units = grad.shape[2]
     for e in range(exp_dev):
         grad[:, e, :] = total[:, e * units : (e + 1) * units]
@@ -572,10 +589,10 @@
             jax.ShapeDtypeStruct((1, NSEQ), FLOAT),
         ],
         scratch_shapes=[
-            pltpu.VMEM((groups, group_rows, flat), HALF),
+            pltpu.VMEM((groups // 2, 2 * group_rows, flat), HALF),
             pltpu.VMEM((groups, feats, group_rows), HALF),
             pltpu.VMEM((groups, 8, rows), FLOAT),
-            pltpu.VMEM((2, feats, group_rows), HALF),
+            pltpu.VMEM((2, feats, 2 * group_rows), HALF),
             pltpu.VMEM((feats, flat), FLOAT),
             pltpu.VMEM((NSEQ, rows), FLOAT),
             pltpu.SemaphoreType.DMA((2, groups)),
@@ -635,15 +652,16 @@
 
     batches = (2, groups - 4, 2)
     spread_0, seq_0, parts_0 = expert_parts(0, batches[0])
-    mixed_0, error_0, squares_0 = residual(0, [parts_0], [seq_0], own_targets, None, None)
+    mixed_0, error_0, squares = residual(0, [parts_0], [seq_0], own_targets, None, [])
     errors_0 = far_errors(error_0)
     blocks, errors_0 = tie((blocks, errors_0))
     blocks[6] = z_far(blocks)
 
     spread_1, seq_1, parts_1 = expert_parts(2, batches[1])
+    blocks[6], parts_1 = tie((blocks[6], parts_1))
     spread_2, seq_2, parts_2 = expert_parts(groups - 2, batches[2])
     mixed, error_1, squares = residual(
-        2, [parts_1, parts_2], [seq_1, seq_2], own_targets, squares_0, mixed_0
+        2, [parts_1, parts_2], [seq_1, seq_2], own_targets, squares, [mixed_0]
     )
     far_squares = [swap(squares, "expert", m) for m in far]
     error_1, far_squares = tie((error_1, far_squares))

time: 174 us -> 160 us (0.920)
  Pallas kernels: 54.3 us -> 34.1 us
  local copies, waits for them, and re-layouts: 10.5 us -> 15.7 us
  waiting for transfers between devices: 56.9 us -> 60.6 us
    pallas_call x3, Pallas kernels: 15.5 us -> 6.56 us  [project(): pl.pallas_call(functools.partial(project_kernel, exp_dev, capacity, rows,...]
    all_to_all x1, waiting for transfers between devices: 0.01 us -> 6.81 us  [feature_plan(): lax.all_to_all(turned.reshape(groups, feats, rows), 'dp', split_axis=0, c...]
    pallas_call x3, Pallas kernels: 13 us -> 7.42 us  [spread_rows(): pl.pallas_call(functools.partial(spread_kernel, exp_dev, capacity, rows,...]
    unnamed x63 -> x45, local copies, waits for them, and re-layouts: 7.38 us -> 12.6 us
    pallas_call x2, Pallas kernels: 5.05 us -> 1.43 us  [residual(): pl.pallas_call(functools.partial(residual_kernel, first, batches, sources...]
    ppermute x33, waiting for transfers between devices: 56.9 us -> 53.8 us  [swap(): return lax.ppermute(block, axis, [(s, s ^ mask) for s in range(size)])]
    pallas_call x1, Pallas kernels: 8.95 us -> 6.97 us  [hidden_rows(): pl.pallas_call(functools.partial(hidden_kernel, experts, capacity), in_sp...]
  transfers between devices with their start and end apart: 35 -> 35, of which waited for: 13 -> 21; matrix products, arithmetic and copies ran while one was open for 2% -> 1% of each run, Pallas kernels for 23% -> 14%
where the time goes in v2:
time: 160 us
  waiting for transfers between devices  60.6 us (38%)
  starting transfers between devices  48.6 us (30%)
  Pallas kernels  34.1 us (21%)
  local copies, waits for them, and re-layouts  15.7 us (10%)
    ppermute x33, waiting for transfers between devices, swap(): return lax.ppermute(block, axis, [(s, s ^ mask) for s in range(size)])  53.8 us
    ppermute x33, starting transfers between devices, swap(): return lax.ppermute(block, axis, [(s, s ^ mask) for s in range(size)])  39.3 us
    unnamed x45, local copies, waits for them, and re-layouts  12.6 us
    pallas_call x1, Pallas kernels, gradient(): pl.pallas_call(functools.partial(gradient_kernel, scale, feat_width, exp_...  9.68 us
    pallas_call x3, Pallas kernels, spread_rows(): pl.pallas_call(functools.partial(spread_kernel, exp_dev, capacity, rows,...  7.42 us
    pallas_call x1, Pallas kernels, hidden_rows(): pl.pallas_call(functools.partial(hidden_kernel, experts, capacity), in_sp...  6.97 us
    all_to_all x1, waiting for transfers between devices, feature_plan(): lax.all_to_all(turned.reshape(groups, feats, rows), 'dp', split_axis=0, c...  6.81 us
    pallas_call x3, Pallas kernels, project(): pl.pallas_call(functools.partial(project_kernel, exp_dev, capacity, rows,...  6.56 us
  transfers between devices with their start and end apart: 35, of which 21 were waited for; matrix products, arithmetic and copies ran while one was open for 1% of the time, Pallas kernels for 14%

profile of v2, /device:TPU:0, one launch (start us, length us, event | category | flops | bytes accessed | tf_op | source)
XLA Modules:
  0.0 160.0 jit_solution(9942477852322076965)
XLA Ops:
  0.6 2.0 %pack_tokens.1.own = bf16[144,2048]{1,0:T(8,128)(2,1)} custom-call(bf16[128,2048]{1,0:T(8,128)(2,1)} %tokens.1, s32[8,128]{1,0:T(8,128)} %bitcast.19, f32[8,128]{1,0:T(8,128)} %bitcast.20, s32[8,128]{1,0:T(8,128)} %bitcast.21, s32[1,128]{1,0:T(1,128)} %bitcast.22), custom_call_target="tpu_custom_call" | custom-call | flops 1 | bytes 1 | tf_op jit(solution)/shard_map/pack_tokens/pallas_call | solution.py:231
  2.7 3.0 %collective-permute-start.1 = (bf16[144,2048]{1,0:T(8,128)(2,1)}, bf16[144,2048]{1,0:T(8,128)(2,1)S(1)}, u32[]{:S(2)}, u32[]{:S(2)}) collective-permute-start(bf16[144,2048]{1,0:T(8,128)(2,1)} %pack_tokens.1.own), channel_id=1, source_target_pairs={{0,2},{1,3},{2,0},{3,1},{4,6},{5,7},{6,4},{7,5},{8,10},{9,11},{10,... | collective-permute-start | bytes 1769480 | tf_op jit(solution)/shard_map/ppermute | solution.py:149
  7.1 2.0 %copy.13 = bf16[2048,128]{1,0:T(8,128)(2,1)} copy(bf16[2048,128]{0,1:T(8,128)(2,1)} %bitcast.17) | data formatting | bytes 1048576 | tf_op jit(solution)/shard_map/optimization_barrier | solution.py:629
  9.2 4.9 %all-to-all-start = ((bf16[8,256,128]{2,1,0:T(8,128)(2,1)}), bf16[8,256,128]{2,1,0:T(8,128)(2,1)S(1)}, u32[]{:S(2)}, u32[]{:S(2)}) async-start(bf16[8,256,128]{2,1,0:T(8,128)(2,1)} %bitcast.5), calls=%async_computation | async-start | bytes 1048576 | tf_op jit(solution)/shard_map/all_to_all | solution.py:630
  14.0 5.1 %collective-permute-done.1.y_side = bf16[144,2048]{1,0:T(8,128)(2,1)S(1)} collective-permute-done((bf16[144,2048]{1,0:T(8,128)(2,1)}, bf16[144,2048]{1,0:T(8,128)(2,1)S(1)}, u32[]{:S(2)}, u32[]{:S(2)}) %collective-permute-start.1) | collective-permute-done | bytes 589856 | tf_op jit(solution)/shard_map/ppermute | solution.py:149
  19.2 1.8 %collective-permute-start.2 = (bf16[80,2048]{1,0:T(8,128)(2,1)S(1)}, bf16[80,2048]{1,0:T(8,128)(2,1)S(1)}, u32[]{:S(2)}, u32[]{:S(2)}) collective-permute-start(bf16[80,2048]{1,0:T(8,128)(2,1)S(1)} %slice.8), channel_id=1, source_target_pairs={{0,1},{1,0},{2,3},{3,2},{4,5},{5,4},{6,7},{7,6},{8,9},{9,8},{10,11... | collective-permute-start | bytes 983048 | tf_op jit(solution)/shard_map/ppermute | solution.py:149
  22.6 6.8 %all-to-all-done.refs_5_.refs_10_ = bf16[8,256,128]{2,1,0:T(8,128)(2,1)S(1)} async-done(((bf16[8,256,128]{2,1,0:T(8,128)(2,1)}), bf16[8,256,128]{2,1,0:T(8,128)(2,1)S(1)}, u32[]{:S(2)}, u32[]{:S(2)}) %all-to-all-start) | async-done | bytes 524320 | tf_op jit(solution)/shard_map/all_to_all | solution.py:630
  29.4 2.8 %copy-done.3 = bf16[4,2048,384]{2,1,0:T(8,128)(2,1)S(1)} copy-done((bf16[4,2048,384]{2,1,0:T(8,128)(2,1)S(1)}, bf16[4,2048,384]{2,1,0:T(8,128)(2,1)}, u32[]{:S(2)}) %copy-start.3) | copy-done | bytes 6291480
  32.2 2.8 %copy-done.4 = bf16[4,2048,384]{2,1,0:T(8,128)(2,1)S(1)} copy-done((bf16[4,2048,384]{2,1,0:T(8,128)(2,1)S(1)}, bf16[4,2048,384]{2,1,0:T(8,128)(2,1)}, u32[]{:S(2)}) %copy-start.4) | copy-done | bytes 6291480
  36.0 7.0 %hidden_rows.1.refs_0_ = bf16[1040,384]{1,0:T(8,128)(2,1)S(1)} custom-call(bf16[144,2048]{1,0:T(8,128)(2,1)S(1)} %copy-done.5, bf16[144,2048]{1,0:T(8,128)(2,1)S(1)} %collective-permute-done.x_side, bf16[144,2048]{1,0:T(8,128)(2,1)S(1)} %collective-permute-done.1.y_side, bf16[80,2048]{1,0:T(8,128)(2,1)S(1)} %collective-permute-done.2.upper, ...), custom_call_target="tpu_custom_call" | custom-call | flops 1 | bytes 1 | tf_op jit(solution)/shard_map/hidden_rows/pallas_call | solution.py:304
  43.1 2.6 %collective-permute-start.6 = (bf16[1040,384]{1,0:T(8,128)(2,1)S(1)}, bf16[1040,384]{1,0:T(8,128)(2,1)S(1)}, u32[]{:S(2)}, u32[]{:S(2)}) collective-permute-start(bf16[1040,384]{1,0:T(8,128)(2,1)S(1)} %hidden_rows.1.refs_0_), channel_id=1, source_target_pairs={{0,16},{4,20},{8,24},{12,28},{16,0},{20,4},{24,8},{28,12},{1,17},{... | collective-permute-start | bytes 2396168 | tf_op jit(solution)/shard_map/ppermute | solution.py:149
  47.4 1.6 %project.3 = (f32[2,8,128]{2,1,0:T(8,128)S(1)}, bf16[2,256,128]{2,1,0:T(8,128)(2,1)S(1)}, bf16[2,256,128]{2,1,0:T(8,128)(2,1)S(1)}, bf16[2,256,128]{2,1,0:T(8,128)(2,1)S(1)}, bf16[2,256,128]{2,1,0:T(8,128)(2,1)S(1)}) custom-call(bf16[1040,384]{1,0:T(8,128)(2,1)S(1)} %hidden_rows.1.refs_0_, bf16[1040,384]{1,0:T(8,128)(2,1)S(1)} %collective-permute-done.4.refs_1_, ...), custom_call_target="tpu_custom_call" | custom-call | flops 1 | bytes 1 | tf_op jit(solution)/shard_map/project/pallas_call | solution.py:362
  52.6 1.9 %spread_rows.3.refs_4_ = bf16[2,512,1536]{2,1,0:T(8,128)(2,1)S(1)} custom-call(bf16[1040,384]{1,0:T(8,128)(2,1)S(1)} %hidden_rows.1.refs_0_, bf16[1040,384]{1,0:T(8,128)(2,1)S(1)} %collective-permute-done.4.refs_1_), custom_call_target="tpu_custom_call" | custom-call | flops 1 | bytes 1 | tf_op jit(solution)/shard_map/spread_rows/pallas_call | solution.py:410
  56.6 1.6 %collective-permute-done.9.refs_3_ = bf16[2,256,128]{2,1,0:T(8,128)(2,1)S(1)} collective-permute-done((bf16[2,256,128]{2,1,0:T(8,128)(2,1)S(1)}, bf16[2,256,128]{2,1,0:T(8,128)(2,1)S(1)}, u32[]{:S(2)}, u32[]{:S(2)}) %collective-permute-start.9) | collective-permute-done | bytes 131104 | tf_op jit(solution)/shard_map/ppermute | solution.py:149
  58.4 1.8 %collective-permute-start.12 = (bf16[512,128]{1,0:T(8,128)(2,1)S(1)}, bf16[512,128]{1,0:T(8,128)(2,1)S(1)}, u32[]{:S(2)}, u32[]{:S(2)}) collective-permute-start(bf16[512,128]{1,0:T(8,128)(2,1)S(1)} %get-tuple-element.80.refs_10_), channel_id=1, source_target_pairs={{0,3},{1,2},{2,1},{3,0},{4,7},{5,6},{6,5},{7,4},{8,11},{9,10},{10,... | collective-permute-start | bytes 393224 | tf_op jit(solution)/shard_map/ppermute | solution.py:149
  62.0 19.5 %collective-permute-done.6.refs_2_ = bf16[1040,384]{1,0:T(8,128)(2,1)S(1)} collective-permute-done((bf16[1040,384]{1,0:T(8,128)(2,1)S(1)}, bf16[1040,384]{1,0:T(8,128)(2,1)S(1)}, u32[]{:S(2)}, u32[]{:S(2)}) %collective-permute-start.6) | collective-permute-done | bytes 798752 | tf_op jit(solution)/shard_map/ppermute | solution.py:149
  85.2 3.3 %project.4 = (f32[4,8,128]{2,1,0:T(8,128)S(1)}, bf16[4,256,128]{2,1,0:T(8,128)(2,1)S(1)}, bf16[4,256,128]{2,1,0:T(8,128)(2,1)S(1)}, bf16[4,256,128]{2,1,0:T(8,128)(2,1)S(1)}, bf16[4,256,128]{2,1,0:T(8,128)(2,1)S(1)}) custom-call(bf16[1040,384]{1,0:T(8,128)(2,1)S(1)} %collective-permute-done.5.refs_0_, bf16[1040,384]{1,0:T(8,128)(2,1)S(1)} %collective-permute-done.14.refs_1_, ...), custom_call_target="tpu_custom_call" | custom-call | flops 1 | bytes 1 | tf_op jit(solution)/shard_map/project/pallas_call | solution.py:362
  92.0 3.7 %spread_rows.4.refs_5_ = bf16[4,512,1536]{2,1,0:T(8,128)(2,1)S(1)} custom-call(bf16[1040,384]{1,0:T(8,128)(2,1)S(1)} %collective-permute-done.5.refs_0_, bf16[1040,384]{1,0:T(8,128)(2,1)S(1)} %collective-permute-done.14.refs_1_, bf16[1040,384]{1,0:T(8,128)(2,1)S(1)} %collective-permute-done.6.refs_2_, bf16[1040,384]{1,0:T(8,128)(2,1)S(1)} %collective-permute-done.15.refs_3_), custom_call_target="tpu_custom_call" | custom-call | flops 1 | bytes 1 | tf_op jit(solution)/shard_map/spread_rows/pallas_call | solution.py:410
  95.8 2.6 %copy-done = bf16[4,512,1536]{2,1,0:T(8,128)(2,1)} copy-done((bf16[4,512,1536]{2,1,0:T(8,128)(2,1)}, bf16[4,512,1536]{2,1,0:T(8,128)(2,1)S(1)}, u32[]{:S(2)}) %copy-start) | copy-done | bytes 6291480
  98.5 3.3 %collective-permute-done.17.refs_2_ = bf16[4,256,128]{2,1,0:T(8,128)(2,1)S(1)} collective-permute-done((bf16[4,256,128]{2,1,0:T(8,128)(2,1)S(1)}, bf16[4,256,128]{2,1,0:T(8,128)(2,1)S(1)}, u32[]{:S(2)}, u32[]{:S(2)}) %collective-permute-start.17) | collective-permute-done | bytes 262176 | tf_op jit(solution)/shard_map/ppermute | solution.py:149
  101.8 1.6 %collective-permute-done.18.refs_3_ = bf16[4,256,128]{2,1,0:T(8,128)(2,1)S(1)} collective-permute-done((bf16[4,256,128]{2,1,0:T(8,128)(2,1)S(1)}, bf16[4,256,128]{2,1,0:T(8,128)(2,1)S(1)}, u32[]{:S(2)}, u32[]{:S(2)}) %collective-permute-start.18) | collective-permute-done | bytes 262176 | tf_op jit(solution)/shard_map/ppermute | solution.py:149
  103.4 2.3 %collective-permute-done.19.refs_1_ = bf16[1040,384]{1,0:T(8,128)(2,1)S(1)} collective-permute-done((bf16[1040,384]{1,0:T(8,128)(2,1)S(1)}, bf16[1040,384]{1,0:T(8,128)(2,1)S(1)}, u32[]{:S(2)}, u32[]{:S(2)}) %collective-permute-start.19) | collective-permute-done | bytes 798752 | tf_op jit(solution)/shard_map/ppermute | solution.py:149
  105.7 1.6 %project.5 = (f32[2,8,128]{2,1,0:T(8,128)S(1)}, bf16[2,256,128]{2,1,0:T(8,128)(2,1)S(1)}, bf16[2,256,128]{2,1,0:T(8,128)(2,1)S(1)}, bf16[2,256,128]{2,1,0:T(8,128)(2,1)S(1)}, bf16[2,256,128]{2,1,0:T(8,128)(2,1)S(1)}) custom-call(bf16[1040,384]{1,0:T(8,128)(2,1)S(1)} %collective-permute-done.13.refs_0_, ...), custom_call_target="tpu_custom_call" | custom-call | flops 1 | bytes 1 | tf_op jit(solution)/shard_map/project/pallas_call | solution.py:362
  111.0 1.9 %spread_rows.5.refs_6_ = bf16[2,512,1536]{2,1,0:T(8,128)(2,1)S(1)} custom-call(bf16[1040,384]{1,0:T(8,128)(2,1)S(1)} %collective-permute-done.13.refs_0_, bf16[1040,384]{1,0:T(8,128)(2,1)S(1)} %collective-permute-done.19.refs_1_), custom_call_target="tpu_custom_call" | custom-call | flops 1 | bytes 1 | tf_op jit(solution)/shard_map/spread_rows/pallas_call | solution.py:410
  112.8 1.7 %copy-done.2 = bf16[2,512,1536]{2,1,0:T(8,128)(2,1)} copy-done((bf16[2,512,1536]{2,1,0:T(8,128)(2,1)}, bf16[2,512,1536]{2,1,0:T(8,128)(2,1)S(1)}, u32[]{:S(2)}) %copy-start.2) | copy-done | bytes 3145752
  114.6 1.8 %collective-permute-done.21.refs_6_ = bf16[2,256,128]{2,1,0:T(8,128)(2,1)S(1)} collective-permute-done((bf16[2,256,128]{2,1,0:T(8,128)(2,1)S(1)}, bf16[2,256,128]{2,1,0:T(8,128)(2,1)S(1)}, u32[]{:S(2)}, u32[]{:S(2)}) %collective-permute-start.21) | collective-permute-done | bytes 131104 | tf_op jit(solution)/shard_map/ppermute | solution.py:149
  117.6 4.4 %all-to-all-start.1 = ((bf16[8,256,128]{2,1,0:T(8,128)(2,1)}), bf16[8,256,128]{2,1,0:T(8,128)(2,1)S(1)}, u32[]{:S(2)}, u32[]{:S(2)}) async-start(bf16[8,256,128]{2,1,0:T(8,128)(2,1)} %get-tuple-element.108), calls=%async_computation.1 | async-start | bytes 1048576 | tf_op jit(solution)/shard_map/all_to_all | solution.py:672
  128.3 1.8 %collective-permute-start.32 = (bf16[1536,128]{1,0:T(8,128)(2,1)S(1)}, bf16[1536,128]{1,0:T(8,128)(2,1)S(1)}, u32[]{:S(2)}, u32[]{:S(2)}) collective-permute-start(bf16[1536,128]{1,0:T(8,128)(2,1)S(1)} %get-tuple-element.120.refs_14_), channel_id=1, source_target_pairs={{0,3},{1,2},{2,1},{3,0},{4,7},{5,6},{6,5},{7,4},{8,11},{9,10},{10,... | collective-permute-start | bytes 1179656 | tf_op jit(solution)/shard_map/ppermute | solution.py:149
  133.0 3.8 %collective-permute-start.29 = (f32[8,128]{1,0:T(8,128)S(1)}, f32[8,128]{1,0:T(8,128)S(1)}, u32[]{:S(2)}, u32[]{:S(2)}) collective-permute-start(f32[8,128]{1,0:T(8,128)S(1)} %add.15.refs_0_), channel_id=1, source_target_pairs={{0,24},{4,28},{8,16},{12,20},{16,8},{20,12},{24,0},{28,4},{1,25},{... | collective-permute-start | bytes 12296 | tf_op jit(solution)/shard_map/ppermute | solution.py:149
  138.6 2.7 %collective-permute-done.28.refs_2_ = f32[8,128]{1,0:T(8,128)S(1)} collective-permute-done((f32[8,128]{1,0:T(8,128)S(1)}, f32[8,128]{1,0:T(8,128)S(1)}, u32[]{:S(2)}, u32[]{:S(2)}) %collective-permute-start.28) | collective-permute-done | bytes 4128 | tf_op jit(solution)/shard_map/ppermute | solution.py:149
  142.0 5.7 %collective-permute-done.31.refs_16_ = bf16[1536,128]{1,0:T(8,128)(2,1)S(1)} collective-permute-done((bf16[1536,128]{1,0:T(8,128)(2,1)S(1)}, bf16[1536,128]{1,0:T(8,128)(2,1)S(1)}, u32[]{:S(2)}, u32[]{:S(2)}) %collective-permute-start.31) | collective-permute-done | bytes 393248 | tf_op jit(solution)/shard_map/ppermute | solution.py:149
  149.3 9.7 %gradient.1 = (f32[256,4,384]{2,1,0:T(4,128)}, f32[1,64]{1,0:T(1,128)}, f32[1,64]{1,0:T(1,128)}) custom-call(f32[8,128]{1,0:T(8,128)} %copy-done.18, f32[8,128]{1,0:T(8,128)} %copy-done.21, f32[8,128]{1,0:T(8,128)} %copy-done.20, f32[8,128]{1,0:T(8,128)} %copy-done.19, bf16[2,512,1536]{2,1,0:T(8,128)(2,1)} %copy-done.1, bf16[4,512,1536]{2,1,0:T(8,128)(2,1)} %copy-done, ...), custom_call_target="tpu_custom_call" | custom-call | flops 1 | bytes 1 | tf_op jit(solution)/shard_map/gradient/pallas_call | solution.py:577
  (100 shorter events, 39.7 us)
Async XLA Ops:
  2.7 16.5 %collective-permute-start.1 = (bf16[144,2048]{1,0:T(8,128)(2,1)}, bf16[144,2048]{1,0:T(8,128)(2,1)S(1)}, u32[]{:S(2)}, u32[]{:S(2)}) collective-permute-start(bf16[144,2048]{1,0:T(8,128)(2,1)} %pack_tokens.1.own), channel_id=1, source_target_pairs={{0,2},{1,3},{2,0},{3,1},{4,6},{5,7},{6,4},{7,5},{8,10},{9,11},{10,... | collective-permute-start | bytes 1769480 | tf_op jit(solution)/shard_map/ppermute | solution.py:149
  5.6 15.3 %collective-permute-start = (bf16[144,2048]{1,0:T(8,128)(2,1)}, bf16[144,2048]{1,0:T(8,128)(2,1)S(1)}, u32[]{:S(2)}, u32[]{:S(2)}) collective-permute-start(bf16[144,2048]{1,0:T(8,128)(2,1)} %pack_tokens.1.own), channel_id=1, source_target_pairs={{0,1},{1,0},{2,3},{3,2},{4,5},{5,4},{6,7},{7,6},{8,9},{9,8},{10,11... | collective-permute-start | bytes 1769480 | tf_op jit(solution)/shard_map/ppermute | solution.py:149
  9.2 20.2 %all-to-all-start = ((bf16[8,256,128]{2,1,0:T(8,128)(2,1)}), bf16[8,256,128]{2,1,0:T(8,128)(2,1)S(1)}, u32[]{:S(2)}, u32[]{:S(2)}) async-start(bf16[8,256,128]{2,1,0:T(8,128)(2,1)} %bitcast.5), calls=%async_computation | async-start | bytes 1048576 | tf_op jit(solution)/shard_map/all_to_all | solution.py:630
  19.2 10.2 %collective-permute-start.2 = (bf16[80,2048]{1,0:T(8,128)(2,1)S(1)}, bf16[80,2048]{1,0:T(8,128)(2,1)S(1)}, u32[]{:S(2)}, u32[]{:S(2)}) collective-permute-start(bf16[80,2048]{1,0:T(8,128)(2,1)S(1)} %slice.8), channel_id=1, source_target_pairs={{0,1},{1,0},{2,3},{3,2},{4,5},{5,4},{6,7},{7,6},{8,9},{9,8},{10,11... | collective-permute-start | bytes 983048 | tf_op jit(solution)/shard_map/ppermute | solution.py:149
  21.0 8.4 %collective-permute-start.3 = (bf16[80,2048]{1,0:T(8,128)(2,1)S(1)}, bf16[80,2048]{1,0:T(8,128)(2,1)S(1)}, u32[]{:S(2)}, u32[]{:S(2)}) collective-permute-start(bf16[80,2048]{1,0:T(8,128)(2,1)S(1)} %slice.9), channel_id=1, source_target_pairs={{0,2},{1,3},{2,0},{3,1},{4,6},{5,7},{6,4},{7,5},{8,10},{9,11},{10,... | collective-permute-start | bytes 983048 | tf_op jit(solution)/shard_map/ppermute | solution.py:149
  43.0 4.4 %collective-permute-start.4 = (bf16[1040,384]{1,0:T(8,128)(2,1)S(1)}, bf16[1040,384]{1,0:T(8,128)(2,1)S(1)}, u32[]{:S(2)}, u32[]{:S(2)}) collective-permute-start(bf16[1040,384]{1,0:T(8,128)(2,1)S(1)} %hidden_rows.1.refs_0_), channel_id=1, source_target_pairs={{0,4},{4,0},{8,12},{12,8},{16,20},{20,16},{24,28},{28,24},{1,5},{5... | collective-permute-start | bytes 2396168 | tf_op jit(solution)/shard_map/ppermute | solution.py:149
  43.1 38.3 %collective-permute-start.6 = (bf16[1040,384]{1,0:T(8,128)(2,1)S(1)}, bf16[1040,384]{1,0:T(8,128)(2,1)S(1)}, u32[]{:S(2)}, u32[]{:S(2)}) collective-permute-start(bf16[1040,384]{1,0:T(8,128)(2,1)S(1)} %hidden_rows.1.refs_0_), channel_id=1, source_target_pairs={{0,16},{4,20},{8,24},{12,28},{16,0},{20,4},{24,8},{28,12},{1,17},{... | collective-permute-start | bytes 2396168 | tf_op jit(solution)/shard_map/ppermute | solution.py:149
  45.7 35.9 %collective-permute-start.5 = (bf16[1040,384]{1,0:T(8,128)(2,1)S(1)}, bf16[1040,384]{1,0:T(8,128)(2,1)S(1)}, u32[]{:S(2)}, u32[]{:S(2)}) collective-permute-start(bf16[1040,384]{1,0:T(8,128)(2,1)S(1)} %hidden_rows.1.refs_0_), channel_id=1, source_target_pairs={{0,8},{4,12},{8,0},{12,4},{16,24},{20,28},{24,16},{28,20},{1,9},{5... | collective-permute-start | bytes 2396168 | tf_op jit(solution)/shard_map/ppermute | solution.py:149
  49.1 6.2 %collective-permute-start.7 = (bf16[2,256,128]{2,1,0:T(8,128)(2,1)S(1)}, bf16[2,256,128]{2,1,0:T(8,128)(2,1)S(1)}, u32[]{:S(2)}, u32[]{:S(2)}) collective-permute-start(bf16[2,256,128]{2,1,0:T(8,128)(2,1)S(1)} %get-tuple-element.71), channel_id=1, source_target_pairs={{0,1},{1,0},{2,3},{3,2},{4,5},{5,4},{6,7},{7,6},{8,9},{9,8},{10,11... | collective-permute-start | bytes 393224 | tf_op jit(solution)/shard_map/ppermute | solution.py:149
  50.3 6.3 %collective-permute-start.8 = (bf16[2,256,128]{2,1,0:T(8,128)(2,1)S(1)}, bf16[2,256,128]{2,1,0:T(8,128)(2,1)S(1)}, u32[]{:S(2)}, u32[]{:S(2)}) collective-permute-start(bf16[2,256,128]{2,1,0:T(8,128)(2,1)S(1)} %get-tuple-element.72), channel_id=1, source_target_pairs={{0,2},{1,3},{2,0},{3,1},{4,6},{5,7},{6,4},{7,5},{8,10},{9,11},{10,... | collective-permute-start | bytes 393224 | tf_op jit(solution)/shard_map/ppermute | solution.py:149
  51.2 7.0 %collective-permute-start.9 = (bf16[2,256,128]{2,1,0:T(8,128)(2,1)S(1)}, bf16[2,256,128]{2,1,0:T(8,128)(2,1)S(1)}, u32[]{:S(2)}, u32[]{:S(2)}) collective-permute-start(bf16[2,256,128]{2,1,0:T(8,128)(2,1)S(1)} %get-tuple-element.73), channel_id=1, source_target_pairs={{0,3},{1,2},{2,1},{3,0},{4,7},{5,6},{6,5},{7,4},{8,11},{9,10},{10,... | collective-permute-start | bytes 393224 | tf_op jit(solution)/shard_map/ppermute | solution.py:149
  58.4 23.2 %collective-permute-start.12 = (bf16[512,128]{1,0:T(8,128)(2,1)S(1)}, bf16[512,128]{1,0:T(8,128)(2,1)S(1)}, u32[]{:S(2)}, u32[]{:S(2)}) collective-permute-start(bf16[512,128]{1,0:T(8,128)(2,1)S(1)} %get-tuple-element.80.refs_10_), channel_id=1, source_target_pairs={{0,3},{1,2},{2,1},{3,0},{4,7},{5,6},{6,5},{7,4},{8,11},{9,10},{10,... | collective-permute-start | bytes 393224 | tf_op jit(solution)/shard_map/ppermute | solution.py:149
  60.2 21.4 %collective-permute-start.11 = (bf16[512,128]{1,0:T(8,128)(2,1)S(1)}, bf16[512,128]{1,0:T(8,128)(2,1)S(1)}, u32[]{:S(2)}, u32[]{:S(2)}) collective-permute-start(bf16[512,128]{1,0:T(8,128)(2,1)S(1)} %get-tuple-element.80.refs_10_), channel_id=1, source_target_pairs={{0,2},{1,3},{2,0},{3,1},{4,6},{5,7},{6,4},{7,5},{8,10},{9,11},{10,... | collective-permute-start | bytes 393224 | tf_op jit(solution)/shard_map/ppermute | solution.py:149
  60.8 20.9 %collective-permute-start.10 = (bf16[512,128]{1,0:T(8,128)(2,1)S(1)}, bf16[512,128]{1,0:T(8,128)(2,1)S(1)}, u32[]{:S(2)}, u32[]{:S(2)}) collective-permute-start(bf16[512,128]{1,0:T(8,128)(2,1)S(1)} %get-tuple-element.80.refs_10_), channel_id=1, source_target_pairs={{0,1},{1,0},{2,3},{3,2},{4,5},{5,4},{6,7},{7,6},{8,9},{9,8},{10,11... | collective-permute-start | bytes 393224 | tf_op jit(solution)/shard_map/ppermute | solution.py:149
  81.8 3.4 %collective-permute-start.15 = (bf16[1040,384]{1,0:T(8,128)(2,1)S(1)}, bf16[1040,384]{1,0:T(8,128)(2,1)S(1)}, u32[]{:S(2)}, u32[]{:S(2)}) collective-permute-start(bf16[1040,384]{1,0:T(8,128)(2,1)S(1)} %collective-permute-done.6.refs_2_), channel_id=1, source_target_pairs={{0,4},{4,0},{8,12},{12,8},{16,20},{20,16},{24,28},{28,24},{1,5},{5... | collective-permute-start | bytes 2396168 | tf_op jit(solution)/shard_map/ppermute | solution.py:149
  82.3 21.2 %collective-permute-start.13 = (bf16[1040,384]{1,0:T(8,128)(2,1)S(1)}, bf16[1040,384]{1,0:T(8,128)(2,1)S(1)}, u32[]{:S(2)}, u32[]{:S(2)}) collective-permute-start(bf16[1040,384]{1,0:T(8,128)(2,1)S(1)} %collective-permute-done.6.refs_2_), channel_id=1, source_target_pairs={{0,8},{4,12},{8,0},{12,4},{16,24},{20,28},{24,16},{28,20},{1,9},{5... | collective-permute-start | bytes 2396168 | tf_op jit(solution)/shard_map/ppermute | solution.py:149
  88.5 10.0 %collective-permute-start.16 = (bf16[4,256,128]{2,1,0:T(8,128)(2,1)S(1)}, bf16[4,256,128]{2,1,0:T(8,128)(2,1)S(1)}, u32[]{:S(2)}, u32[]{:S(2)}) collective-permute-start(bf16[4,256,128]{2,1,0:T(8,128)(2,1)S(1)} %get-tuple-element.84), channel_id=1, source_target_pairs={{0,1},{1,0},{2,3},{3,2},{4,5},{5,4},{6,7},{7,6},{8,9},{9,8},{10,11... | collective-permute-start | bytes 786440 | tf_op jit(solution)/shard_map/ppermute | solution.py:149
  89.6 12.2 %collective-permute-start.17 = (bf16[4,256,128]{2,1,0:T(8,128)(2,1)S(1)}, bf16[4,256,128]{2,1,0:T(8,128)(2,1)S(1)}, u32[]{:S(2)}, u32[]{:S(2)}) collective-permute-start(bf16[4,256,128]{2,1,0:T(8,128)(2,1)S(1)} %get-tuple-element.85), channel_id=1, source_target_pairs={{0,2},{1,3},{2,0},{3,1},{4,6},{5,7},{6,4},{7,5},{8,10},{9,11},{10,... | collective-permute-start | bytes 786440 | tf_op jit(solution)/shard_map/ppermute | solution.py:149
  90.6 12.9 %collective-permute-start.18 = (bf16[4,256,128]{2,1,0:T(8,128)(2,1)S(1)}, bf16[4,256,128]{2,1,0:T(8,128)(2,1)S(1)}, u32[]{:S(2)}, u32[]{:S(2)}) collective-permute-start(bf16[4,256,128]{2,1,0:T(8,128)(2,1)S(1)} %get-tuple-element.86), channel_id=1, source_target_pairs={{0,3},{1,2},{2,1},{3,0},{4,7},{5,6},{6,5},{7,4},{8,11},{9,10},{10,... | collective-permute-start | bytes 786440 | tf_op jit(solution)/shard_map/ppermute | solution.py:149
  107.4 7.2 %collective-permute-start.20 = (bf16[2,256,128]{2,1,0:T(8,128)(2,1)S(1)}, bf16[2,256,128]{2,1,0:T(8,128)(2,1)S(1)}, u32[]{:S(2)}, u32[]{:S(2)}) collective-permute-start(bf16[2,256,128]{2,1,0:T(8,128)(2,1)S(1)} %get-tuple-element.97), channel_id=1, source_target_pairs={{0,1},{1,0},{2,3},{3,2},{4,5},{5,4},{6,7},{7,6},{8,9},{9,8},{10,11... | collective-permute-start | bytes 393224 | tf_op jit(solution)/shard_map/ppermute | solution.py:149
  108.3 8.1 %collective-permute-start.21 = (bf16[2,256,128]{2,1,0:T(8,128)(2,1)S(1)}, bf16[2,256,128]{2,1,0:T(8,128)(2,1)S(1)}, u32[]{:S(2)}, u32[]{:S(2)}) collective-permute-start(bf16[2,256,128]{2,1,0:T(8,128)(2,1)S(1)} %get-tuple-element.98), channel_id=1, source_target_pairs={{0,2},{1,3},{2,0},{3,1},{4,6},{5,7},{6,4},{7,5},{8,10},{9,11},{10,... | collective-permute-start | bytes 393224 | tf_op jit(solution)/shard_map/ppermute | solution.py:149
  109.8 6.6 %collective-permute-start.22 = (bf16[2,256,128]{2,1,0:T(8,128)(2,1)S(1)}, bf16[2,256,128]{2,1,0:T(8,128)(2,1)S(1)}, u32[]{:S(2)}, u32[]{:S(2)}) collective-permute-start(bf16[2,256,128]{2,1,0:T(8,128)(2,1)S(1)} %get-tuple-element.99), channel_id=1, source_target_pairs={{0,3},{1,2},{2,1},{3,0},{4,7},{5,6},{6,5},{7,4},{8,11},{9,10},{10,... | collective-permute-start | bytes 393224 | tf_op jit(solution)/shard_map/ppermute | solution.py:149
  117.6 41.4 %all-to-all-start.1 = ((bf16[8,256,128]{2,1,0:T(8,128)(2,1)}), bf16[8,256,128]{2,1,0:T(8,128)(2,1)S(1)}, u32[]{:S(2)}, u32[]{:S(2)}) async-start(bf16[8,256,128]{2,1,0:T(8,128)(2,1)} %get-tuple-element.108), calls=%async_computation.1 | async-start | bytes 1048576 | tf_op jit(solution)/shard_map/all_to_all | solution.py:672
  122.0 4.5 %collective-permute-start.25 = (f32[8,128]{1,0:T(8,128)S(1)}, f32[8,128]{1,0:T(8,128)S(1)}, u32[]{:S(2)}, u32[]{:S(2)}) collective-permute-start(f32[8,128]{1,0:T(8,128)S(1)} %get-tuple-element.109), channel_id=1, source_target_pairs={{0,3},{1,2},{2,1},{3,0},{4,7},{5,6},{6,5},{7,4},{8,11},{9,10},{10,... | collective-permute-start | bytes 12296 | tf_op jit(solution)/shard_map/ppermute | solution.py:149
  123.5 3.6 %collective-permute-start.24 = (f32[8,128]{1,0:T(8,128)S(1)}, f32[8,128]{1,0:T(8,128)S(1)}, u32[]{:S(2)}, u32[]{:S(2)}) collective-permute-start(f32[8,128]{1,0:T(8,128)S(1)} %get-tuple-element.109), channel_id=1, source_target_pairs={{0,2},{1,3},{2,0},{3,1},{4,6},{5,7},{6,4},{7,5},{8,10},{9,11},{10,... | collective-permute-start | bytes 12296 | tf_op jit(solution)/shard_map/ppermute | solution.py:149
  124.7 3.6 %collective-permute-start.23 = (f32[8,128]{1,0:T(8,128)S(1)}, f32[8,128]{1,0:T(8,128)S(1)}, u32[]{:S(2)}, u32[]{:S(2)}) collective-permute-start(f32[8,128]{1,0:T(8,128)S(1)} %get-tuple-element.109), channel_id=1, source_target_pairs={{0,1},{1,0},{2,3},{3,2},{4,5},{5,4},{6,7},{7,6},{8,9},{9,8},{10,11... | collective-permute-start | bytes 12296 | tf_op jit(solution)/shard_map/ppermute | solution.py:149
  128.3 13.7 %collective-permute-start.32 = (bf16[1536,128]{1,0:T(8,128)(2,1)S(1)}, bf16[1536,128]{1,0:T(8,128)(2,1)S(1)}, u32[]{:S(2)}, u32[]{:S(2)}) collective-permute-start(bf16[1536,128]{1,0:T(8,128)(2,1)S(1)} %get-tuple-element.120.refs_14_), channel_id=1, source_target_pairs={{0,3},{1,2},{2,1},{3,0},{4,7},{5,6},{6,5},{7,4},{8,11},{9,10},{10,... | collective-permute-start | bytes 1179656 | tf_op jit(solution)/shard_map/ppermute | solution.py:149
  130.1 17.7 %collective-permute-start.31 = (bf16[1536,128]{1,0:T(8,128)(2,1)S(1)}, bf16[1536,128]{1,0:T(8,128)(2,1)S(1)}, u32[]{:S(2)}, u32[]{:S(2)}) collective-permute-start(bf16[1536,128]{1,0:T(8,128)(2,1)S(1)} %get-tuple-element.120.refs_14_), channel_id=1, source_target_pairs={{0,2},{1,3},{2,0},{3,1},{4,6},{5,7},{6,4},{7,5},{8,10},{9,11},{10,... | collective-permute-start | bytes 1179656 | tf_op jit(solution)/shard_map/ppermute | solution.py:149
  130.6 17.2 %collective-permute-start.30 = (bf16[1536,128]{1,0:T(8,128)(2,1)S(1)}, bf16[1536,128]{1,0:T(8,128)(2,1)S(1)}, u32[]{:S(2)}, u32[]{:S(2)}) collective-permute-start(bf16[1536,128]{1,0:T(8,128)(2,1)S(1)} %get-tuple-element.120.refs_14_), channel_id=1, source_target_pairs={{0,1},{1,0},{2,3},{3,2},{4,5},{5,4},{6,7},{7,6},{8,9},{9,8},{10,11... | collective-permute-start | bytes 1179656 | tf_op jit(solution)/shard_map/ppermute | solution.py:149
  133.0 5.4 %collective-permute-start.29 = (f32[8,128]{1,0:T(8,128)S(1)}, f32[8,128]{1,0:T(8,128)S(1)}, u32[]{:S(2)}, u32[]{:S(2)}) collective-permute-start(f32[8,128]{1,0:T(8,128)S(1)} %add.15.refs_0_), channel_id=1, source_target_pairs={{0,24},{4,28},{8,16},{12,20},{16,8},{20,12},{24,0},{28,4},{1,25},{... | collective-permute-start | bytes 12296 | tf_op jit(solution)/shard_map/ppermute | solution.py:149
  136.8 4.5 %collective-permute-start.28 = (f32[8,128]{1,0:T(8,128)S(1)}, f32[8,128]{1,0:T(8,128)S(1)}, u32[]{:S(2)}, u32[]{:S(2)}) collective-permute-start(f32[8,128]{1,0:T(8,128)S(1)} %add.15.refs_0_), channel_id=1, source_target_pairs={{0,16},{4,20},{8,24},{12,28},{16,0},{20,4},{24,8},{28,12},{1,17},{... | collective-permute-start | bytes 12296 | tf_op jit(solution)/shard_map/ppermute | solution.py:149
  138.4 3.6 %collective-permute-start.27 = (f32[8,128]{1,0:T(8,128)S(1)}, f32[8,128]{1,0:T(8,128)S(1)}, u32[]{:S(2)}, u32[]{:S(2)}) collective-permute-start(f32[8,128]{1,0:T(8,128)S(1)} %add.15.refs_0_), channel_id=1, source_target_pairs={{0,8},{4,12},{8,0},{12,4},{16,24},{20,28},{24,16},{28,20},{1,9},{5... | collective-permute-start | bytes 12296 | tf_op jit(solution)/shard_map/ppermute | solution.py:149
  (25 other events, 332.9 us)

commit v3 on v2

--- a/solution.py
+++ b/solution.py
@@ -315,7 +315,7 @@
             pltpu.SemaphoreType.DMA((exp_dev,)),
         ],
         cost_estimate=cost(),
-        compiler_params=params(36),
+        compiler_params=params(56),
         name="hidden_rows",
     )(*tokens, w_gate, w_up)
 
@@ -562,7 +562,7 @@
         return (jnp.where(is_above, lower, middle), jnp.where(is_above, middle, upper))
 
     lower, upper = lax.fori_loop(
-        0, BISECT_STEPS, advance, (-bound, bound), unroll=8
+        0, BISECT_STEPS, advance, (-bound, bound), unroll=True
     )
     excess = jnp.maximum(loss - 0.5 * (lower + upper), 0.0)
     return excess / jnp.sum(excess, axis=0, keepdims=True)

time: 160 us -> 156 us (0.975)
  local copies, waits for them, and re-layouts: 15.7 us -> 12 us
  Pallas kernels: 34.1 us -> 35.9 us
  starting transfers between devices: 48.6 us -> 46.9 us
    unnamed x45 -> x49, local copies, waits for them, and re-layouts: 12.6 us -> 8.9 us
    pallas_call x1, Pallas kernels: 6.97 us -> 8.76 us  [hidden_rows(): pl.pallas_call(functools.partial(hidden_kernel, experts, capacity), in_sp...]
  transfers between devices with their start and end apart: 35 -> 35, of which waited for: 21 -> 20; matrix products, arithmetic and copies ran while one was open for 1% -> 1% of each run, Pallas kernels for 14% -> 14%
where the time goes in v3:
time: 156 us; the launch traced here: 155 us
  waiting for transfers between devices  59.8 us (38%)
  starting transfers between devices  46.9 us (30%)
  Pallas kernels  35.9 us (23%)
  local copies, waits for them, and re-layouts  12 us (8%)
    ppermute x33, waiting for transfers between devices, swap(): return lax.ppermute(block, axis, [(s, s ^ mask) for s in range(size)])  53 us
    ppermute x33, starting transfers between devices, swap(): return lax.ppermute(block, axis, [(s, s ^ mask) for s in range(size)])  38.1 us
    pallas_call x1, Pallas kernels, gradient(): pl.pallas_call(functools.partial(gradient_kernel, scale, feat_width, exp_...  9.67 us
    unnamed x49, local copies, waits for them, and re-layouts  8.9 us
    pallas_call x1, Pallas kernels, hidden_rows(): pl.pallas_call(functools.partial(hidden_kernel, experts, capacity), in_sp...  8.76 us
    pallas_call x3, Pallas kernels, spread_rows(): pl.pallas_call(functools.partial(spread_kernel, exp_dev, capacity, rows,...  7.42 us
    all_to_all x1, waiting for transfers between devices, feature_plan(): lax.all_to_all(turned.reshape(groups, feats, rows), 'dp', split_axis=0, c...  6.8 us
    pallas_call x3, Pallas kernels, project(): pl.pallas_call(functools.partial(project_kernel, exp_dev, capacity, rows,...  6.55 us
  transfers between devices with their start and end apart: 35, of which 20 were waited for; matrix products, arithmetic and copies ran while one was open for 1% of the time, Pallas kernels for 14%

profile of v3, /device:TPU:0, one launch (start us, length us, event | category | flops | bytes accessed | tf_op | source)
XLA Modules:
  0.0 155.5 jit_solution(12530310274312779093)
XLA Ops:
  0.6 2.0 %pack_tokens.1.own = bf16[144,2048]{1,0:T(8,128)(2,1)} custom-call(bf16[128,2048]{1,0:T(8,128)(2,1)} %tokens.1, s32[8,128]{1,0:T(8,128)} %bitcast.19, f32[8,128]{1,0:T(8,128)} %bitcast.20, s32[8,128]{1,0:T(8,128)} %bitcast.21, s32[1,128]{1,0:T(1,128)} %bitcast.22), custom_call_target="tpu_custom_call" | custom-call | flops 1 | bytes 1 | tf_op jit(solution)/shard_map/pack_tokens/pallas_call | solution.py:231
  2.7 3.0 %collective-permute-start.1 = (bf16[144,2048]{1,0:T(8,128)(2,1)}, bf16[144,2048]{1,0:T(8,128)(2,1)S(1)}, u32[]{:S(2)}, u32[]{:S(2)}) collective-permute-start(bf16[144,2048]{1,0:T(8,128)(2,1)} %pack_tokens.1.own), channel_id=1, source_target_pairs={{0,2},{1,3},{2,0},{3,1},{4,6},{5,7},{6,4},{7,5},{8,10},{9,11},{10,... | collective-permute-start | bytes 1769480 | tf_op jit(solution)/shard_map/ppermute | solution.py:149
  7.1 2.0 %copy.13 = bf16[2048,128]{1,0:T(8,128)(2,1)} copy(bf16[2048,128]{0,1:T(8,128)(2,1)} %bitcast.17) | data formatting | bytes 1048576 | tf_op jit(solution)/shard_map/optimization_barrier | solution.py:629
  9.2 4.9 %all-to-all-start = ((bf16[8,256,128]{2,1,0:T(8,128)(2,1)}), bf16[8,256,128]{2,1,0:T(8,128)(2,1)S(1)}, u32[]{:S(2)}, u32[]{:S(2)}) async-start(bf16[8,256,128]{2,1,0:T(8,128)(2,1)} %bitcast.5), calls=%async_computation | async-start | bytes 1048576 | tf_op jit(solution)/shard_map/all_to_all | solution.py:630
  14.0 5.1 %collective-permute-done.1.y_side = bf16[144,2048]{1,0:T(8,128)(2,1)S(1)} collective-permute-done((bf16[144,2048]{1,0:T(8,128)(2,1)}, bf16[144,2048]{1,0:T(8,128)(2,1)S(1)}, u32[]{:S(2)}, u32[]{:S(2)}) %collective-permute-start.1) | collective-permute-done | bytes 589856 | tf_op jit(solution)/shard_map/ppermute | solution.py:149
  19.2 1.8 %collective-permute-start.2 = (bf16[80,2048]{1,0:T(8,128)(2,1)S(1)}, bf16[80,2048]{1,0:T(8,128)(2,1)S(1)}, u32[]{:S(2)}, u32[]{:S(2)}) collective-permute-start(bf16[80,2048]{1,0:T(8,128)(2,1)S(1)} %slice.8), channel_id=1, source_target_pairs={{0,1},{1,0},{2,3},{3,2},{4,5},{5,4},{6,7},{7,6},{8,9},{9,8},{10,11... | collective-permute-start | bytes 983048 | tf_op jit(solution)/shard_map/ppermute | solution.py:149
  21.0 1.6 %collective-permute-start.3 = (bf16[80,2048]{1,0:T(8,128)(2,1)S(1)}, bf16[80,2048]{1,0:T(8,128)(2,1)}, u32[]{:S(2)}, u32[]{:S(2)}) collective-permute-start(bf16[80,2048]{1,0:T(8,128)(2,1)S(1)} %slice.9), channel_id=1, source_target_pairs={{0,2},{1,3},{2,0},{3,1},{4,6},{5,7},{6,4},{7,5},{8,10},{9,11},{10,... | collective-permute-start | bytes 983048 | tf_op jit(solution)/shard_map/ppermute | solution.py:149
  22.6 6.8 %all-to-all-done.refs_5_.refs_10_ = bf16[8,256,128]{2,1,0:T(8,128)(2,1)S(1)} async-done(((bf16[8,256,128]{2,1,0:T(8,128)(2,1)}), bf16[8,256,128]{2,1,0:T(8,128)(2,1)S(1)}, u32[]{:S(2)}, u32[]{:S(2)}) %all-to-all-start) | async-done | bytes 524320 | tf_op jit(solution)/shard_map/all_to_all | solution.py:630
  30.1 8.8 %hidden_rows.1.refs_0_ = bf16[1040,384]{1,0:T(8,128)(2,1)} custom-call(bf16[144,2048]{1,0:T(8,128)(2,1)} %pack_tokens.1.own, bf16[144,2048]{1,0:T(8,128)(2,1)} %copy-done.11, bf16[144,2048]{1,0:T(8,128)(2,1)} %copy-done.10, bf16[80,2048]{1,0:T(8,128)(2,1)} %copy-done.16, bf16[80,2048]{1,0:T(8,128)(2,1)} %collective-permute-done.3.lower, ...), custom_call_target="tpu_custom_call" | custom-call | flops 1 | bytes 1 | tf_op jit(solution)/shard_map/hidden_rows/pallas_call | solution.py:304
  39.0 2.0 %collective-permute-start.6 = (bf16[1040,384]{1,0:T(8,128)(2,1)}, bf16[1040,384]{1,0:T(8,128)(2,1)S(1)}, u32[]{:S(2)}, u32[]{:S(2)}) collective-permute-start(bf16[1040,384]{1,0:T(8,128)(2,1)} %hidden_rows.1.refs_0_), channel_id=1, source_target_pairs={{0,16},{4,20},{8,24},{12,28},{16,0},{20,4},{24,8},{28,12},{1,17},{... | collective-permute-start | bytes 2396168 | tf_op jit(solution)/shard_map/ppermute | solution.py:149
  43.9 1.6 %project.3 = (f32[2,8,128]{2,1,0:T(8,128)S(1)}, bf16[2,256,128]{2,1,0:T(8,128)(2,1)S(1)}, bf16[2,256,128]{2,1,0:T(8,128)(2,1)S(1)}, bf16[2,256,128]{2,1,0:T(8,128)(2,1)S(1)}, bf16[2,256,128]{2,1,0:T(8,128)(2,1)S(1)}) custom-call(bf16[1040,384]{1,0:T(8,128)(2,1)S(1)} %copy-done.3, bf16[1040,384]{1,0:T(8,128)(2,1)S(1)} %collective-permute-done.4.refs_1_, ...), custom_call_target="tpu_custom_call" | custom-call | flops 1 | bytes 1 | tf_op jit(solution)/shard_map/project/pallas_call | solution.py:362
  50.2 1.8 %spread_rows.3.refs_4_ = bf16[2,512,1536]{2,1,0:T(8,128)(2,1)S(1)} custom-call(bf16[1040,384]{1,0:T(8,128)(2,1)S(1)} %copy-done.4, bf16[1040,384]{1,0:T(8,128)(2,1)S(1)} %collective-permute-done.4.refs_1_), custom_call_target="tpu_custom_call" | custom-call | flops 1 | bytes 1 | tf_op jit(solution)/shard_map/spread_rows/pallas_call | solution.py:410
  54.8 1.8 %collective-permute-start.12 = (bf16[512,128]{1,0:T(8,128)(2,1)S(1)}, bf16[512,128]{1,0:T(8,128)(2,1)S(1)}, u32[]{:S(2)}, u32[]{:S(2)}) collective-permute-start(bf16[512,128]{1,0:T(8,128)(2,1)S(1)} %get-tuple-element.80.refs_10_), channel_id=1, source_target_pairs={{0,3},{1,2},{2,1},{3,0},{4,7},{5,6},{6,5},{7,4},{8,11},{9,10},{10,... | collective-permute-start | bytes 393224 | tf_op jit(solution)/shard_map/ppermute | solution.py:149
  58.4 19.1 %collective-permute-done.6.refs_2_ = bf16[1040,384]{1,0:T(8,128)(2,1)S(1)} collective-permute-done((bf16[1040,384]{1,0:T(8,128)(2,1)}, bf16[1040,384]{1,0:T(8,128)(2,1)S(1)}, u32[]{:S(2)}, u32[]{:S(2)}) %collective-permute-start.6) | collective-permute-done | bytes 798752 | tf_op jit(solution)/shard_map/ppermute | solution.py:149
  81.3 3.3 %project.4 = (f32[4,8,128]{2,1,0:T(8,128)S(1)}, bf16[4,256,128]{2,1,0:T(8,128)(2,1)S(1)}, bf16[4,256,128]{2,1,0:T(8,128)(2,1)S(1)}, bf16[4,256,128]{2,1,0:T(8,128)(2,1)S(1)}, bf16[4,256,128]{2,1,0:T(8,128)(2,1)S(1)}) custom-call(bf16[1040,384]{1,0:T(8,128)(2,1)S(1)} %collective-permute-done.5.refs_0_, bf16[1040,384]{1,0:T(8,128)(2,1)S(1)} %collective-permute-done.14.refs_1_, ...), custom_call_target="tpu_custom_call" | custom-call | flops 1 | bytes 1 | tf_op jit(solution)/shard_map/project/pallas_call | solution.py:362
  86.3 1.8 %collective-permute-start.18 = (bf16[4,256,128]{2,1,0:T(8,128)(2,1)S(1)}, bf16[4,256,128]{2,1,0:T(8,128)(2,1)S(1)}, u32[]{:S(2)}, u32[]{:S(2)}) collective-permute-start(bf16[4,256,128]{2,1,0:T(8,128)(2,1)S(1)} %get-tuple-element.86), channel_id=1, source_target_pairs={{0,3},{1,2},{2,1},{3,0},{4,7},{5,6},{6,5},{7,4},{8,11},{9,10},{10,... | collective-permute-start | bytes 786440 | tf_op jit(solution)/shard_map/ppermute | solution.py:149
  88.1 3.7 %spread_rows.4.refs_5_ = bf16[4,512,1536]{2,1,0:T(8,128)(2,1)S(1)} custom-call(bf16[1040,384]{1,0:T(8,128)(2,1)S(1)} %collective-permute-done.5.refs_0_, bf16[1040,384]{1,0:T(8,128)(2,1)S(1)} %collective-permute-done.14.refs_1_, bf16[1040,384]{1,0:T(8,128)(2,1)S(1)} %collective-permute-done.6.refs_2_, bf16[1040,384]{1,0:T(8,128)(2,1)S(1)} %collective-permute-done.15.refs_3_), custom_call_target="tpu_custom_call" | custom-call | flops 1 | bytes 1 | tf_op jit(solution)/shard_map/spread_rows/pallas_call | solution.py:410
  91.9 2.6 %copy-done = bf16[4,512,1536]{2,1,0:T(8,128)(2,1)} copy-done((bf16[4,512,1536]{2,1,0:T(8,128)(2,1)}, bf16[4,512,1536]{2,1,0:T(8,128)(2,1)S(1)}, u32[]{:S(2)}) %copy-start) | copy-done | bytes 6291480
  94.5 4.4 %collective-permute-done.18.refs_3_ = bf16[4,256,128]{2,1,0:T(8,128)(2,1)S(1)} collective-permute-done((bf16[4,256,128]{2,1,0:T(8,128)(2,1)S(1)}, bf16[4,256,128]{2,1,0:T(8,128)(2,1)S(1)}, u32[]{:S(2)}, u32[]{:S(2)}) %collective-permute-start.18) | collective-permute-done | bytes 262176 | tf_op jit(solution)/shard_map/ppermute | solution.py:149
  98.9 2.3 %collective-permute-done.19.refs_1_ = bf16[1040,384]{1,0:T(8,128)(2,1)S(1)} collective-permute-done((bf16[1040,384]{1,0:T(8,128)(2,1)S(1)}, bf16[1040,384]{1,0:T(8,128)(2,1)S(1)}, u32[]{:S(2)}, u32[]{:S(2)}) %collective-permute-start.19) | collective-permute-done | bytes 798752 | tf_op jit(solution)/shard_map/ppermute | solution.py:149
  101.2 1.6 %project.5 = (f32[2,8,128]{2,1,0:T(8,128)S(1)}, bf16[2,256,128]{2,1,0:T(8,128)(2,1)S(1)}, bf16[2,256,128]{2,1,0:T(8,128)(2,1)S(1)}, bf16[2,256,128]{2,1,0:T(8,128)(2,1)S(1)}, bf16[2,256,128]{2,1,0:T(8,128)(2,1)S(1)}) custom-call(bf16[1040,384]{1,0:T(8,128)(2,1)S(1)} %collective-permute-done.13.refs_0_, ...), custom_call_target="tpu_custom_call" | custom-call | flops 1 | bytes 1 | tf_op jit(solution)/shard_map/project/pallas_call | solution.py:362
  106.5 1.9 %spread_rows.5.refs_6_ = bf16[2,512,1536]{2,1,0:T(8,128)(2,1)S(1)} custom-call(bf16[1040,384]{1,0:T(8,128)(2,1)S(1)} %collective-permute-done.13.refs_0_, bf16[1040,384]{1,0:T(8,128)(2,1)S(1)} %collective-permute-done.19.refs_1_), custom_call_target="tpu_custom_call" | custom-call | flops 1 | bytes 1 | tf_op jit(solution)/shard_map/spread_rows/pallas_call | solution.py:410
  108.3 1.7 %copy-done.2 = bf16[2,512,1536]{2,1,0:T(8,128)(2,1)} copy-done((bf16[2,512,1536]{2,1,0:T(8,128)(2,1)}, bf16[2,512,1536]{2,1,0:T(8,128)(2,1)S(1)}, u32[]{:S(2)}) %copy-start.2) | copy-done | bytes 3145752
  110.1 2.4 %collective-permute-done.21.refs_6_ = bf16[2,256,128]{2,1,0:T(8,128)(2,1)S(1)} collective-permute-done((bf16[2,256,128]{2,1,0:T(8,128)(2,1)S(1)}, bf16[2,256,128]{2,1,0:T(8,128)(2,1)S(1)}, u32[]{:S(2)}, u32[]{:S(2)}) %collective-permute-start.21) | collective-permute-done | bytes 131104 | tf_op jit(solution)/shard_map/ppermute | solution.py:149
  113.7 3.9 %all-to-all-start.1 = ((bf16[8,256,128]{2,1,0:T(8,128)(2,1)}), bf16[8,256,128]{2,1,0:T(8,128)(2,1)S(1)}, u32[]{:S(2)}, u32[]{:S(2)}) async-start(bf16[8,256,128]{2,1,0:T(8,128)(2,1)} %get-tuple-element.108), calls=%async_computation.1 | async-start | bytes 1048576 | tf_op jit(solution)/shard_map/all_to_all | solution.py:672
  117.5 1.7 %collective-permute-start.25 = (f32[8,128]{1,0:T(8,128)S(1)}, f32[8,128]{1,0:T(8,128)S(1)}, u32[]{:S(2)}, u32[]{:S(2)}) collective-permute-start(f32[8,128]{1,0:T(8,128)S(1)} %get-tuple-element.109), channel_id=1, source_target_pairs={{0,3},{1,2},{2,1},{3,0},{4,7},{5,6},{6,5},{7,4},{8,11},{9,10},{10,... | collective-permute-start | bytes 12296 | tf_op jit(solution)/shard_map/ppermute | solution.py:149
  123.8 1.8 %collective-permute-start.32 = (bf16[1536,128]{1,0:T(8,128)(2,1)S(1)}, bf16[1536,128]{1,0:T(8,128)(2,1)S(1)}, u32[]{:S(2)}, u32[]{:S(2)}) collective-permute-start(bf16[1536,128]{1,0:T(8,128)(2,1)S(1)} %get-tuple-element.120.refs_14_), channel_id=1, source_target_pairs={{0,3},{1,2},{2,1},{3,0},{4,7},{5,6},{6,5},{7,4},{8,11},{9,10},{10,... | collective-permute-start | bytes 1179656 | tf_op jit(solution)/shard_map/ppermute | solution.py:149
  128.5 3.8 %collective-permute-start.29 = (f32[8,128]{1,0:T(8,128)S(1)}, f32[8,128]{1,0:T(8,128)S(1)}, u32[]{:S(2)}, u32[]{:S(2)}) collective-permute-start(f32[8,128]{1,0:T(8,128)S(1)} %add.15.refs_0_), channel_id=1, source_target_pairs={{0,24},{4,28},{8,16},{12,20},{16,8},{20,12},{24,0},{28,4},{1,25},{... | collective-permute-start | bytes 12296 | tf_op jit(solution)/shard_map/ppermute | solution.py:149
  132.3 1.6 %collective-permute-done.29.refs_3_ = f32[8,128]{1,0:T(8,128)S(1)} collective-permute-done((f32[8,128]{1,0:T(8,128)S(1)}, f32[8,128]{1,0:T(8,128)S(1)}, u32[]{:S(2)}, u32[]{:S(2)}) %collective-permute-start.29) | collective-permute-done | bytes 4128 | tf_op jit(solution)/shard_map/ppermute | solution.py:149
  134.1 2.7 %collective-permute-done.28.refs_2_ = f32[8,128]{1,0:T(8,128)S(1)} collective-permute-done((f32[8,128]{1,0:T(8,128)S(1)}, f32[8,128]{1,0:T(8,128)S(1)}, u32[]{:S(2)}, u32[]{:S(2)}) %collective-permute-start.28) | collective-permute-done | bytes 4128 | tf_op jit(solution)/shard_map/ppermute | solution.py:149
  137.5 5.7 %collective-permute-done.31.refs_16_ = bf16[1536,128]{1,0:T(8,128)(2,1)S(1)} collective-permute-done((bf16[1536,128]{1,0:T(8,128)(2,1)S(1)}, bf16[1536,128]{1,0:T(8,128)(2,1)S(1)}, u32[]{:S(2)}, u32[]{:S(2)}) %collective-permute-start.31) | collective-permute-done | bytes 393248 | tf_op jit(solution)/shard_map/ppermute | solution.py:149
  144.8 9.7 %gradient.1 = (f32[256,4,384]{2,1,0:T(4,128)}, f32[1,64]{1,0:T(1,128)}, f32[1,64]{1,0:T(1,128)}) custom-call(f32[8,128]{1,0:T(8,128)} %copy-done.20, f32[8,128]{1,0:T(8,128)} %copy-done.23, f32[8,128]{1,0:T(8,128)} %copy-done.22, f32[8,128]{1,0:T(8,128)} %copy-done.21, bf16[2,512,1536]{2,1,0:T(8,128)(2,1)} %copy-done.1, bf16[4,512,1536]{2,1,0:T(8,128)(2,1)} %copy-done, ...), custom_call_target="tpu_custom_call" | custom-call | flops 1 | bytes 1 | tf_op jit(solution)/shard_map/gradient/pallas_call | solution.py:577
  (104 shorter events, 35.5 us)
Async XLA Ops:
  2.7 16.5 %collective-permute-start.1 = (bf16[144,2048]{1,0:T(8,128)(2,1)}, bf16[144,2048]{1,0:T(8,128)(2,1)S(1)}, u32[]{:S(2)}, u32[]{:S(2)}) collective-permute-start(bf16[144,2048]{1,0:T(8,128)(2,1)} %pack_tokens.1.own), channel_id=1, source_target_pairs={{0,2},{1,3},{2,0},{3,1},{4,6},{5,7},{6,4},{7,5},{8,10},{9,11},{10,... | collective-permute-start | bytes 1769480 | tf_op jit(solution)/shard_map/ppermute | solution.py:149
  5.6 15.3 %collective-permute-start = (bf16[144,2048]{1,0:T(8,128)(2,1)}, bf16[144,2048]{1,0:T(8,128)(2,1)S(1)}, u32[]{:S(2)}, u32[]{:S(2)}) collective-permute-start(bf16[144,2048]{1,0:T(8,128)(2,1)} %pack_tokens.1.own), channel_id=1, source_target_pairs={{0,1},{1,0},{2,3},{3,2},{4,5},{5,4},{6,7},{7,6},{8,9},{9,8},{10,11... | collective-permute-start | bytes 1769480 | tf_op jit(solution)/shard_map/ppermute | solution.py:149
  9.2 20.2 %all-to-all-start = ((bf16[8,256,128]{2,1,0:T(8,128)(2,1)}), bf16[8,256,128]{2,1,0:T(8,128)(2,1)S(1)}, u32[]{:S(2)}, u32[]{:S(2)}) async-start(bf16[8,256,128]{2,1,0:T(8,128)(2,1)} %bitcast.5), calls=%async_computation | async-start | bytes 1048576 | tf_op jit(solution)/shard_map/all_to_all | solution.py:630
  19.2 10.2 %collective-permute-start.2 = (bf16[80,2048]{1,0:T(8,128)(2,1)S(1)}, bf16[80,2048]{1,0:T(8,128)(2,1)S(1)}, u32[]{:S(2)}, u32[]{:S(2)}) collective-permute-start(bf16[80,2048]{1,0:T(8,128)(2,1)S(1)} %slice.8), channel_id=1, source_target_pairs={{0,1},{1,0},{2,3},{3,2},{4,5},{5,4},{6,7},{7,6},{8,9},{9,8},{10,11... | collective-permute-start | bytes 983048 | tf_op jit(solution)/shard_map/ppermute | solution.py:149
  21.0 8.5 %collective-permute-start.3 = (bf16[80,2048]{1,0:T(8,128)(2,1)S(1)}, bf16[80,2048]{1,0:T(8,128)(2,1)}, u32[]{:S(2)}, u32[]{:S(2)}) collective-permute-start(bf16[80,2048]{1,0:T(8,128)(2,1)S(1)} %slice.9), channel_id=1, source_target_pairs={{0,2},{1,3},{2,0},{3,1},{4,6},{5,7},{6,4},{7,5},{8,10},{9,11},{10,... | collective-permute-start | bytes 983048 | tf_op jit(solution)/shard_map/ppermute | solution.py:149
  38.9 3.8 %collective-permute-start.4 = (bf16[1040,384]{1,0:T(8,128)(2,1)}, bf16[1040,384]{1,0:T(8,128)(2,1)S(1)}, u32[]{:S(2)}, u32[]{:S(2)}) collective-permute-start(bf16[1040,384]{1,0:T(8,128)(2,1)} %hidden_rows.1.refs_0_), channel_id=1, source_target_pairs={{0,4},{4,0},{8,12},{12,8},{16,20},{20,16},{24,28},{28,24},{1,5},{5... | collective-permute-start | bytes 2396168 | tf_op jit(solution)/shard_map/ppermute | solution.py:149
  39.0 38.6 %collective-permute-start.6 = (bf16[1040,384]{1,0:T(8,128)(2,1)}, bf16[1040,384]{1,0:T(8,128)(2,1)S(1)}, u32[]{:S(2)}, u32[]{:S(2)}) collective-permute-start(bf16[1040,384]{1,0:T(8,128)(2,1)} %hidden_rows.1.refs_0_), channel_id=1, source_target_pairs={{0,16},{4,20},{8,24},{12,28},{16,0},{20,4},{24,8},{28,12},{1,17},{... | collective-permute-start | bytes 2396168 | tf_op jit(solution)/shard_map/ppermute | solution.py:149
  41.0 36.7 %collective-permute-start.5 = (bf16[1040,384]{1,0:T(8,128)(2,1)}, bf16[1040,384]{1,0:T(8,128)(2,1)S(1)}, u32[]{:S(2)}, u32[]{:S(2)}) collective-permute-start(bf16[1040,384]{1,0:T(8,128)(2,1)} %hidden_rows.1.refs_0_), channel_id=1, source_target_pairs={{0,8},{4,12},{8,0},{12,4},{16,24},{20,28},{24,16},{28,20},{1,9},{5... | collective-permute-start | bytes 2396168 | tf_op jit(solution)/shard_map/ppermute | solution.py:149
  45.5 6.6 %collective-permute-start.7 = (bf16[2,256,128]{2,1,0:T(8,128)(2,1)S(1)}, bf16[2,256,128]{2,1,0:T(8,128)(2,1)S(1)}, u32[]{:S(2)}, u32[]{:S(2)}) collective-permute-start(bf16[2,256,128]{2,1,0:T(8,128)(2,1)S(1)} %get-tuple-element.71), channel_id=1, source_target_pairs={{0,1},{1,0},{2,3},{3,2},{4,5},{5,4},{6,7},{7,6},{8,9},{9,8},{10,11... | collective-permute-start | bytes 393224 | tf_op jit(solution)/shard_map/ppermute | solution.py:149
  46.7 6.6 %collective-permute-start.8 = (bf16[2,256,128]{2,1,0:T(8,128)(2,1)S(1)}, bf16[2,256,128]{2,1,0:T(8,128)(2,1)S(1)}, u32[]{:S(2)}, u32[]{:S(2)}) collective-permute-start(bf16[2,256,128]{2,1,0:T(8,128)(2,1)S(1)} %get-tuple-element.72), channel_id=1, source_target_pairs={{0,2},{1,3},{2,0},{3,1},{4,6},{5,7},{6,4},{7,5},{8,10},{9,11},{10,... | collective-permute-start | bytes 393224 | tf_op jit(solution)/shard_map/ppermute | solution.py:149
  47.9 6.8 %collective-permute-start.9 = (bf16[2,256,128]{2,1,0:T(8,128)(2,1)S(1)}, bf16[2,256,128]{2,1,0:T(8,128)(2,1)S(1)}, u32[]{:S(2)}, u32[]{:S(2)}) collective-permute-start(bf16[2,256,128]{2,1,0:T(8,128)(2,1)S(1)} %get-tuple-element.73), channel_id=1, source_target_pairs={{0,3},{1,2},{2,1},{3,0},{4,7},{5,6},{6,5},{7,4},{8,11},{9,10},{10,... | collective-permute-start | bytes 393224 | tf_op jit(solution)/shard_map/ppermute | solution.py:149
  54.8 22.9 %collective-permute-start.12 = (bf16[512,128]{1,0:T(8,128)(2,1)S(1)}, bf16[512,128]{1,0:T(8,128)(2,1)S(1)}, u32[]{:S(2)}, u32[]{:S(2)}) collective-permute-start(bf16[512,128]{1,0:T(8,128)(2,1)S(1)} %get-tuple-element.80.refs_10_), channel_id=1, source_target_pairs={{0,3},{1,2},{2,1},{3,0},{4,7},{5,6},{6,5},{7,4},{8,11},{9,10},{10,... | collective-permute-start | bytes 393224 | tf_op jit(solution)/shard_map/ppermute | solution.py:149
  56.7 21.1 %collective-permute-start.11 = (bf16[512,128]{1,0:T(8,128)(2,1)S(1)}, bf16[512,128]{1,0:T(8,128)(2,1)S(1)}, u32[]{:S(2)}, u32[]{:S(2)}) collective-permute-start(bf16[512,128]{1,0:T(8,128)(2,1)S(1)} %get-tuple-element.80.refs_10_), channel_id=1, source_target_pairs={{0,2},{1,3},{2,0},{3,1},{4,6},{5,7},{6,4},{7,5},{8,10},{9,11},{10,... | collective-permute-start | bytes 393224 | tf_op jit(solution)/shard_map/ppermute | solution.py:149
  57.2 20.6 %collective-permute-start.10 = (bf16[512,128]{1,0:T(8,128)(2,1)S(1)}, bf16[512,128]{1,0:T(8,128)(2,1)S(1)}, u32[]{:S(2)}, u32[]{:S(2)}) collective-permute-start(bf16[512,128]{1,0:T(8,128)(2,1)S(1)} %get-tuple-element.80.refs_10_), channel_id=1, source_target_pairs={{0,1},{1,0},{2,3},{3,2},{4,5},{5,4},{6,7},{7,6},{8,9},{9,8},{10,11... | collective-permute-start | bytes 393224 | tf_op jit(solution)/shard_map/ppermute | solution.py:149
  77.8 3.4 %collective-permute-start.15 = (bf16[1040,384]{1,0:T(8,128)(2,1)S(1)}, bf16[1040,384]{1,0:T(8,128)(2,1)S(1)}, u32[]{:S(2)}, u32[]{:S(2)}) collective-permute-start(bf16[1040,384]{1,0:T(8,128)(2,1)S(1)} %collective-permute-done.6.refs_2_), channel_id=1, source_target_pairs={{0,4},{4,0},{8,12},{12,8},{16,20},{20,16},{24,28},{28,24},{1,5},{5... | collective-permute-start | bytes 2396168 | tf_op jit(solution)/shard_map/ppermute | solution.py:149
  78.3 20.6 %collective-permute-start.13 = (bf16[1040,384]{1,0:T(8,128)(2,1)S(1)}, bf16[1040,384]{1,0:T(8,128)(2,1)S(1)}, u32[]{:S(2)}, u32[]{:S(2)}) collective-permute-start(bf16[1040,384]{1,0:T(8,128)(2,1)S(1)} %collective-permute-done.6.refs_2_), channel_id=1, source_target_pairs={{0,8},{4,12},{8,0},{12,4},{16,24},{20,28},{24,16},{28,20},{1,9},{5... | collective-permute-start | bytes 2396168 | tf_op jit(solution)/shard_map/ppermute | solution.py:149
  84.6 10.0 %collective-permute-start.16 = (bf16[4,256,128]{2,1,0:T(8,128)(2,1)S(1)}, bf16[4,256,128]{2,1,0:T(8,128)(2,1)S(1)}, u32[]{:S(2)}, u32[]{:S(2)}) collective-permute-start(bf16[4,256,128]{2,1,0:T(8,128)(2,1)S(1)} %get-tuple-element.84), channel_id=1, source_target_pairs={{0,1},{1,0},{2,3},{3,2},{4,5},{5,4},{6,7},{7,6},{8,9},{9,8},{10,11... | collective-permute-start | bytes 786440 | tf_op jit(solution)/shard_map/ppermute | solution.py:149
  85.2 9.4 %collective-permute-start.17 = (bf16[4,256,128]{2,1,0:T(8,128)(2,1)S(1)}, bf16[4,256,128]{2,1,0:T(8,128)(2,1)S(1)}, u32[]{:S(2)}, u32[]{:S(2)}) collective-permute-start(bf16[4,256,128]{2,1,0:T(8,128)(2,1)S(1)} %get-tuple-element.85), channel_id=1, source_target_pairs={{0,2},{1,3},{2,0},{3,1},{4,6},{5,7},{6,4},{7,5},{8,10},{9,11},{10,... | collective-permute-start | bytes 786440 | tf_op jit(solution)/shard_map/ppermute | solution.py:149
  86.3 12.6 %collective-permute-start.18 = (bf16[4,256,128]{2,1,0:T(8,128)(2,1)S(1)}, bf16[4,256,128]{2,1,0:T(8,128)(2,1)S(1)}, u32[]{:S(2)}, u32[]{:S(2)}) collective-permute-start(bf16[4,256,128]{2,1,0:T(8,128)(2,1)S(1)} %get-tuple-element.86), channel_id=1, source_target_pairs={{0,3},{1,2},{2,1},{3,0},{4,7},{5,6},{6,5},{7,4},{8,11},{9,10},{10,... | collective-permute-start | bytes 786440 | tf_op jit(solution)/shard_map/ppermute | solution.py:149
  102.9 7.2 %collective-permute-start.20 = (bf16[2,256,128]{2,1,0:T(8,128)(2,1)S(1)}, bf16[2,256,128]{2,1,0:T(8,128)(2,1)S(1)}, u32[]{:S(2)}, u32[]{:S(2)}) collective-permute-start(bf16[2,256,128]{2,1,0:T(8,128)(2,1)S(1)} %get-tuple-element.97), channel_id=1, source_target_pairs={{0,1},{1,0},{2,3},{3,2},{4,5},{5,4},{6,7},{7,6},{8,9},{9,8},{10,11... | collective-permute-start | bytes 393224 | tf_op jit(solution)/shard_map/ppermute | solution.py:149
  104.4 8.1 %collective-permute-start.21 = (bf16[2,256,128]{2,1,0:T(8,128)(2,1)S(1)}, bf16[2,256,128]{2,1,0:T(8,128)(2,1)S(1)}, u32[]{:S(2)}, u32[]{:S(2)}) collective-permute-start(bf16[2,256,128]{2,1,0:T(8,128)(2,1)S(1)} %get-tuple-element.98), channel_id=1, source_target_pairs={{0,2},{1,3},{2,0},{3,1},{4,6},{5,7},{6,4},{7,5},{8,10},{9,11},{10,... | collective-permute-start | bytes 393224 | tf_op jit(solution)/shard_map/ppermute | solution.py:149
  105.3 7.2 %collective-permute-start.22 = (bf16[2,256,128]{2,1,0:T(8,128)(2,1)S(1)}, bf16[2,256,128]{2,1,0:T(8,128)(2,1)S(1)}, u32[]{:S(2)}, u32[]{:S(2)}) collective-permute-start(bf16[2,256,128]{2,1,0:T(8,128)(2,1)S(1)} %get-tuple-element.99), channel_id=1, source_target_pairs={{0,3},{1,2},{2,1},{3,0},{4,7},{5,6},{6,5},{7,4},{8,11},{9,10},{10,... | collective-permute-start | bytes 393224 | tf_op jit(solution)/shard_map/ppermute | solution.py:149
  113.7 40.8 %all-to-all-start.1 = ((bf16[8,256,128]{2,1,0:T(8,128)(2,1)}), bf16[8,256,128]{2,1,0:T(8,128)(2,1)S(1)}, u32[]{:S(2)}, u32[]{:S(2)}) async-start(bf16[8,256,128]{2,1,0:T(8,128)(2,1)} %get-tuple-element.108), calls=%async_computation.1 | async-start | bytes 1048576 | tf_op jit(solution)/shard_map/all_to_all | solution.py:672
  117.5 4.5 %collective-permute-start.25 = (f32[8,128]{1,0:T(8,128)S(1)}, f32[8,128]{1,0:T(8,128)S(1)}, u32[]{:S(2)}, u32[]{:S(2)}) collective-permute-start(f32[8,128]{1,0:T(8,128)S(1)} %get-tuple-element.109), channel_id=1, source_target_pairs={{0,3},{1,2},{2,1},{3,0},{4,7},{5,6},{6,5},{7,4},{8,11},{9,10},{10,... | collective-permute-start | bytes 12296 | tf_op jit(solution)/shard_map/ppermute | solution.py:149
  119.3 3.6 %collective-permute-start.24 = (f32[8,128]{1,0:T(8,128)S(1)}, f32[8,128]{1,0:T(8,128)S(1)}, u32[]{:S(2)}, u32[]{:S(2)}) collective-permute-start(f32[8,128]{1,0:T(8,128)S(1)} %get-tuple-element.109), channel_id=1, source_target_pairs={{0,2},{1,3},{2,0},{3,1},{4,6},{5,7},{6,4},{7,5},{8,10},{9,11},{10,... | collective-permute-start | bytes 12296 | tf_op jit(solution)/shard_map/ppermute | solution.py:149
  120.2 3.6 %collective-permute-start.23 = (f32[8,128]{1,0:T(8,128)S(1)}, f32[8,128]{1,0:T(8,128)S(1)}, u32[]{:S(2)}, u32[]{:S(2)}) collective-permute-start(f32[8,128]{1,0:T(8,128)S(1)} %get-tuple-element.109), channel_id=1, source_target_pairs={{0,1},{1,0},{2,3},{3,2},{4,5},{5,4},{6,7},{7,6},{8,9},{9,8},{10,11... | collective-permute-start | bytes 12296 | tf_op jit(solution)/shard_map/ppermute | solution.py:149
  123.8 13.7 %collective-permute-start.32 = (bf16[1536,128]{1,0:T(8,128)(2,1)S(1)}, bf16[1536,128]{1,0:T(8,128)(2,1)S(1)}, u32[]{:S(2)}, u32[]{:S(2)}) collective-permute-start(bf16[1536,128]{1,0:T(8,128)(2,1)S(1)} %get-tuple-element.120.refs_14_), channel_id=1, source_target_pairs={{0,3},{1,2},{2,1},{3,0},{4,7},{5,6},{6,5},{7,4},{8,11},{9,10},{10,... | collective-permute-start | bytes 1179656 | tf_op jit(solution)/shard_map/ppermute | solution.py:149
  125.6 17.7 %collective-permute-start.31 = (bf16[1536,128]{1,0:T(8,128)(2,1)S(1)}, bf16[1536,128]{1,0:T(8,128)(2,1)S(1)}, u32[]{:S(2)}, u32[]{:S(2)}) collective-permute-start(bf16[1536,128]{1,0:T(8,128)(2,1)S(1)} %get-tuple-element.120.refs_14_), channel_id=1, source_target_pairs={{0,2},{1,3},{2,0},{3,1},{4,6},{5,7},{6,4},{7,5},{8,10},{9,11},{10,... | collective-permute-start | bytes 1179656 | tf_op jit(solution)/shard_map/ppermute | solution.py:149
  126.1 17.2 %collective-permute-start.30 = (bf16[1536,128]{1,0:T(8,128)(2,1)S(1)}, bf16[1536,128]{1,0:T(8,128)(2,1)S(1)}, u32[]{:S(2)}, u32[]{:S(2)}) collective-permute-start(bf16[1536,128]{1,0:T(8,128)(2,1)S(1)} %get-tuple-element.120.refs_14_), channel_id=1, source_target_pairs={{0,1},{1,0},{2,3},{3,2},{4,5},{5,4},{6,7},{7,6},{8,9},{9,8},{10,11... | collective-permute-start | bytes 1179656 | tf_op jit(solution)/shard_map/ppermute | solution.py:149
  128.5 5.4 %collective-permute-start.29 = (f32[8,128]{1,0:T(8,128)S(1)}, f32[8,128]{1,0:T(8,128)S(1)}, u32[]{:S(2)}, u32[]{:S(2)}) collective-permute-start(f32[8,128]{1,0:T(8,128)S(1)} %add.15.refs_0_), channel_id=1, source_target_pairs={{0,24},{4,28},{8,16},{12,20},{16,8},{20,12},{24,0},{28,4},{1,25},{... | collective-permute-start | bytes 12296 | tf_op jit(solution)/shard_map/ppermute | solution.py:149
  132.3 4.5 %collective-permute-start.28 = (f32[8,128]{1,0:T(8,128)S(1)}, f32[8,128]{1,0:T(8,128)S(1)}, u32[]{:S(2)}, u32[]{:S(2)}) collective-permute-start(f32[8,128]{1,0:T(8,128)S(1)} %add.15.refs_0_), channel_id=1, source_target_pairs={{0,16},{4,20},{8,24},{12,28},{16,0},{20,4},{24,8},{28,12},{1,17},{... | collective-permute-start | bytes 12296 | tf_op jit(solution)/shard_map/ppermute | solution.py:149
  133.9 3.6 %collective-permute-start.27 = (f32[8,128]{1,0:T(8,128)S(1)}, f32[8,128]{1,0:T(8,128)S(1)}, u32[]{:S(2)}, u32[]{:S(2)}) collective-permute-start(f32[8,128]{1,0:T(8,128)S(1)} %add.15.refs_0_), channel_id=1, source_target_pairs={{0,8},{4,12},{8,0},{12,4},{16,24},{20,28},{24,16},{28,20},{1,9},{5... | collective-permute-start | bytes 12296 | tf_op jit(solution)/shard_map/ppermute | solution.py:149
  (27 other events, 355.4 us)

commit v4 on v3

--- a/solution.py
+++ b/solution.py
@@ -424,56 +424,84 @@
     )(*blocks)
 
 
-def residual_kernel(first, batches, sources, *refs):
-    parts, refs = refs[: sources * len(batches)], refs[sources * len(batches) :]
-    seqs, (targets, *refs) = refs[: len(batches)], refs[len(batches) :]
+def residual_kernel(first, slots, sources, carried, ordered, *refs):
+    parts, (seq, targets, *refs) = refs[:sources], refs[sources:]
     if first:
         before, refs = refs[0], refs[1:]
-    combined, errors, squares = refs[-3:]
+    if carried:
+        refs[-2][0:carried, :] = refs[0][...]
+        refs = refs[1:]
+    *blocks, errors, squares = refs
     feats, rows = targets.shape[1:]
     me = lax.axis_index("dp")
     number = lax.broadcasted_iota(jnp.int32, (NSEQ, rows), 0).astype(FLOAT)
     squared = jnp.zeros((NSEQ, rows), FLOAT)
-    slot = 0
-    for block in refs[:-3]:
-        for s in range(block.shape[0]):
-            combined[me ^ slot] = block[s]
-            slot += 1
-    ordered = len(refs) > 3
-    slot = 0
-    for b, slots in enumerate(batches):
-        here = parts[b * sources : (b + 1) * sources]
-        for s in range(slots):
-            total = tree_sum([part[s].astype(FLOAT) for part in here])
-            combined[me ^ (first + slot) if ordered else slot] = total.astype(HALF)
-            error = total - targets[me ^ (first + slot)].astype(FLOAT)
-            errors[slot * feats : (slot + 1) * feats, :] = error.astype(HALF)
-            per_token = jnp.sum(error * error, axis=0, keepdims=True)
-            squared += jnp.where(seqs[b][s, 0:1, :] == number, per_token, 0.0)
-            slot += 1
+    if ordered:
+        for s in range(first):
+            blocks[-1][me ^ s] = blocks[s][...]
+    for s in range(slots):
+        total = tree_sum([part[s].astype(FLOAT) for part in parts])
+        if ordered:
+            blocks[-1][me ^ (first + s)] = total.astype(HALF)
+        else:
+            blocks[s][...] = total.astype(HALF)
+        error = total - targets[me ^ (first + s)].astype(FLOAT)
+        errors[carried + s * feats : carried + (s + 1) * feats, :] = error.astype(HALF)
+        per_token = jnp.sum(error * error, axis=0, keepdims=True)
+        squared += jnp.where(seq[s, 0:1, :] == number, per_token, 0.0)
     sums = jnp.broadcast_to(col_to_row(jnp.sum(squared, axis=1, keepdims=True)), (8, LANES))
     squares[...] = sums + before[...] if first else sums
 
 
-def residual(first, parts, seqs, targets, before, earlier):
-    feats, rows = targets.shape[1:]
-    batches = tuple(batch[0].shape[0] for batch in parts)
-    sources = len(parts[0])
-    slots = sum(batches)
-    extra = [before, *earlier] if first else []
-    return pl.pallas_call(
-        functools.partial(residual_kernel, first, batches, sources),
-        in_specs=in_vmem((sources + 1) * len(batches) + 1 + len(extra)),
-        out_specs=in_vmem(3),
-        out_shape=[
-            jax.ShapeDtypeStruct((slots + first * (len(earlier) > 0), feats, rows), HALF),
-            jax.ShapeDtypeStruct((slots * feats, rows), HALF),
+def residual(first, parts, seq, targets, before=(), errors=(), earlier=()):
+    groups, feats, rows = targets.shape
+    slots = parts[0].shape[0]
+    sources = len(parts)
+    ordered = len(earlier) > 0
+    carried = sum(block.shape[0] for block in errors)
+    if ordered:
+        blocks = [jax.ShapeDtypeStruct((groups, feats, rows), HALF)]
+    else:
+        blocks = [jax.ShapeDtypeStruct((feats, rows), HALF)] * slots
+    extra = [*before, *errors, *earlier]
+    *combined, errors, squares = pl.pallas_call(
+        functools.partial(residual_kernel, first, slots, sources, carried, ordered),
+        in_specs=in_vmem(sources + 2 + len(extra)),
+        out_specs=in_vmem(len(blocks) + 2),
+        out_shape=blocks
+        + [
+            jax.ShapeDtypeStruct((carried + slots * feats, rows), HALF),
             jax.ShapeDtypeStruct((8, LANES), FLOAT),
         ],
         cost_estimate=cost(),
         compiler_params=params(16),
         name="residual",
-    )(*[part for batch in parts for part in batch], *seqs, targets, *extra)
+    )(*parts, seq, targets, *extra)
+    return combined, errors, squares
+
+
+def gather_features_kernel(first, whole, *refs):
+    late, out = refs[:-1], refs[-1]
+    groups, feats, _ = whole.shape
+    me = lax.axis_index("dp")
+    for g in range(groups):
+        out[:, g * feats : (g + 1) * feats] = whole[g].T
+    for k, block in enumerate(late):
+        start = pl.multiple_of((me ^ (first + k)) * feats, feats)
+        out[:, pl.ds(start, feats)] = block[...].T
+
+
+def gather_features(first, whole, late):
+    groups, feats, rows = whole.shape
+    return pl.pallas_call(
+        functools.partial(gather_features_kernel, first),
+        in_specs=in_vmem(1 + len(late)),
+        out_specs=pl.BlockSpec(memory_space=pltpu.VMEM),
+        out_shape=jax.ShapeDtypeStruct((rows, feats * groups), HALF),
+        cost_estimate=cost(),
+        compiler_params=params(16),
+        name="gather_features",
+    )(whole, *late)
 
 
 def gradient_kernel(scale, feat_width, exp_dev, terms, batches, parts, sources, *refs):
@@ -581,7 +609,8 @@
         in_specs=in_vmem(len(squares))
         + [pl.BlockSpec(memory_space=pl.ANY)] * len(spreads)
         + in_vmem(len(seqs))
-        + [pl.BlockSpec(memory_space=pl.ANY)] * len(errors),
+        + [pl.BlockSpec(memory_space=pl.ANY)] * (len(errors) - sources)
+        + in_vmem(sources),
         out_specs=in_vmem(3),
         out_shape=[
             jax.ShapeDtypeStruct((feats, exp_dev, units), FLOAT),
@@ -598,7 +627,7 @@
             pltpu.SemaphoreType.DMA((2, groups)),
         ],
         cost_estimate=cost(),
-        compiler_params=params(),
+        compiler_params=params(58),
         name="gradient",
     )(*squares, *spreads, *seqs, *errors)
 
@@ -652,24 +681,28 @@
 
     batches = (2, groups - 4, 2)
     spread_0, seq_0, parts_0 = expert_parts(0, batches[0])
-    mixed_0, error_0, squares = residual(0, [parts_0], [seq_0], own_targets, None, [])
+    mixed_0, error_0, squares = residual(0, parts_0, seq_0, own_targets)
     errors_0 = far_errors(error_0)
     blocks, errors_0 = tie((blocks, errors_0))
     blocks[6] = z_far(blocks)
 
     spread_1, seq_1, parts_1 = expert_parts(2, batches[1])
     blocks[6], parts_1 = tie((blocks[6], parts_1))
+    mixed_1, error_1, squares = residual(
+        2, parts_1, seq_1, own_targets, before=[squares], earlier=mixed_0
+    )
+    mixed_1 = lax.all_to_all(mixed_1[0], "dp", split_axis=0, concat_axis=0, tiled=True)
     spread_2, seq_2, parts_2 = expert_parts(groups - 2, batches[2])
-    mixed, error_1, squares = residual(
-        2, [parts_1, parts_2], [seq_1, seq_2], own_targets, squares, [mixed_0]
-    )
-    far_squares = [swap(squares, "expert", m) for m in far]
-    error_1, far_squares = tie((error_1, far_squares))
+    mixed_2, error_1, squares = residual(
+        groups - 2, parts_2, seq_2, own_targets, before=[squares], errors=[error_1]
+    )
     errors_1 = far_errors(error_1)
-    squares = tree_sum([squares] + far_squares)
+    mixed_2 = [swap(block, "dp", groups - 2 + s) for s, block in enumerate(mixed_2)]
+    mixed = gather_features(groups - 2, mixed_1, mixed_2)
     squares = squares + swap(squares, "dp", 1)
-    all_squares = [squares] + [swap(squares, "dp", m) for m in range(2, groups, 2)]
-    mixed = lax.all_to_all(mixed, "dp", split_axis=0, concat_axis=0, tiled=True)
+    squares = tree_sum([squares] + [swap(squares, "dp", m) for m in range(2, groups, 2)])
+    squares, mixed = tie((squares, mixed))
+    all_squares = [squares] + [swap(squares, "expert", m) for m in far]
     grad_down, seq_loss, dual_weight = gradient(
         all_squares,
         [spread_0, spread_1, spread_2],
@@ -683,7 +716,7 @@
         exp_dev,
     )
     return (
-        mixed.reshape(feat_width, rows).T,
+        mixed,
         seq_loss.reshape(NSEQ),
         dual_weight.reshape(NSEQ),
         grad_down,

time: 156 us -> 158 us (1.013)
  starting transfers between devices: 46.9 us -> 49.7 us
  waiting for transfers between devices: 59.8 us -> 57.5 us
    ppermute x33 -> x35, waiting for transfers between devices: 53 us -> 50.7 us  [swap(): return lax.ppermute(block, axis, [(s, s ^ mask) for s in range(size)])]
    ppermute x33 -> x35, starting transfers between devices: 38.1 us -> 40.2 us  [swap(): return lax.ppermute(block, axis, [(s, s ^ mask) for s in range(size)])]
    unnamed x49 -> x55, local copies, waits for them, and re-layouts: 8.9 us -> 10.5 us
  transfers between devices with their start and end apart: 35 -> 37, of which waited for: 20 -> 20; matrix products, arithmetic and copies ran while one was open for 1% -> 1% of each run, Pallas kernels for 14% -> 10%
where the time goes in v4:
time: 158 us; the launch traced here: 157 us
  waiting for transfers between devices  57.5 us (36%)
  starting transfers between devices  49.7 us (31%)
  Pallas kernels  36.5 us (23%)
  local copies, waits for them, and re-layouts  12.6 us (8%)
    ppermute x35, waiting for transfers between devices, swap(): return lax.ppermute(block, axis, [(s, s ^ mask) for s in range(size)])  50.7 us
    ppermute x35, starting transfers between devices, swap(): return lax.ppermute(block, axis, [(s, s ^ mask) for s in range(size)])  40.2 us
    unnamed x55, local copies, waits for them, and re-layouts  10.5 us
    pallas_call x1, Pallas kernels, gradient(): pl.pallas_call(functools.partial(gradient_kernel, scale, feat_width, exp_...  9.92 us
    pallas_call x1, Pallas kernels, hidden_rows(): pl.pallas_call(functools.partial(hidden_kernel, experts, capacity), in_sp...  8.76 us
    pallas_call x3, Pallas kernels, spread_rows(): pl.pallas_call(functools.partial(spread_kernel, exp_dev, capacity, rows,...  7.41 us
    all_to_all x1, waiting for transfers between devices, feature_plan(): lax.all_to_all(turned.reshape(groups, feats, rows), 'dp', split_axis=0, c...  6.8 us
    pallas_call x3, Pallas kernels, project(): pl.pallas_call(functools.partial(project_kernel, exp_dev, capacity, rows,...  6.56 us
  transfers between devices with their start and end apart: 37, of which 20 were waited for; matrix products, arithmetic and copies ran while one was open for 1% of the time, Pallas kernels for 10%

profile of v4, /device:TPU:0, one launch (start us, length us, event | category | flops | bytes accessed | tf_op | source)
XLA Modules:
  0.0 157.3 jit_solution(16751355550321525530)
XLA Ops:
  0.6 2.1 %pack_tokens.1.own = bf16[144,2048]{1,0:T(8,128)(2,1)} custom-call(bf16[128,2048]{1,0:T(8,128)(2,1)} %tokens.1, s32[8,128]{1,0:T(8,128)} %bitcast.15, f32[8,128]{1,0:T(8,128)} %bitcast.16, s32[8,128]{1,0:T(8,128)} %bitcast.17, s32[1,128]{1,0:T(1,128)} %bitcast.18), custom_call_target="tpu_custom_call" | custom-call | flops 1 | bytes 1 | tf_op jit(solution)/shard_map/pack_tokens/pallas_call | solution.py:231
  2.7 3.0 %collective-permute-start.1 = (bf16[144,2048]{1,0:T(8,128)(2,1)}, bf16[144,2048]{1,0:T(8,128)(2,1)S(1)}, u32[]{:S(2)}, u32[]{:S(2)}) collective-permute-start(bf16[144,2048]{1,0:T(8,128)(2,1)} %pack_tokens.1.own), channel_id=1, source_target_pairs={{0,2},{1,3},{2,0},{3,1},{4,6},{5,7},{6,4},{7,5},{8,10},{9,11},{10,... | collective-permute-start | bytes 1769480 | tf_op jit(solution)/shard_map/ppermute | solution.py:149
  7.2 2.0 %copy.13 = bf16[2048,128]{1,0:T(8,128)(2,1)} copy(bf16[2048,128]{0,1:T(8,128)(2,1)} %bitcast.14) | data formatting | bytes 1048576 | tf_op jit(solution)/shard_map/optimization_barrier | solution.py:658
  9.2 4.9 %all-to-all-start = ((bf16[8,256,128]{2,1,0:T(8,128)(2,1)}), bf16[8,256,128]{2,1,0:T(8,128)(2,1)S(1)}, u32[]{:S(2)}, u32[]{:S(2)}) async-start(bf16[8,256,128]{2,1,0:T(8,128)(2,1)} %bitcast.5), calls=%async_computation | async-start | bytes 1048576 | tf_op jit(solution)/shard_map/all_to_all | solution.py:659
  14.1 5.1 %collective-permute-done.1.y_side = bf16[144,2048]{1,0:T(8,128)(2,1)S(1)} collective-permute-done((bf16[144,2048]{1,0:T(8,128)(2,1)}, bf16[144,2048]{1,0:T(8,128)(2,1)S(1)}, u32[]{:S(2)}, u32[]{:S(2)}) %collective-permute-start.1) | collective-permute-done | bytes 589856 | tf_op jit(solution)/shard_map/ppermute | solution.py:149
  19.2 1.8 %collective-permute-start.2 = (bf16[80,2048]{1,0:T(8,128)(2,1)S(1)}, bf16[80,2048]{1,0:T(8,128)(2,1)S(1)}, u32[]{:S(2)}, u32[]{:S(2)}) collective-permute-start(bf16[80,2048]{1,0:T(8,128)(2,1)S(1)} %slice.8), channel_id=1, source_target_pairs={{0,1},{1,0},{2,3},{3,2},{4,5},{5,4},{6,7},{7,6},{8,9},{9,8},{10,11... | collective-permute-start | bytes 983048 | tf_op jit(solution)/shard_map/ppermute | solution.py:149
  21.0 1.6 %collective-permute-start.3 = (bf16[80,2048]{1,0:T(8,128)(2,1)S(1)}, bf16[80,2048]{1,0:T(8,128)(2,1)}, u32[]{:S(2)}, u32[]{:S(2)}) collective-permute-start(bf16[80,2048]{1,0:T(8,128)(2,1)S(1)} %slice.9), channel_id=1, source_target_pairs={{0,2},{1,3},{2,0},{3,1},{4,6},{5,7},{6,4},{7,5},{8,10},{9,11},{10,... | collective-permute-start | bytes 983048 | tf_op jit(solution)/shard_map/ppermute | solution.py:149
  22.6 6.8 %all-to-all-done.refs_5_ = bf16[8,256,128]{2,1,0:T(8,128)(2,1)S(1)} async-done(((bf16[8,256,128]{2,1,0:T(8,128)(2,1)}), bf16[8,256,128]{2,1,0:T(8,128)(2,1)S(1)}, u32[]{:S(2)}, u32[]{:S(2)}) %all-to-all-start) | async-done | bytes 524320 | tf_op jit(solution)/shard_map/all_to_all | solution.py:659
  30.2 8.8 %hidden_rows.1.refs_0_ = bf16[1040,384]{1,0:T(8,128)(2,1)} custom-call(bf16[144,2048]{1,0:T(8,128)(2,1)} %pack_tokens.1.own, bf16[144,2048]{1,0:T(8,128)(2,1)} %copy-done.14, bf16[144,2048]{1,0:T(8,128)(2,1)} %copy-done.13, bf16[80,2048]{1,0:T(8,128)(2,1)} %copy-done.19, bf16[80,2048]{1,0:T(8,128)(2,1)} %collective-permute-done.3.lower, ...), custom_call_target="tpu_custom_call" | custom-call | flops 1 | bytes 1 | tf_op jit(solution)/shard_map/hidden_rows/pallas_call | solution.py:304
  39.0 2.0 %collective-permute-start.6 = (bf16[1040,384]{1,0:T(8,128)(2,1)}, bf16[1040,384]{1,0:T(8,128)(2,1)S(1)}, u32[]{:S(2)}, u32[]{:S(2)}) collective-permute-start(bf16[1040,384]{1,0:T(8,128)(2,1)} %hidden_rows.1.refs_0_), channel_id=1, source_target_pairs={{0,16},{4,20},{8,24},{12,28},{16,0},{20,4},{24,8},{28,12},{1,17},{... | collective-permute-start | bytes 2396168 | tf_op jit(solution)/shard_map/ppermute | solution.py:149
  43.9 1.6 %project.3 = (f32[2,8,128]{2,1,0:T(8,128)S(1)}, bf16[2,256,128]{2,1,0:T(8,128)(2,1)S(1)}, bf16[2,256,128]{2,1,0:T(8,128)(2,1)S(1)}, bf16[2,256,128]{2,1,0:T(8,128)(2,1)S(1)}, bf16[2,256,128]{2,1,0:T(8,128)(2,1)S(1)}) custom-call(bf16[1040,384]{1,0:T(8,128)(2,1)S(1)} %copy-done.3, bf16[1040,384]{1,0:T(8,128)(2,1)S(1)} %collective-permute-done.4.refs_1_, ...), custom_call_target="tpu_custom_call" | custom-call | flops 1 | bytes 1 | tf_op jit(solution)/shard_map/project/pallas_call | solution.py:362
  50.2 1.8 %spread_rows.3.refs_4_ = bf16[2,512,1536]{2,1,0:T(8,128)(2,1)S(1)} custom-call(bf16[1040,384]{1,0:T(8,128)(2,1)S(1)} %copy-done.4, bf16[1040,384]{1,0:T(8,128)(2,1)S(1)} %collective-permute-done.4.refs_1_), custom_call_target="tpu_custom_call" | custom-call | flops 1 | bytes 1 | tf_op jit(solution)/shard_map/spread_rows/pallas_call | solution.py:410
  54.9 1.8 %collective-permute-start.12 = (bf16[512,128]{1,0:T(8,128)(2,1)S(1)}, bf16[512,128]{1,0:T(8,128)(2,1)S(1)}, u32[]{:S(2)}, u32[]{:S(2)}) collective-permute-start(bf16[512,128]{1,0:T(8,128)(2,1)S(1)} %get-tuple-element.83.refs_10_), channel_id=1, source_target_pairs={{0,3},{1,2},{2,1},{3,0},{4,7},{5,6},{6,5},{7,4},{8,11},{9,10},{10,... | collective-permute-start | bytes 393224 | tf_op jit(solution)/shard_map/ppermute | solution.py:149
  58.4 19.1 %collective-permute-done.6.refs_2_ = bf16[1040,384]{1,0:T(8,128)(2,1)S(1)} collective-permute-done((bf16[1040,384]{1,0:T(8,128)(2,1)}, bf16[1040,384]{1,0:T(8,128)(2,1)S(1)}, u32[]{:S(2)}, u32[]{:S(2)}) %collective-permute-start.6) | collective-permute-done | bytes 798752 | tf_op jit(solution)/shard_map/ppermute | solution.py:149
  81.3 3.3 %project.4 = (f32[4,8,128]{2,1,0:T(8,128)S(1)}, bf16[4,256,128]{2,1,0:T(8,128)(2,1)S(1)}, bf16[4,256,128]{2,1,0:T(8,128)(2,1)S(1)}, bf16[4,256,128]{2,1,0:T(8,128)(2,1)S(1)}, bf16[4,256,128]{2,1,0:T(8,128)(2,1)S(1)}) custom-call(bf16[1040,384]{1,0:T(8,128)(2,1)S(1)} %collective-permute-done.5.refs_0_, bf16[1040,384]{1,0:T(8,128)(2,1)S(1)} %collective-permute-done.14.refs_1_, ...), custom_call_target="tpu_custom_call" | custom-call | flops 1 | bytes 1 | tf_op jit(solution)/shard_map/project/pallas_call | solution.py:362
  86.3 1.8 %collective-permute-start.18 = (bf16[4,256,128]{2,1,0:T(8,128)(2,1)S(1)}, bf16[4,256,128]{2,1,0:T(8,128)(2,1)S(1)}, u32[]{:S(2)}, u32[]{:S(2)}) collective-permute-start(bf16[4,256,128]{2,1,0:T(8,128)(2,1)S(1)} %get-tuple-element.89), channel_id=1, source_target_pairs={{0,3},{1,2},{2,1},{3,0},{4,7},{5,6},{6,5},{7,4},{8,11},{9,10},{10,... | collective-permute-start | bytes 786440 | tf_op jit(solution)/shard_map/ppermute | solution.py:149
  88.1 3.7 %spread_rows.4.refs_5_ = bf16[4,512,1536]{2,1,0:T(8,128)(2,1)S(1)} custom-call(bf16[1040,384]{1,0:T(8,128)(2,1)S(1)} %collective-permute-done.5.refs_0_, bf16[1040,384]{1,0:T(8,128)(2,1)S(1)} %collective-permute-done.14.refs_1_, bf16[1040,384]{1,0:T(8,128)(2,1)S(1)} %collective-permute-done.6.refs_2_, bf16[1040,384]{1,0:T(8,128)(2,1)S(1)} %collective-permute-done.15.refs_3_), custom_call_target="tpu_custom_call" | custom-call | flops 1 | bytes 1 | tf_op jit(solution)/shard_map/spread_rows/pallas_call | solution.py:410
  91.9 2.6 %copy-done = bf16[4,512,1536]{2,1,0:T(8,128)(2,1)} copy-done((bf16[4,512,1536]{2,1,0:T(8,128)(2,1)}, bf16[4,512,1536]{2,1,0:T(8,128)(2,1)S(1)}, u32[]{:S(2)}) %copy-start) | copy-done | bytes 6291480
  94.5 4.4 %collective-permute-done.18.refs_3_ = bf16[4,256,128]{2,1,0:T(8,128)(2,1)S(1)} collective-permute-done((bf16[4,256,128]{2,1,0:T(8,128)(2,1)S(1)}, bf16[4,256,128]{2,1,0:T(8,128)(2,1)S(1)}, u32[]{:S(2)}, u32[]{:S(2)}) %collective-permute-start.18) | collective-permute-done | bytes 262176 | tf_op jit(solution)/shard_map/ppermute | solution.py:149
  100.8 4.6 %all-to-all-start.1 = ((bf16[8,256,128]{2,1,0:T(8,128)(2,1)}), bf16[8,256,128]{2,1,0:T(8,128)(2,1)S(1)}, u32[]{:S(2)}, u32[]{:S(2)}) async-start(bf16[8,256,128]{2,1,0:T(8,128)(2,1)} %copy-done.5), calls=%async_computation.1 | async-start | bytes 1048576 | tf_op jit(solution)/shard_map/all_to_all | solution.py:694
  105.4 1.6 %project.5 = (f32[2,8,128]{2,1,0:T(8,128)S(1)}, bf16[2,256,128]{2,1,0:T(8,128)(2,1)S(1)}, bf16[2,256,128]{2,1,0:T(8,128)(2,1)S(1)}, bf16[2,256,128]{2,1,0:T(8,128)(2,1)S(1)}, bf16[2,256,128]{2,1,0:T(8,128)(2,1)S(1)}) custom-call(bf16[1040,384]{1,0:T(8,128)(2,1)S(1)} %collective-permute-done.13.refs_0_, ...), custom_call_target="tpu_custom_call" | custom-call | flops 1 | bytes 1 | tf_op jit(solution)/shard_map/project/pallas_call | solution.py:362
  110.6 1.9 %spread_rows.5.refs_6_ = bf16[2,512,1536]{2,1,0:T(8,128)(2,1)S(1)} custom-call(bf16[1040,384]{1,0:T(8,128)(2,1)S(1)} %collective-permute-done.13.refs_0_, bf16[1040,384]{1,0:T(8,128)(2,1)S(1)} %collective-permute-done.19.refs_1_), custom_call_target="tpu_custom_call" | custom-call | flops 1 | bytes 1 | tf_op jit(solution)/shard_map/spread_rows/pallas_call | solution.py:410
  112.5 1.7 %copy-done.2 = bf16[2,512,1536]{2,1,0:T(8,128)(2,1)} copy-done((bf16[2,512,1536]{2,1,0:T(8,128)(2,1)}, bf16[2,512,1536]{2,1,0:T(8,128)(2,1)S(1)}, u32[]{:S(2)}) %copy-start.2) | copy-done | bytes 3145752
  116.6 1.8 %collective-permute-start.34 = (bf16[1536,128]{1,0:T(8,128)(2,1)S(1)}, bf16[1536,128]{1,0:T(8,128)(2,1)S(1)}, u32[]{:S(2)}, u32[]{:S(2)}) collective-permute-start(bf16[1536,128]{1,0:T(8,128)(2,1)S(1)} %get-tuple-element.126.refs_14_), channel_id=1, source_target_pairs={{0,3},{1,2},{2,1},{3,0},{4,7},{5,6},{6,5},{7,4},{8,11},{9,10},{10,... | collective-permute-start | bytes 1179656 | tf_op jit(solution)/shard_map/ppermute | solution.py:149
  121.3 3.5 %collective-permute-start.26 = (f32[8,128]{1,0:T(8,128)S(1)}, f32[8,128]{1,0:T(8,128)S(1)}, u32[]{:S(2)}, u32[]{:S(2)}) collective-permute-start(f32[8,128]{1,0:T(8,128)S(1)} %add.12), channel_id=1, source_target_pairs={{0,24},{4,28},{8,16},{12,20},{16,8},{20,12},{24,0},{28,4},{1,25},{... | collective-permute-start | bytes 12296 | tf_op jit(solution)/shard_map/ppermute | solution.py:149
  124.8 1.9 %collective-permute-done.26 = f32[8,128]{1,0:T(8,128)S(1)} collective-permute-done((f32[8,128]{1,0:T(8,128)S(1)}, f32[8,128]{1,0:T(8,128)S(1)}, u32[]{:S(2)}, u32[]{:S(2)}) %collective-permute-start.26) | collective-permute-done | bytes 4128 | tf_op jit(solution)/shard_map/ppermute | solution.py:149
  126.7 2.6 %collective-permute-done.25 = f32[8,128]{1,0:T(8,128)S(1)} collective-permute-done((f32[8,128]{1,0:T(8,128)S(1)}, f32[8,128]{1,0:T(8,128)S(1)}, u32[]{:S(2)}, u32[]{:S(2)}) %collective-permute-start.25) | collective-permute-done | bytes 4128 | tf_op jit(solution)/shard_map/ppermute | solution.py:149
  131.6 4.2 %collective-permute-done.27.refs_0_ = bf16[256,128]{1,0:T(8,128)(2,1)S(1)} collective-permute-done((bf16[256,128]{1,0:T(8,128)(2,1)S(1)}, bf16[256,128]{1,0:T(8,128)(2,1)S(1)}, u32[]{:S(2)}, u32[]{:S(2)}) %collective-permute-start.27) | collective-permute-done | bytes 65568 | tf_op jit(solution)/shard_map/ppermute | solution.py:149
  137.5 1.7 %collective-permute-start.31 = (f32[8,128]{1,0:T(8,128)S(1)}, f32[8,128]{1,0:T(8,128)S(1)}, u32[]{:S(2)}, u32[]{:S(2)}) collective-permute-start(f32[8,128]{1,0:T(8,128)S(1)} %add_add_fusion.refs_0_), channel_id=1, source_target_pairs={{0,3},{1,2},{2,1},{3,0},{4,7},{5,6},{6,5},{7,4},{8,11},{9,10},{10,... | collective-permute-start | bytes 12296 | tf_op jit(solution)/shard_map/ppermute | solution.py:149
  140.2 1.8 %collective-permute-done.31.refs_3_ = f32[8,128]{1,0:T(8,128)S(1)} collective-permute-done((f32[8,128]{1,0:T(8,128)S(1)}, f32[8,128]{1,0:T(8,128)S(1)}, u32[]{:S(2)}, u32[]{:S(2)}) %collective-permute-start.31) | collective-permute-done | bytes 4128 | tf_op jit(solution)/shard_map/ppermute | solution.py:149
  143.3 2.4 %collective-permute-done.29.refs_1_ = f32[8,128]{1,0:T(8,128)S(1)} collective-permute-done((f32[8,128]{1,0:T(8,128)S(1)}, f32[8,128]{1,0:T(8,128)S(1)}, u32[]{:S(2)}, u32[]{:S(2)}) %collective-permute-start.29) | collective-permute-done | bytes 4128 | tf_op jit(solution)/shard_map/ppermute | solution.py:149
  147.3 9.9 %gradient.1 = (f32[256,4,384]{2,1,0:T(4,128)}, f32[1,64]{1,0:T(1,128)}, f32[1,64]{1,0:T(1,128)}) custom-call(f32[8,128]{1,0:T(8,128)} %copy-done.23, f32[8,128]{1,0:T(8,128)} %copy-done.26, f32[8,128]{1,0:T(8,128)} %copy-done.25, f32[8,128]{1,0:T(8,128)} %copy-done.24, bf16[2,512,1536]{2,1,0:T(8,128)(2,1)} %copy-done.1, bf16[4,512,1536]{2,1,0:T(8,128)(2,1)} %copy-done, ...), custom_call_target="tpu_custom_call" | custom-call | flops 1 | bytes 1 | tf_op jit(solution)/shard_map/gradient/pallas_call | solution.py:605
  (115 shorter events, 38.2 us)
Async XLA Ops:
  2.7 16.5 %collective-permute-start.1 = (bf16[144,2048]{1,0:T(8,128)(2,1)}, bf16[144,2048]{1,0:T(8,128)(2,1)S(1)}, u32[]{:S(2)}, u32[]{:S(2)}) collective-permute-start(bf16[144,2048]{1,0:T(8,128)(2,1)} %pack_tokens.1.own), channel_id=1, source_target_pairs={{0,2},{1,3},{2,0},{3,1},{4,6},{5,7},{6,4},{7,5},{8,10},{9,11},{10,... | collective-permute-start | bytes 1769480 | tf_op jit(solution)/shard_map/ppermute | solution.py:149
  5.7 15.3 %collective-permute-start = (bf16[144,2048]{1,0:T(8,128)(2,1)}, bf16[144,2048]{1,0:T(8,128)(2,1)S(1)}, u32[]{:S(2)}, u32[]{:S(2)}) collective-permute-start(bf16[144,2048]{1,0:T(8,128)(2,1)} %pack_tokens.1.own), channel_id=1, source_target_pairs={{0,1},{1,0},{2,3},{3,2},{4,5},{5,4},{6,7},{7,6},{8,9},{9,8},{10,11... | collective-permute-start | bytes 1769480 | tf_op jit(solution)/shard_map/ppermute | solution.py:149
  9.2 20.2 %all-to-all-start = ((bf16[8,256,128]{2,1,0:T(8,128)(2,1)}), bf16[8,256,128]{2,1,0:T(8,128)(2,1)S(1)}, u32[]{:S(2)}, u32[]{:S(2)}) async-start(bf16[8,256,128]{2,1,0:T(8,128)(2,1)} %bitcast.5), calls=%async_computation | async-start | bytes 1048576 | tf_op jit(solution)/shard_map/all_to_all | solution.py:659
  19.2 10.2 %collective-permute-start.2 = (bf16[80,2048]{1,0:T(8,128)(2,1)S(1)}, bf16[80,2048]{1,0:T(8,128)(2,1)S(1)}, u32[]{:S(2)}, u32[]{:S(2)}) collective-permute-start(bf16[80,2048]{1,0:T(8,128)(2,1)S(1)} %slice.8), channel_id=1, source_target_pairs={{0,1},{1,0},{2,3},{3,2},{4,5},{5,4},{6,7},{7,6},{8,9},{9,8},{10,11... | collective-permute-start | bytes 983048 | tf_op jit(solution)/shard_map/ppermute | solution.py:149
  21.0 8.5 %collective-permute-start.3 = (bf16[80,2048]{1,0:T(8,128)(2,1)S(1)}, bf16[80,2048]{1,0:T(8,128)(2,1)}, u32[]{:S(2)}, u32[]{:S(2)}) collective-permute-start(bf16[80,2048]{1,0:T(8,128)(2,1)S(1)} %slice.9), channel_id=1, source_target_pairs={{0,2},{1,3},{2,0},{3,1},{4,6},{5,7},{6,4},{7,5},{8,10},{9,11},{10,... | collective-permute-start | bytes 983048 | tf_op jit(solution)/shard_map/ppermute | solution.py:149
  38.9 3.8 %collective-permute-start.4 = (bf16[1040,384]{1,0:T(8,128)(2,1)}, bf16[1040,384]{1,0:T(8,128)(2,1)S(1)}, u32[]{:S(2)}, u32[]{:S(2)}) collective-permute-start(bf16[1040,384]{1,0:T(8,128)(2,1)} %hidden_rows.1.refs_0_), channel_id=1, source_target_pairs={{0,4},{4,0},{8,12},{12,8},{16,20},{20,16},{24,28},{28,24},{1,5},{5... | collective-permute-start | bytes 2396168 | tf_op jit(solution)/shard_map/ppermute | solution.py:149
  39.0 38.6 %collective-permute-start.6 = (bf16[1040,384]{1,0:T(8,128)(2,1)}, bf16[1040,384]{1,0:T(8,128)(2,1)S(1)}, u32[]{:S(2)}, u32[]{:S(2)}) collective-permute-start(bf16[1040,384]{1,0:T(8,128)(2,1)} %hidden_rows.1.refs_0_), channel_id=1, source_target_pairs={{0,16},{4,20},{8,24},{12,28},{16,0},{20,4},{24,8},{28,12},{1,17},{... | collective-permute-start | bytes 2396168 | tf_op jit(solution)/shard_map/ppermute | solution.py:149
  41.0 36.7 %collective-permute-start.5 = (bf16[1040,384]{1,0:T(8,128)(2,1)}, bf16[1040,384]{1,0:T(8,128)(2,1)S(1)}, u32[]{:S(2)}, u32[]{:S(2)}) collective-permute-start(bf16[1040,384]{1,0:T(8,128)(2,1)} %hidden_rows.1.refs_0_), channel_id=1, source_target_pairs={{0,8},{4,12},{8,0},{12,4},{16,24},{20,28},{24,16},{28,20},{1,9},{5... | collective-permute-start | bytes 2396168 | tf_op jit(solution)/shard_map/ppermute | solution.py:149
  45.5 6.6 %collective-permute-start.7 = (bf16[2,256,128]{2,1,0:T(8,128)(2,1)S(1)}, bf16[2,256,128]{2,1,0:T(8,128)(2,1)S(1)}, u32[]{:S(2)}, u32[]{:S(2)}) collective-permute-start(bf16[2,256,128]{2,1,0:T(8,128)(2,1)S(1)} %get-tuple-element.74), channel_id=1, source_target_pairs={{0,1},{1,0},{2,3},{3,2},{4,5},{5,4},{6,7},{7,6},{8,9},{9,8},{10,11... | collective-permute-start | bytes 393224 | tf_op jit(solution)/shard_map/ppermute | solution.py:149
  46.7 6.6 %collective-permute-start.8 = (bf16[2,256,128]{2,1,0:T(8,128)(2,1)S(1)}, bf16[2,256,128]{2,1,0:T(8,128)(2,1)S(1)}, u32[]{:S(2)}, u32[]{:S(2)}) collective-permute-start(bf16[2,256,128]{2,1,0:T(8,128)(2,1)S(1)} %get-tuple-element.75), channel_id=1, source_target_pairs={{0,2},{1,3},{2,0},{3,1},{4,6},{5,7},{6,4},{7,5},{8,10},{9,11},{10,... | collective-permute-start | bytes 393224 | tf_op jit(solution)/shard_map/ppermute | solution.py:149
  47.9 6.8 %collective-permute-start.9 = (bf16[2,256,128]{2,1,0:T(8,128)(2,1)S(1)}, bf16[2,256,128]{2,1,0:T(8,128)(2,1)S(1)}, u32[]{:S(2)}, u32[]{:S(2)}) collective-permute-start(bf16[2,256,128]{2,1,0:T(8,128)(2,1)S(1)} %get-tuple-element.76), channel_id=1, source_target_pairs={{0,3},{1,2},{2,1},{3,0},{4,7},{5,6},{6,5},{7,4},{8,11},{9,10},{10,... | collective-permute-start | bytes 393224 | tf_op jit(solution)/shard_map/ppermute | solution.py:149
  54.9 22.9 %collective-permute-start.12 = (bf16[512,128]{1,0:T(8,128)(2,1)S(1)}, bf16[512,128]{1,0:T(8,128)(2,1)S(1)}, u32[]{:S(2)}, u32[]{:S(2)}) collective-permute-start(bf16[512,128]{1,0:T(8,128)(2,1)S(1)} %get-tuple-element.83.refs_10_), channel_id=1, source_target_pairs={{0,3},{1,2},{2,1},{3,0},{4,7},{5,6},{6,5},{7,4},{8,11},{9,10},{10,... | collective-permute-start | bytes 393224 | tf_op jit(solution)/shard_map/ppermute | solution.py:149
  56.7 21.1 %collective-permute-start.11 = (bf16[512,128]{1,0:T(8,128)(2,1)S(1)}, bf16[512,128]{1,0:T(8,128)(2,1)S(1)}, u32[]{:S(2)}, u32[]{:S(2)}) collective-permute-start(bf16[512,128]{1,0:T(8,128)(2,1)S(1)} %get-tuple-element.83.refs_10_), channel_id=1, source_target_pairs={{0,2},{1,3},{2,0},{3,1},{4,6},{5,7},{6,4},{7,5},{8,10},{9,11},{10,... | collective-permute-start | bytes 393224 | tf_op jit(solution)/shard_map/ppermute | solution.py:149
  57.2 20.6 %collective-permute-start.10 = (bf16[512,128]{1,0:T(8,128)(2,1)S(1)}, bf16[512,128]{1,0:T(8,128)(2,1)S(1)}, u32[]{:S(2)}, u32[]{:S(2)}) collective-permute-start(bf16[512,128]{1,0:T(8,128)(2,1)S(1)} %get-tuple-element.83.refs_10_), channel_id=1, source_target_pairs={{0,1},{1,0},{2,3},{3,2},{4,5},{5,4},{6,7},{7,6},{8,9},{9,8},{10,11... | collective-permute-start | bytes 393224 | tf_op jit(solution)/shard_map/ppermute | solution.py:149
  78.4 20.6 %collective-permute-start.13 = (bf16[1040,384]{1,0:T(8,128)(2,1)S(1)}, bf16[1040,384]{1,0:T(8,128)(2,1)S(1)}, u32[]{:S(2)}, u32[]{:S(2)}) collective-permute-start(bf16[1040,384]{1,0:T(8,128)(2,1)S(1)} %collective-permute-done.6.refs_2_), channel_id=1, source_target_pairs={{0,8},{4,12},{8,0},{12,4},{16,24},{20,28},{24,16},{28,20},{1,9},{5... | collective-permute-start | bytes 2396168 | tf_op jit(solution)/shard_map/ppermute | solution.py:149
  84.6 9.9 %collective-permute-start.16 = (bf16[4,256,128]{2,1,0:T(8,128)(2,1)S(1)}, bf16[4,256,128]{2,1,0:T(8,128)(2,1)S(1)}, u32[]{:S(2)}, u32[]{:S(2)}) collective-permute-start(bf16[4,256,128]{2,1,0:T(8,128)(2,1)S(1)} %get-tuple-element.87), channel_id=1, source_target_pairs={{0,1},{1,0},{2,3},{3,2},{4,5},{5,4},{6,7},{7,6},{8,9},{9,8},{10,11... | collective-permute-start | bytes 786440 | tf_op jit(solution)/shard_map/ppermute | solution.py:149
  85.2 9.3 %collective-permute-start.17 = (bf16[4,256,128]{2,1,0:T(8,128)(2,1)S(1)}, bf16[4,256,128]{2,1,0:T(8,128)(2,1)S(1)}, u32[]{:S(2)}, u32[]{:S(2)}) collective-permute-start(bf16[4,256,128]{2,1,0:T(8,128)(2,1)S(1)} %get-tuple-element.88), channel_id=1, source_target_pairs={{0,2},{1,3},{2,0},{3,1},{4,6},{5,7},{6,4},{7,5},{8,10},{9,11},{10,... | collective-permute-start | bytes 786440 | tf_op jit(solution)/shard_map/ppermute | solution.py:149
  86.3 12.6 %collective-permute-start.18 = (bf16[4,256,128]{2,1,0:T(8,128)(2,1)S(1)}, bf16[4,256,128]{2,1,0:T(8,128)(2,1)S(1)}, u32[]{:S(2)}, u32[]{:S(2)}) collective-permute-start(bf16[4,256,128]{2,1,0:T(8,128)(2,1)S(1)} %get-tuple-element.89), channel_id=1, source_target_pairs={{0,3},{1,2},{2,1},{3,0},{4,7},{5,6},{6,5},{7,4},{8,11},{9,10},{10,... | collective-permute-start | bytes 786440 | tf_op jit(solution)/shard_map/ppermute | solution.py:149
  99.0 6.4 %collective-permute-start.19 = (bf16[1040,384]{1,0:T(8,128)(2,1)S(1)}, bf16[1040,384]{1,0:T(8,128)(2,1)S(1)}, u32[]{:S(2)}, u32[]{:S(2)}) collective-permute-start(bf16[1040,384]{1,0:T(8,128)(2,1)S(1)} %collective-permute-done.13.refs_0_), channel_id=1, source_target_pairs={{0,4},{4,0},{8,12},{12,8},{16,20},{20,16},{24,28},{28,24},{1,5},{5... | collective-permute-start | bytes 2396168 | tf_op jit(solution)/shard_map/ppermute | solution.py:149
  100.8 30.8 %all-to-all-start.1 = ((bf16[8,256,128]{2,1,0:T(8,128)(2,1)}), bf16[8,256,128]{2,1,0:T(8,128)(2,1)S(1)}, u32[]{:S(2)}, u32[]{:S(2)}) async-start(bf16[8,256,128]{2,1,0:T(8,128)(2,1)} %copy-done.5), calls=%async_computation.1 | async-start | bytes 1048576 | tf_op jit(solution)/shard_map/all_to_all | solution.py:694
  107.1 7.2 %collective-permute-start.20 = (bf16[2,256,128]{2,1,0:T(8,128)(2,1)S(1)}, bf16[2,256,128]{2,1,0:T(8,128)(2,1)S(1)}, u32[]{:S(2)}, u32[]{:S(2)}) collective-permute-start(bf16[2,256,128]{2,1,0:T(8,128)(2,1)S(1)} %get-tuple-element.96), channel_id=1, source_target_pairs={{0,1},{1,0},{2,3},{3,2},{4,5},{5,4},{6,7},{7,6},{8,9},{9,8},{10,11... | collective-permute-start | bytes 393224 | tf_op jit(solution)/shard_map/ppermute | solution.py:149
  107.9 7.5 %collective-permute-start.21 = (bf16[2,256,128]{2,1,0:T(8,128)(2,1)S(1)}, bf16[2,256,128]{2,1,0:T(8,128)(2,1)S(1)}, u32[]{:S(2)}, u32[]{:S(2)}) collective-permute-start(bf16[2,256,128]{2,1,0:T(8,128)(2,1)S(1)} %get-tuple-element.97), channel_id=1, source_target_pairs={{0,2},{1,3},{2,0},{3,1},{4,6},{5,7},{6,4},{7,5},{8,10},{9,11},{10,... | collective-permute-start | bytes 393224 | tf_op jit(solution)/shard_map/ppermute | solution.py:149
  109.4 6.9 %collective-permute-start.22 = (bf16[2,256,128]{2,1,0:T(8,128)(2,1)S(1)}, bf16[2,256,128]{2,1,0:T(8,128)(2,1)S(1)}, u32[]{:S(2)}, u32[]{:S(2)}) collective-permute-start(bf16[2,256,128]{2,1,0:T(8,128)(2,1)S(1)} %get-tuple-element.98), channel_id=1, source_target_pairs={{0,3},{1,2},{2,1},{3,0},{4,7},{5,6},{6,5},{7,4},{8,11},{9,10},{10,... | collective-permute-start | bytes 393224 | tf_op jit(solution)/shard_map/ppermute | solution.py:149
  116.6 29.1 %collective-permute-start.34 = (bf16[1536,128]{1,0:T(8,128)(2,1)S(1)}, bf16[1536,128]{1,0:T(8,128)(2,1)S(1)}, u32[]{:S(2)}, u32[]{:S(2)}) collective-permute-start(bf16[1536,128]{1,0:T(8,128)(2,1)S(1)} %get-tuple-element.126.refs_14_), channel_id=1, source_target_pairs={{0,3},{1,2},{2,1},{3,0},{4,7},{5,6},{6,5},{7,4},{8,11},{9,10},{10,... | collective-permute-start | bytes 1179656 | tf_op jit(solution)/shard_map/ppermute | solution.py:149
  118.4 27.3 %collective-permute-start.33 = (bf16[1536,128]{1,0:T(8,128)(2,1)S(1)}, bf16[1536,128]{1,0:T(8,128)(2,1)S(1)}, u32[]{:S(2)}, u32[]{:S(2)}) collective-permute-start(bf16[1536,128]{1,0:T(8,128)(2,1)S(1)} %get-tuple-element.126.refs_14_), channel_id=1, source_target_pairs={{0,2},{1,3},{2,0},{3,1},{4,6},{5,7},{6,4},{7,5},{8,10},{9,11},{10,... | collective-permute-start | bytes 1179656 | tf_op jit(solution)/shard_map/ppermute | solution.py:149
  119.3 26.3 %collective-permute-start.32 = (bf16[1536,128]{1,0:T(8,128)(2,1)S(1)}, bf16[1536,128]{1,0:T(8,128)(2,1)S(1)}, u32[]{:S(2)}, u32[]{:S(2)}) collective-permute-start(bf16[1536,128]{1,0:T(8,128)(2,1)S(1)} %get-tuple-element.126.refs_14_), channel_id=1, source_target_pairs={{0,1},{1,0},{2,3},{3,2},{4,5},{5,4},{6,7},{7,6},{8,9},{9,8},{10,11... | collective-permute-start | bytes 1179656 | tf_op jit(solution)/shard_map/ppermute | solution.py:149
  121.3 5.4 %collective-permute-start.26 = (f32[8,128]{1,0:T(8,128)S(1)}, f32[8,128]{1,0:T(8,128)S(1)}, u32[]{:S(2)}, u32[]{:S(2)}) collective-permute-start(f32[8,128]{1,0:T(8,128)S(1)} %add.12), channel_id=1, source_target_pairs={{0,24},{4,28},{8,16},{12,20},{16,8},{20,12},{24,0},{28,4},{1,25},{... | collective-permute-start | bytes 12296 | tf_op jit(solution)/shard_map/ppermute | solution.py:149
  124.8 4.5 %collective-permute-start.25 = (f32[8,128]{1,0:T(8,128)S(1)}, f32[8,128]{1,0:T(8,128)S(1)}, u32[]{:S(2)}, u32[]{:S(2)}) collective-permute-start(f32[8,128]{1,0:T(8,128)S(1)} %add.12), channel_id=1, source_target_pairs={{0,16},{4,20},{8,24},{12,28},{16,0},{20,4},{24,8},{28,12},{1,17},{... | collective-permute-start | bytes 12296 | tf_op jit(solution)/shard_map/ppermute | solution.py:149
  129.3 6.5 %collective-permute-start.27 = (bf16[256,128]{1,0:T(8,128)(2,1)S(1)}, bf16[256,128]{1,0:T(8,128)(2,1)S(1)}, u32[]{:S(2)}, u32[]{:S(2)}) collective-permute-start(bf16[256,128]{1,0:T(8,128)(2,1)S(1)} %get-tuple-element.116), channel_id=1, source_target_pairs={{0,24},{4,28},{8,16},{12,20},{16,8},{20,12},{24,0},{28,4},{1,25},{... | collective-permute-start | bytes 196616 | tf_op jit(solution)/shard_map/ppermute | solution.py:149
  130.3 6.2 %collective-permute-start.28 = (bf16[256,128]{1,0:T(8,128)(2,1)S(1)}, bf16[256,128]{1,0:T(8,128)(2,1)S(1)}, u32[]{:S(2)}, u32[]{:S(2)}) collective-permute-start(bf16[256,128]{1,0:T(8,128)(2,1)S(1)} %get-tuple-element.117), channel_id=1, source_target_pairs={{0,28},{4,24},{8,20},{12,16},{16,12},{20,8},{24,4},{28,0},{1,29},{... | collective-permute-start | bytes 196616 | tf_op jit(solution)/shard_map/ppermute | solution.py:149
  137.5 4.5 %collective-permute-start.31 = (f32[8,128]{1,0:T(8,128)S(1)}, f32[8,128]{1,0:T(8,128)S(1)}, u32[]{:S(2)}, u32[]{:S(2)}) collective-permute-start(f32[8,128]{1,0:T(8,128)S(1)} %add_add_fusion.refs_0_), channel_id=1, source_target_pairs={{0,3},{1,2},{2,1},{3,0},{4,7},{5,6},{6,5},{7,4},{8,11},{9,10},{10,... | collective-permute-start | bytes 12296 | tf_op jit(solution)/shard_map/ppermute | solution.py:149
  139.3 4.0 %collective-permute-start.30 = (f32[8,128]{1,0:T(8,128)S(1)}, f32[8,128]{1,0:T(8,128)S(1)}, u32[]{:S(2)}, u32[]{:S(2)}) collective-permute-start(f32[8,128]{1,0:T(8,128)S(1)} %add_add_fusion.refs_0_), channel_id=1, source_target_pairs={{0,2},{1,3},{2,0},{3,1},{4,6},{5,7},{6,4},{7,5},{8,10},{9,11},{10,... | collective-permute-start | bytes 12296 | tf_op jit(solution)/shard_map/ppermute | solution.py:149
  (32 other events, 300.9 us)

commit v5 on v4

--- a/solution.py
+++ b/solution.py
@@ -701,7 +701,6 @@
     mixed = gather_features(groups - 2, mixed_1, mixed_2)
     squares = squares + swap(squares, "dp", 1)
     squares = tree_sum([squares] + [swap(squares, "dp", m) for m in range(2, groups, 2)])
-    squares, mixed = tie((squares, mixed))
     all_squares = [squares] + [swap(squares, "expert", m) for m in far]
     grad_down, seq_loss, dual_weight = gradient(
         all_squares,

time: 158 us -> 159 us (level)
  starting transfers between devices: 49.7 us -> 51.8 us
    ppermute x35, starting transfers between devices: 40.2 us -> 42.3 us  [swap(): return lax.ppermute(block, axis, [(s, s ^ mask) for s in range(size)])]
where the time goes in v5:
time: 159 us; the launch traced here: 158 us
  waiting for transfers between devices  56.3 us (35%)
  starting transfers between devices  51.8 us (33%)
  Pallas kernels  36.5 us (23%)
  local copies, waits for them, and re-layouts  12.6 us (8%)
    ppermute x35, waiting for transfers between devices, swap(): return lax.ppermute(block, axis, [(s, s ^ mask) for s in range(size)])  49.5 us
    ppermute x35, starting transfers between devices, swap(): return lax.ppermute(block, axis, [(s, s ^ mask) for s in range(size)])  42.3 us
    unnamed x55, local copies, waits for them, and re-layouts  10.5 us
    pallas_call x1, Pallas kernels, gradient(): pl.pallas_call(functools.partial(gradient_kernel, scale, feat_width, exp_...  9.92 us
    pallas_call x1, Pallas kernels, hidden_rows(): pl.pallas_call(functools.partial(hidden_kernel, experts, capacity), in_sp...  8.76 us
    pallas_call x3, Pallas kernels, spread_rows(): pl.pallas_call(functools.partial(spread_kernel, exp_dev, capacity, rows,...  7.41 us
    all_to_all x1, waiting for transfers between devices, feature_plan(): lax.all_to_all(turned.reshape(groups, feats, rows), 'dp', split_axis=0, c...  6.8 us
    pallas_call x3, Pallas kernels, project(): pl.pallas_call(functools.partial(project_kernel, exp_dev, capacity, rows,...  6.56 us
  transfers between devices with their start and end apart: 37, of which 20 were waited for; matrix products, arithmetic and copies ran while one was open for 1% of the time, Pallas kernels for 10%

profile of v5, /device:TPU:0, one launch (start us, length us, event | category | flops | bytes accessed | tf_op | source)
XLA Modules:
  0.0 158.3 jit_solution(2608875641207197534)
XLA Ops:
  0.6 2.1 %pack_tokens.1.own = bf16[144,2048]{1,0:T(8,128)(2,1)} custom-call(bf16[128,2048]{1,0:T(8,128)(2,1)} %tokens.1, s32[8,128]{1,0:T(8,128)} %bitcast.15, f32[8,128]{1,0:T(8,128)} %bitcast.16, s32[8,128]{1,0:T(8,128)} %bitcast.17, s32[1,128]{1,0:T(1,128)} %bitcast.18), custom_call_target="tpu_custom_call" | custom-call | flops 1 | bytes 1 | tf_op jit(solution)/shard_map/pack_tokens/pallas_call | solution.py:231
  2.7 3.0 %collective-permute-start.1 = (bf16[144,2048]{1,0:T(8,128)(2,1)}, bf16[144,2048]{1,0:T(8,128)(2,1)S(1)}, u32[]{:S(2)}, u32[]{:S(2)}) collective-permute-start(bf16[144,2048]{1,0:T(8,128)(2,1)} %pack_tokens.1.own), channel_id=1, source_target_pairs={{0,2},{1,3},{2,0},{3,1},{4,6},{5,7},{6,4},{7,5},{8,10},{9,11},{10,... | collective-permute-start | bytes 1769480 | tf_op jit(solution)/shard_map/ppermute | solution.py:149
  7.2 2.0 %copy.13 = bf16[2048,128]{1,0:T(8,128)(2,1)} copy(bf16[2048,128]{0,1:T(8,128)(2,1)} %bitcast.14) | data formatting | bytes 1048576 | tf_op jit(solution)/shard_map/optimization_barrier | solution.py:658
  9.2 4.9 %all-to-all-start = ((bf16[8,256,128]{2,1,0:T(8,128)(2,1)}), bf16[8,256,128]{2,1,0:T(8,128)(2,1)S(1)}, u32[]{:S(2)}, u32[]{:S(2)}) async-start(bf16[8,256,128]{2,1,0:T(8,128)(2,1)} %bitcast.5), calls=%async_computation | async-start | bytes 1048576 | tf_op jit(solution)/shard_map/all_to_all | solution.py:659
  14.1 5.1 %collective-permute-done.1.y_side = bf16[144,2048]{1,0:T(8,128)(2,1)S(1)} collective-permute-done((bf16[144,2048]{1,0:T(8,128)(2,1)}, bf16[144,2048]{1,0:T(8,128)(2,1)S(1)}, u32[]{:S(2)}, u32[]{:S(2)}) %collective-permute-start.1) | collective-permute-done | bytes 589856 | tf_op jit(solution)/shard_map/ppermute | solution.py:149
  19.2 1.8 %collective-permute-start.2 = (bf16[80,2048]{1,0:T(8,128)(2,1)S(1)}, bf16[80,2048]{1,0:T(8,128)(2,1)S(1)}, u32[]{:S(2)}, u32[]{:S(2)}) collective-permute-start(bf16[80,2048]{1,0:T(8,128)(2,1)S(1)} %slice.8), channel_id=1, source_target_pairs={{0,1},{1,0},{2,3},{3,2},{4,5},{5,4},{6,7},{7,6},{8,9},{9,8},{10,11... | collective-permute-start | bytes 983048 | tf_op jit(solution)/shard_map/ppermute | solution.py:149
  21.0 1.6 %collective-permute-start.3 = (bf16[80,2048]{1,0:T(8,128)(2,1)S(1)}, bf16[80,2048]{1,0:T(8,128)(2,1)}, u32[]{:S(2)}, u32[]{:S(2)}) collective-permute-start(bf16[80,2048]{1,0:T(8,128)(2,1)S(1)} %slice.9), channel_id=1, source_target_pairs={{0,2},{1,3},{2,0},{3,1},{4,6},{5,7},{6,4},{7,5},{8,10},{9,11},{10,... | collective-permute-start | bytes 983048 | tf_op jit(solution)/shard_map/ppermute | solution.py:149
  22.6 6.8 %all-to-all-done.refs_5_ = bf16[8,256,128]{2,1,0:T(8,128)(2,1)S(1)} async-done(((bf16[8,256,128]{2,1,0:T(8,128)(2,1)}), bf16[8,256,128]{2,1,0:T(8,128)(2,1)S(1)}, u32[]{:S(2)}, u32[]{:S(2)}) %all-to-all-start) | async-done | bytes 524320 | tf_op jit(solution)/shard_map/all_to_all | solution.py:659
  30.2 8.8 %hidden_rows.1.refs_0_ = bf16[1040,384]{1,0:T(8,128)(2,1)} custom-call(bf16[144,2048]{1,0:T(8,128)(2,1)} %pack_tokens.1.own, bf16[144,2048]{1,0:T(8,128)(2,1)} %copy-done.14, bf16[144,2048]{1,0:T(8,128)(2,1)} %copy-done.13, bf16[80,2048]{1,0:T(8,128)(2,1)} %copy-done.19, bf16[80,2048]{1,0:T(8,128)(2,1)} %collective-permute-done.3.lower, ...), custom_call_target="tpu_custom_call" | custom-call | flops 1 | bytes 1 | tf_op jit(solution)/shard_map/hidden_rows/pallas_call | solution.py:304
  39.0 2.0 %collective-permute-start.6 = (bf16[1040,384]{1,0:T(8,128)(2,1)}, bf16[1040,384]{1,0:T(8,128)(2,1)S(1)}, u32[]{:S(2)}, u32[]{:S(2)}) collective-permute-start(bf16[1040,384]{1,0:T(8,128)(2,1)} %hidden_rows.1.refs_0_), channel_id=1, source_target_pairs={{0,16},{4,20},{8,24},{12,28},{16,0},{20,4},{24,8},{28,12},{1,17},{... | collective-permute-start | bytes 2396168 | tf_op jit(solution)/shard_map/ppermute | solution.py:149
  41.0 1.6 collective-permute-start.5
  43.9 1.6 %project.3 = (f32[2,8,128]{2,1,0:T(8,128)S(1)}, bf16[2,256,128]{2,1,0:T(8,128)(2,1)S(1)}, bf16[2,256,128]{2,1,0:T(8,128)(2,1)S(1)}, bf16[2,256,128]{2,1,0:T(8,128)(2,1)S(1)}, bf16[2,256,128]{2,1,0:T(8,128)(2,1)S(1)}) custom-call(bf16[1040,384]{1,0:T(8,128)(2,1)S(1)} %copy-done.3, bf16[1040,384]{1,0:T(8,128)(2,1)S(1)} %collective-permute-done.4.refs_1_, ...), custom_call_target="tpu_custom_call" | custom-call | flops 1 | bytes 1 | tf_op jit(solution)/shard_map/project/pallas_call | solution.py:362
  50.2 1.8 %spread_rows.3.refs_4_ = bf16[2,512,1536]{2,1,0:T(8,128)(2,1)S(1)} custom-call(bf16[1040,384]{1,0:T(8,128)(2,1)S(1)} %copy-done.4, bf16[1040,384]{1,0:T(8,128)(2,1)S(1)} %collective-permute-done.4.refs_1_), custom_call_target="tpu_custom_call" | custom-call | flops 1 | bytes 1 | tf_op jit(solution)/shard_map/spread_rows/pallas_call | solution.py:410
  54.9 1.8 %collective-permute-start.12 = (bf16[512,128]{1,0:T(8,128)(2,1)S(1)}, bf16[512,128]{1,0:T(8,128)(2,1)S(1)}, u32[]{:S(2)}, u32[]{:S(2)}) collective-permute-start(bf16[512,128]{1,0:T(8,128)(2,1)S(1)} %get-tuple-element.81.refs_10_), channel_id=1, source_target_pairs={{0,3},{1,2},{2,1},{3,0},{4,7},{5,6},{6,5},{7,4},{8,11},{9,10},{10,... | collective-permute-start | bytes 393224 | tf_op jit(solution)/shard_map/ppermute | solution.py:149
  58.4 19.1 %collective-permute-done.6.refs_2_ = bf16[1040,384]{1,0:T(8,128)(2,1)S(1)} collective-permute-done((bf16[1040,384]{1,0:T(8,128)(2,1)}, bf16[1040,384]{1,0:T(8,128)(2,1)S(1)}, u32[]{:S(2)}, u32[]{:S(2)}) %collective-permute-start.6) | collective-permute-done | bytes 798752 | tf_op jit(solution)/shard_map/ppermute | solution.py:149
  81.3 3.3 %project.4 = (f32[4,8,128]{2,1,0:T(8,128)S(1)}, bf16[4,256,128]{2,1,0:T(8,128)(2,1)S(1)}, bf16[4,256,128]{2,1,0:T(8,128)(2,1)S(1)}, bf16[4,256,128]{2,1,0:T(8,128)(2,1)S(1)}, bf16[4,256,128]{2,1,0:T(8,128)(2,1)S(1)}) custom-call(bf16[1040,384]{1,0:T(8,128)(2,1)S(1)} %collective-permute-done.5.refs_0_, bf16[1040,384]{1,0:T(8,128)(2,1)S(1)} %collective-permute-done.14.refs_1_, ...), custom_call_target="tpu_custom_call" | custom-call | flops 1 | bytes 1 | tf_op jit(solution)/shard_map/project/pallas_call | solution.py:362
  86.3 1.8 %collective-permute-start.18 = (bf16[4,256,128]{2,1,0:T(8,128)(2,1)S(1)}, bf16[4,256,128]{2,1,0:T(8,128)(2,1)S(1)}, u32[]{:S(2)}, u32[]{:S(2)}) collective-permute-start(bf16[4,256,128]{2,1,0:T(8,128)(2,1)S(1)} %get-tuple-element.87), channel_id=1, source_target_pairs={{0,3},{1,2},{2,1},{3,0},{4,7},{5,6},{6,5},{7,4},{8,11},{9,10},{10,... | collective-permute-start | bytes 786440 | tf_op jit(solution)/shard_map/ppermute | solution.py:149
  88.1 3.7 %spread_rows.4.refs_5_ = bf16[4,512,1536]{2,1,0:T(8,128)(2,1)S(1)} custom-call(bf16[1040,384]{1,0:T(8,128)(2,1)S(1)} %collective-permute-done.5.refs_0_, bf16[1040,384]{1,0:T(8,128)(2,1)S(1)} %collective-permute-done.14.refs_1_, bf16[1040,384]{1,0:T(8,128)(2,1)S(1)} %collective-permute-done.6.refs_2_, bf16[1040,384]{1,0:T(8,128)(2,1)S(1)} %collective-permute-done.15.refs_3_), custom_call_target="tpu_custom_call" | custom-call | flops 1 | bytes 1 | tf_op jit(solution)/shard_map/spread_rows/pallas_call | solution.py:410
  91.9 2.6 %copy-done = bf16[4,512,1536]{2,1,0:T(8,128)(2,1)} copy-done((bf16[4,512,1536]{2,1,0:T(8,128)(2,1)}, bf16[4,512,1536]{2,1,0:T(8,128)(2,1)S(1)}, u32[]{:S(2)}) %copy-start) | copy-done | bytes 6291480
  94.5 4.4 %collective-permute-done.18.refs_3_ = bf16[4,256,128]{2,1,0:T(8,128)(2,1)S(1)} collective-permute-done((bf16[4,256,128]{2,1,0:T(8,128)(2,1)S(1)}, bf16[4,256,128]{2,1,0:T(8,128)(2,1)S(1)}, u32[]{:S(2)}, u32[]{:S(2)}) %collective-permute-start.18) | collective-permute-done | bytes 262176 | tf_op jit(solution)/shard_map/ppermute | solution.py:149
  100.8 4.6 %all-to-all-start.1 = ((bf16[8,256,128]{2,1,0:T(8,128)(2,1)}), bf16[8,256,128]{2,1,0:T(8,128)(2,1)S(1)}, u32[]{:S(2)}, u32[]{:S(2)}) async-start(bf16[8,256,128]{2,1,0:T(8,128)(2,1)} %copy-done.5), calls=%async_computation.1 | async-start | bytes 1048576 | tf_op jit(solution)/shard_map/all_to_all | solution.py:694
  105.4 1.6 %project.5 = (f32[2,8,128]{2,1,0:T(8,128)S(1)}, bf16[2,256,128]{2,1,0:T(8,128)(2,1)S(1)}, bf16[2,256,128]{2,1,0:T(8,128)(2,1)S(1)}, bf16[2,256,128]{2,1,0:T(8,128)(2,1)S(1)}, bf16[2,256,128]{2,1,0:T(8,128)(2,1)S(1)}) custom-call(bf16[1040,384]{1,0:T(8,128)(2,1)S(1)} %collective-permute-done.13.refs_0_, ...), custom_call_target="tpu_custom_call" | custom-call | flops 1 | bytes 1 | tf_op jit(solution)/shard_map/project/pallas_call | solution.py:362
  110.6 1.9 %spread_rows.5.refs_6_ = bf16[2,512,1536]{2,1,0:T(8,128)(2,1)S(1)} custom-call(bf16[1040,384]{1,0:T(8,128)(2,1)S(1)} %collective-permute-done.13.refs_0_, bf16[1040,384]{1,0:T(8,128)(2,1)S(1)} %collective-permute-done.19.refs_1_), custom_call_target="tpu_custom_call" | custom-call | flops 1 | bytes 1 | tf_op jit(solution)/shard_map/spread_rows/pallas_call | solution.py:410
  112.5 1.7 %copy-done.2 = bf16[2,512,1536]{2,1,0:T(8,128)(2,1)} copy-done((bf16[2,512,1536]{2,1,0:T(8,128)(2,1)}, bf16[2,512,1536]{2,1,0:T(8,128)(2,1)S(1)}, u32[]{:S(2)}) %copy-start.2) | copy-done | bytes 3145752
  116.6 1.8 %collective-permute-start.34 = (bf16[1536,128]{1,0:T(8,128)(2,1)S(1)}, bf16[1536,128]{1,0:T(8,128)(2,1)S(1)}, u32[]{:S(2)}, u32[]{:S(2)}) collective-permute-start(bf16[1536,128]{1,0:T(8,128)(2,1)S(1)} %get-tuple-element.122.refs_14_), channel_id=1, source_target_pairs={{0,3},{1,2},{2,1},{3,0},{4,7},{5,6},{6,5},{7,4},{8,11},{9,10},{10,... | collective-permute-start | bytes 1179656 | tf_op jit(solution)/shard_map/ppermute | solution.py:149
  121.3 3.5 %collective-permute-start.28 = (f32[8,128]{1,0:T(8,128)S(1)}, f32[8,128]{1,0:T(8,128)S(1)}, u32[]{:S(2)}, u32[]{:S(2)}) collective-permute-start(f32[8,128]{1,0:T(8,128)S(1)} %add.12), channel_id=1, source_target_pairs={{0,24},{4,28},{8,16},{12,20},{16,8},{20,12},{24,0},{28,4},{1,25},{... | collective-permute-start | bytes 12296 | tf_op jit(solution)/shard_map/ppermute | solution.py:149
  124.8 1.9 %collective-permute-done.28 = f32[8,128]{1,0:T(8,128)S(1)} collective-permute-done((f32[8,128]{1,0:T(8,128)S(1)}, f32[8,128]{1,0:T(8,128)S(1)}, u32[]{:S(2)}, u32[]{:S(2)}) %collective-permute-start.28) | collective-permute-done | bytes 4128 | tf_op jit(solution)/shard_map/ppermute | solution.py:149
  126.7 2.6 %collective-permute-done.27 = f32[8,128]{1,0:T(8,128)S(1)} collective-permute-done((f32[8,128]{1,0:T(8,128)S(1)}, f32[8,128]{1,0:T(8,128)S(1)}, u32[]{:S(2)}, u32[]{:S(2)}) %collective-permute-start.27) | collective-permute-done | bytes 4128 | tf_op jit(solution)/shard_map/ppermute | solution.py:149
  130.3 1.7 %collective-permute-start.31 = (f32[8,128]{1,0:T(8,128)S(1)}, f32[8,128]{1,0:T(8,128)S(1)}, u32[]{:S(2)}, u32[]{:S(2)}) collective-permute-start(f32[8,128]{1,0:T(8,128)S(1)} %add_add_fusion.refs_0_), channel_id=1, source_target_pairs={{0,3},{1,2},{2,1},{3,0},{4,7},{5,6},{6,5},{7,4},{8,11},{9,10},{10,... | collective-permute-start | bytes 12296 | tf_op jit(solution)/shard_map/ppermute | solution.py:149
  132.1 3.5 %collective-permute-start.23 = (bf16[256,128]{1,0:T(8,128)(2,1)S(1)}, bf16[256,128]{1,0:T(8,128)(2,1)S(1)}, u32[]{:S(2)}, u32[]{:S(2)}) collective-permute-start(bf16[256,128]{1,0:T(8,128)(2,1)S(1)} %get-tuple-element.113), channel_id=1, source_target_pairs={{0,24},{4,28},{8,16},{12,20},{16,8},{20,12},{24,0},{28,4},{1,25},{... | collective-permute-start | bytes 196616 | tf_op jit(solution)/shard_map/ppermute | solution.py:149
  139.1 3.9 %collective-permute-done.24.refs_1_ = bf16[256,128]{1,0:T(8,128)(2,1)S(1)} collective-permute-done((bf16[256,128]{1,0:T(8,128)(2,1)S(1)}, bf16[256,128]{1,0:T(8,128)(2,1)S(1)}, u32[]{:S(2)}, u32[]{:S(2)}) %collective-permute-start.24) | collective-permute-done | bytes 65568 | tf_op jit(solution)/shard_map/ppermute | solution.py:149
  148.2 9.9 %gradient.1 = (f32[256,4,384]{2,1,0:T(4,128)}, f32[1,64]{1,0:T(1,128)}, f32[1,64]{1,0:T(1,128)}) custom-call(f32[8,128]{1,0:T(8,128)} %copy-done.23, f32[8,128]{1,0:T(8,128)} %copy-done.26, f32[8,128]{1,0:T(8,128)} %copy-done.25, f32[8,128]{1,0:T(8,128)} %copy-done.24, bf16[2,512,1536]{2,1,0:T(8,128)(2,1)} %copy-done.1, bf16[4,512,1536]{2,1,0:T(8,128)(2,1)} %copy-done, ...), custom_call_target="tpu_custom_call" | custom-call | flops 1 | bytes 1 | tf_op jit(solution)/shard_map/gradient/pallas_call | solution.py:605
  (115 shorter events, 38.6 us)
Async XLA Ops:
  2.7 16.5 %collective-permute-start.1 = (bf16[144,2048]{1,0:T(8,128)(2,1)}, bf16[144,2048]{1,0:T(8,128)(2,1)S(1)}, u32[]{:S(2)}, u32[]{:S(2)}) collective-permute-start(bf16[144,2048]{1,0:T(8,128)(2,1)} %pack_tokens.1.own), channel_id=1, source_target_pairs={{0,2},{1,3},{2,0},{3,1},{4,6},{5,7},{6,4},{7,5},{8,10},{9,11},{10,... | collective-permute-start | bytes 1769480 | tf_op jit(solution)/shard_map/ppermute | solution.py:149
  5.7 15.3 %collective-permute-start = (bf16[144,2048]{1,0:T(8,128)(2,1)}, bf16[144,2048]{1,0:T(8,128)(2,1)S(1)}, u32[]{:S(2)}, u32[]{:S(2)}) collective-permute-start(bf16[144,2048]{1,0:T(8,128)(2,1)} %pack_tokens.1.own), channel_id=1, source_target_pairs={{0,1},{1,0},{2,3},{3,2},{4,5},{5,4},{6,7},{7,6},{8,9},{9,8},{10,11... | collective-permute-start | bytes 1769480 | tf_op jit(solution)/shard_map/ppermute | solution.py:149
  9.2 20.2 %all-to-all-start = ((bf16[8,256,128]{2,1,0:T(8,128)(2,1)}), bf16[8,256,128]{2,1,0:T(8,128)(2,1)S(1)}, u32[]{:S(2)}, u32[]{:S(2)}) async-start(bf16[8,256,128]{2,1,0:T(8,128)(2,1)} %bitcast.5), calls=%async_computation | async-start | bytes 1048576 | tf_op jit(solution)/shard_map/all_to_all | solution.py:659
  19.2 10.2 %collective-permute-start.2 = (bf16[80,2048]{1,0:T(8,128)(2,1)S(1)}, bf16[80,2048]{1,0:T(8,128)(2,1)S(1)}, u32[]{:S(2)}, u32[]{:S(2)}) collective-permute-start(bf16[80,2048]{1,0:T(8,128)(2,1)S(1)} %slice.8), channel_id=1, source_target_pairs={{0,1},{1,0},{2,3},{3,2},{4,5},{5,4},{6,7},{7,6},{8,9},{9,8},{10,11... | collective-permute-start | bytes 983048 | tf_op jit(solution)/shard_map/ppermute | solution.py:149
  21.0 8.5 %collective-permute-start.3 = (bf16[80,2048]{1,0:T(8,128)(2,1)S(1)}, bf16[80,2048]{1,0:T(8,128)(2,1)}, u32[]{:S(2)}, u32[]{:S(2)}) collective-permute-start(bf16[80,2048]{1,0:T(8,128)(2,1)S(1)} %slice.9), channel_id=1, source_target_pairs={{0,2},{1,3},{2,0},{3,1},{4,6},{5,7},{6,4},{7,5},{8,10},{9,11},{10,... | collective-permute-start | bytes 983048 | tf_op jit(solution)/shard_map/ppermute | solution.py:149
  38.9 3.8 %collective-permute-start.4 = (bf16[1040,384]{1,0:T(8,128)(2,1)}, bf16[1040,384]{1,0:T(8,128)(2,1)S(1)}, u32[]{:S(2)}, u32[]{:S(2)}) collective-permute-start(bf16[1040,384]{1,0:T(8,128)(2,1)} %hidden_rows.1.refs_0_), channel_id=1, source_target_pairs={{0,4},{4,0},{8,12},{12,8},{16,20},{20,16},{24,28},{28,24},{1,5},{5... | collective-permute-start | bytes 2396168 | tf_op jit(solution)/shard_map/ppermute | solution.py:149
  39.0 38.6 %collective-permute-start.6 = (bf16[1040,384]{1,0:T(8,128)(2,1)}, bf16[1040,384]{1,0:T(8,128)(2,1)S(1)}, u32[]{:S(2)}, u32[]{:S(2)}) collective-permute-start(bf16[1040,384]{1,0:T(8,128)(2,1)} %hidden_rows.1.refs_0_), channel_id=1, source_target_pairs={{0,16},{4,20},{8,24},{12,28},{16,0},{20,4},{24,8},{28,12},{1,17},{... | collective-permute-start | bytes 2396168 | tf_op jit(solution)/shard_map/ppermute | solution.py:149
  41.0 36.7 %collective-permute-start.5 = (bf16[1040,384]{1,0:T(8,128)(2,1)}, bf16[1040,384]{1,0:T(8,128)(2,1)S(1)}, u32[]{:S(2)}, u32[]{:S(2)}) collective-permute-start(bf16[1040,384]{1,0:T(8,128)(2,1)} %hidden_rows.1.refs_0_), channel_id=1, source_target_pairs={{0,8},{4,12},{8,0},{12,4},{16,24},{20,28},{24,16},{28,20},{1,9},{5... | collective-permute-start | bytes 2396168 | tf_op jit(solution)/shard_map/ppermute | solution.py:149
  45.5 6.6 %collective-permute-start.7 = (bf16[2,256,128]{2,1,0:T(8,128)(2,1)S(1)}, bf16[2,256,128]{2,1,0:T(8,128)(2,1)S(1)}, u32[]{:S(2)}, u32[]{:S(2)}) collective-permute-start(bf16[2,256,128]{2,1,0:T(8,128)(2,1)S(1)} %get-tuple-element.72), channel_id=1, source_target_pairs={{0,1},{1,0},{2,3},{3,2},{4,5},{5,4},{6,7},{7,6},{8,9},{9,8},{10,11... | collective-permute-start | bytes 393224 | tf_op jit(solution)/shard_map/ppermute | solution.py:149
  46.7 6.6 %collective-permute-start.8 = (bf16[2,256,128]{2,1,0:T(8,128)(2,1)S(1)}, bf16[2,256,128]{2,1,0:T(8,128)(2,1)S(1)}, u32[]{:S(2)}, u32[]{:S(2)}) collective-permute-start(bf16[2,256,128]{2,1,0:T(8,128)(2,1)S(1)} %get-tuple-element.73), channel_id=1, source_target_pairs={{0,2},{1,3},{2,0},{3,1},{4,6},{5,7},{6,4},{7,5},{8,10},{9,11},{10,... | collective-permute-start | bytes 393224 | tf_op jit(solution)/shard_map/ppermute | solution.py:149
  47.9 6.8 %collective-permute-start.9 = (bf16[2,256,128]{2,1,0:T(8,128)(2,1)S(1)}, bf16[2,256,128]{2,1,0:T(8,128)(2,1)S(1)}, u32[]{:S(2)}, u32[]{:S(2)}) collective-permute-start(bf16[2,256,128]{2,1,0:T(8,128)(2,1)S(1)} %get-tuple-element.74), channel_id=1, source_target_pairs={{0,3},{1,2},{2,1},{3,0},{4,7},{5,6},{6,5},{7,4},{8,11},{9,10},{10,... | collective-permute-start | bytes 393224 | tf_op jit(solution)/shard_map/ppermute | solution.py:149
  54.9 22.9 %collective-permute-start.12 = (bf16[512,128]{1,0:T(8,128)(2,1)S(1)}, bf16[512,128]{1,0:T(8,128)(2,1)S(1)}, u32[]{:S(2)}, u32[]{:S(2)}) collective-permute-start(bf16[512,128]{1,0:T(8,128)(2,1)S(1)} %get-tuple-element.81.refs_10_), channel_id=1, source_target_pairs={{0,3},{1,2},{2,1},{3,0},{4,7},{5,6},{6,5},{7,4},{8,11},{9,10},{10,... | collective-permute-start | bytes 393224 | tf_op jit(solution)/shard_map/ppermute | solution.py:149
  56.7 21.1 %collective-permute-start.11 = (bf16[512,128]{1,0:T(8,128)(2,1)S(1)}, bf16[512,128]{1,0:T(8,128)(2,1)S(1)}, u32[]{:S(2)}, u32[]{:S(2)}) collective-permute-start(bf16[512,128]{1,0:T(8,128)(2,1)S(1)} %get-tuple-element.81.refs_10_), channel_id=1, source_target_pairs={{0,2},{1,3},{2,0},{3,1},{4,6},{5,7},{6,4},{7,5},{8,10},{9,11},{10,... | collective-permute-start | bytes 393224 | tf_op jit(solution)/shard_map/ppermute | solution.py:149
  57.2 20.6 %collective-permute-start.10 = (bf16[512,128]{1,0:T(8,128)(2,1)S(1)}, bf16[512,128]{1,0:T(8,128)(2,1)S(1)}, u32[]{:S(2)}, u32[]{:S(2)}) collective-permute-start(bf16[512,128]{1,0:T(8,128)(2,1)S(1)} %get-tuple-element.81.refs_10_), channel_id=1, source_target_pairs={{0,1},{1,0},{2,3},{3,2},{4,5},{5,4},{6,7},{7,6},{8,9},{9,8},{10,11... | collective-permute-start | bytes 393224 | tf_op jit(solution)/shard_map/ppermute | solution.py:149
  78.4 20.6 %collective-permute-start.13 = (bf16[1040,384]{1,0:T(8,128)(2,1)S(1)}, bf16[1040,384]{1,0:T(8,128)(2,1)S(1)}, u32[]{:S(2)}, u32[]{:S(2)}) collective-permute-start(bf16[1040,384]{1,0:T(8,128)(2,1)S(1)} %collective-permute-done.6.refs_2_), channel_id=1, source_target_pairs={{0,8},{4,12},{8,0},{12,4},{16,24},{20,28},{24,16},{28,20},{1,9},{5... | collective-permute-start | bytes 2396168 | tf_op jit(solution)/shard_map/ppermute | solution.py:149
  84.6 9.9 %collective-permute-start.16 = (bf16[4,256,128]{2,1,0:T(8,128)(2,1)S(1)}, bf16[4,256,128]{2,1,0:T(8,128)(2,1)S(1)}, u32[]{:S(2)}, u32[]{:S(2)}) collective-permute-start(bf16[4,256,128]{2,1,0:T(8,128)(2,1)S(1)} %get-tuple-element.85), channel_id=1, source_target_pairs={{0,1},{1,0},{2,3},{3,2},{4,5},{5,4},{6,7},{7,6},{8,9},{9,8},{10,11... | collective-permute-start | bytes 786440 | tf_op jit(solution)/shard_map/ppermute | solution.py:149
  85.2 9.3 %collective-permute-start.17 = (bf16[4,256,128]{2,1,0:T(8,128)(2,1)S(1)}, bf16[4,256,128]{2,1,0:T(8,128)(2,1)S(1)}, u32[]{:S(2)}, u32[]{:S(2)}) collective-permute-start(bf16[4,256,128]{2,1,0:T(8,128)(2,1)S(1)} %get-tuple-element.86), channel_id=1, source_target_pairs={{0,2},{1,3},{2,0},{3,1},{4,6},{5,7},{6,4},{7,5},{8,10},{9,11},{10,... | collective-permute-start | bytes 786440 | tf_op jit(solution)/shard_map/ppermute | solution.py:149
  86.3 12.6 %collective-permute-start.18 = (bf16[4,256,128]{2,1,0:T(8,128)(2,1)S(1)}, bf16[4,256,128]{2,1,0:T(8,128)(2,1)S(1)}, u32[]{:S(2)}, u32[]{:S(2)}) collective-permute-start(bf16[4,256,128]{2,1,0:T(8,128)(2,1)S(1)} %get-tuple-element.87), channel_id=1, source_target_pairs={{0,3},{1,2},{2,1},{3,0},{4,7},{5,6},{6,5},{7,4},{8,11},{9,10},{10,... | collective-permute-start | bytes 786440 | tf_op jit(solution)/shard_map/ppermute | solution.py:149
  99.0 6.4 %collective-permute-start.19 = (bf16[1040,384]{1,0:T(8,128)(2,1)S(1)}, bf16[1040,384]{1,0:T(8,128)(2,1)S(1)}, u32[]{:S(2)}, u32[]{:S(2)}) collective-permute-start(bf16[1040,384]{1,0:T(8,128)(2,1)S(1)} %collective-permute-done.13.refs_0_), channel_id=1, source_target_pairs={{0,4},{4,0},{8,12},{12,8},{16,20},{20,16},{24,28},{28,24},{1,5},{5... | collective-permute-start | bytes 2396168 | tf_op jit(solution)/shard_map/ppermute | solution.py:149
  100.8 43.4 %all-to-all-start.1 = ((bf16[8,256,128]{2,1,0:T(8,128)(2,1)}), bf16[8,256,128]{2,1,0:T(8,128)(2,1)S(1)}, u32[]{:S(2)}, u32[]{:S(2)}) async-start(bf16[8,256,128]{2,1,0:T(8,128)(2,1)} %copy-done.5), calls=%async_computation.1 | async-start | bytes 1048576 | tf_op jit(solution)/shard_map/all_to_all | solution.py:694
  107.1 7.2 %collective-permute-start.20 = (bf16[2,256,128]{2,1,0:T(8,128)(2,1)S(1)}, bf16[2,256,128]{2,1,0:T(8,128)(2,1)S(1)}, u32[]{:S(2)}, u32[]{:S(2)}) collective-permute-start(bf16[2,256,128]{2,1,0:T(8,128)(2,1)S(1)} %get-tuple-element.103), channel_id=1, source_target_pairs={{0,1},{1,0},{2,3},{3,2},{4,5},{5,4},{6,7},{7,6},{8,9},{9,8},{10,11... | collective-permute-start | bytes 393224 | tf_op jit(solution)/shard_map/ppermute | solution.py:149
  107.9 7.5 %collective-permute-start.21 = (bf16[2,256,128]{2,1,0:T(8,128)(2,1)S(1)}, bf16[2,256,128]{2,1,0:T(8,128)(2,1)S(1)}, u32[]{:S(2)}, u32[]{:S(2)}) collective-permute-start(bf16[2,256,128]{2,1,0:T(8,128)(2,1)S(1)} %get-tuple-element.104), channel_id=1, source_target_pairs={{0,2},{1,3},{2,0},{3,1},{4,6},{5,7},{6,4},{7,5},{8,10},{9,11},{10,... | collective-permute-start | bytes 393224 | tf_op jit(solution)/shard_map/ppermute | solution.py:149
  109.4 6.9 %collective-permute-start.22 = (bf16[2,256,128]{2,1,0:T(8,128)(2,1)S(1)}, bf16[2,256,128]{2,1,0:T(8,128)(2,1)S(1)}, u32[]{:S(2)}, u32[]{:S(2)}) collective-permute-start(bf16[2,256,128]{2,1,0:T(8,128)(2,1)S(1)} %get-tuple-element.105), channel_id=1, source_target_pairs={{0,3},{1,2},{2,1},{3,0},{4,7},{5,6},{6,5},{7,4},{8,11},{9,10},{10,... | collective-permute-start | bytes 393224 | tf_op jit(solution)/shard_map/ppermute | solution.py:149
  116.6 30.0 %collective-permute-start.34 = (bf16[1536,128]{1,0:T(8,128)(2,1)S(1)}, bf16[1536,128]{1,0:T(8,128)(2,1)S(1)}, u32[]{:S(2)}, u32[]{:S(2)}) collective-permute-start(bf16[1536,128]{1,0:T(8,128)(2,1)S(1)} %get-tuple-element.122.refs_14_), channel_id=1, source_target_pairs={{0,3},{1,2},{2,1},{3,0},{4,7},{5,6},{6,5},{7,4},{8,11},{9,10},{10,... | collective-permute-start | bytes 1179656 | tf_op jit(solution)/shard_map/ppermute | solution.py:149
  118.4 28.2 %collective-permute-start.33 = (bf16[1536,128]{1,0:T(8,128)(2,1)S(1)}, bf16[1536,128]{1,0:T(8,128)(2,1)S(1)}, u32[]{:S(2)}, u32[]{:S(2)}) collective-permute-start(bf16[1536,128]{1,0:T(8,128)(2,1)S(1)} %get-tuple-element.122.refs_14_), channel_id=1, source_target_pairs={{0,2},{1,3},{2,0},{3,1},{4,6},{5,7},{6,4},{7,5},{8,10},{9,11},{10,... | collective-permute-start | bytes 1179656 | tf_op jit(solution)/shard_map/ppermute | solution.py:149
  119.3 27.3 %collective-permute-start.32 = (bf16[1536,128]{1,0:T(8,128)(2,1)S(1)}, bf16[1536,128]{1,0:T(8,128)(2,1)S(1)}, u32[]{:S(2)}, u32[]{:S(2)}) collective-permute-start(bf16[1536,128]{1,0:T(8,128)(2,1)S(1)} %get-tuple-element.122.refs_14_), channel_id=1, source_target_pairs={{0,1},{1,0},{2,3},{3,2},{4,5},{5,4},{6,7},{7,6},{8,9},{9,8},{10,11... | collective-permute-start | bytes 1179656 | tf_op jit(solution)/shard_map/ppermute | solution.py:149
  121.3 5.4 %collective-permute-start.28 = (f32[8,128]{1,0:T(8,128)S(1)}, f32[8,128]{1,0:T(8,128)S(1)}, u32[]{:S(2)}, u32[]{:S(2)}) collective-permute-start(f32[8,128]{1,0:T(8,128)S(1)} %add.12), channel_id=1, source_target_pairs={{0,24},{4,28},{8,16},{12,20},{16,8},{20,12},{24,0},{28,4},{1,25},{... | collective-permute-start | bytes 12296 | tf_op jit(solution)/shard_map/ppermute | solution.py:149
  124.8 4.5 %collective-permute-start.27 = (f32[8,128]{1,0:T(8,128)S(1)}, f32[8,128]{1,0:T(8,128)S(1)}, u32[]{:S(2)}, u32[]{:S(2)}) collective-permute-start(f32[8,128]{1,0:T(8,128)S(1)} %add.12), channel_id=1, source_target_pairs={{0,16},{4,20},{8,24},{12,28},{16,0},{20,4},{24,8},{28,12},{1,17},{... | collective-permute-start | bytes 12296 | tf_op jit(solution)/shard_map/ppermute | solution.py:149
  130.3 6.5 %collective-permute-start.31 = (f32[8,128]{1,0:T(8,128)S(1)}, f32[8,128]{1,0:T(8,128)S(1)}, u32[]{:S(2)}, u32[]{:S(2)}) collective-permute-start(f32[8,128]{1,0:T(8,128)S(1)} %add_add_fusion.refs_0_), channel_id=1, source_target_pairs={{0,3},{1,2},{2,1},{3,0},{4,7},{5,6},{6,5},{7,4},{8,11},{9,10},{10,... | collective-permute-start | bytes 12296 | tf_op jit(solution)/shard_map/ppermute | solution.py:149
  132.1 6.1 %collective-permute-start.23 = (bf16[256,128]{1,0:T(8,128)(2,1)S(1)}, bf16[256,128]{1,0:T(8,128)(2,1)S(1)}, u32[]{:S(2)}, u32[]{:S(2)}) collective-permute-start(bf16[256,128]{1,0:T(8,128)(2,1)S(1)} %get-tuple-element.113), channel_id=1, source_target_pairs={{0,24},{4,28},{8,16},{12,20},{16,8},{20,12},{24,0},{28,4},{1,25},{... | collective-permute-start | bytes 196616 | tf_op jit(solution)/shard_map/ppermute | solution.py:149
  136.8 6.2 %collective-permute-start.24 = (bf16[256,128]{1,0:T(8,128)(2,1)S(1)}, bf16[256,128]{1,0:T(8,128)(2,1)S(1)}, u32[]{:S(2)}, u32[]{:S(2)}) collective-permute-start(bf16[256,128]{1,0:T(8,128)(2,1)S(1)} %get-tuple-element.114), channel_id=1, source_target_pairs={{0,28},{4,24},{8,20},{12,16},{16,12},{20,8},{24,4},{28,0},{1,29},{... | collective-permute-start | bytes 196616 | tf_op jit(solution)/shard_map/ppermute | solution.py:149
  138.1 7.1 %collective-permute-start.30 = (f32[8,128]{1,0:T(8,128)S(1)}, f32[8,128]{1,0:T(8,128)S(1)}, u32[]{:S(2)}, u32[]{:S(2)}) collective-permute-start(f32[8,128]{1,0:T(8,128)S(1)} %add_add_fusion.refs_0_), channel_id=1, source_target_pairs={{0,2},{1,3},{2,0},{3,1},{4,6},{5,7},{6,4},{7,5},{8,10},{9,11},{10,... | collective-permute-start | bytes 12296 | tf_op jit(solution)/shard_map/ppermute | solution.py:149
  (32 other events, 310.2 us)

commit v6 on v3

--- a/solution.py
+++ b/solution.py
@@ -242,9 +242,14 @@
 def hidden_kernel(experts, capacity, own, x_side, y_side, upper, lower, *refs):
     w_gate, w_up, out, joined, info, picked, probs, both, arrived = refs
     exp_dev, _, units = w_gate.shape
+    piece = both.shape[1] // 4
     for e in range(exp_dev):
-        pltpu.make_async_copy(w_gate.at[e], both.at[e, :, pl.ds(0, units)], arrived.at[e]).start()
-        pltpu.make_async_copy(w_up.at[e], both.at[e, :, pl.ds(units, units)], arrived.at[e]).start()
+        for k, weights in enumerate((w_gate, w_up)):
+            for p in range(4):
+                lines = pl.ds(p * piece, piece)
+                pltpu.make_async_copy(
+                    weights.at[e, lines], both.at[e, lines, pl.ds(k * units, units)], arrived.at[e]
+                ).start()
     joined[0 : upper.shape[0], :] = upper[...]
     joined[joined.shape[0] - lower.shape[0] :, :] = lower[...]
     tokens = [own, x_side, y_side, joined]

time: 156 us -> 156 us (level)
  no operation moved by 1% of the time
where the time goes in v6:
time: 156 us; the launch traced here: 155 us
  waiting for transfers between devices  59.8 us (38%)
  starting transfers between devices  46.9 us (30%)
  Pallas kernels  35.8 us (23%)
  local copies, waits for them, and re-layouts  12 us (8%)
    ppermute x33, waiting for transfers between devices, swap(): return lax.ppermute(block, axis, [(s, s ^ mask) for s in range(size)])  53 us
    ppermute x33, starting transfers between devices, swap(): return lax.ppermute(block, axis, [(s, s ^ mask) for s in range(size)])  38.1 us
    pallas_call x1, Pallas kernels, gradient(): pl.pallas_call(functools.partial(gradient_kernel, scale, feat_width, exp_...  9.67 us
    unnamed x49, local copies, waits for them, and re-layouts  8.9 us
    pallas_call x1, Pallas kernels, hidden_rows(): pl.pallas_call(functools.partial(hidden_kernel, experts, capacity), in_sp...  8.7 us
    pallas_call x3, Pallas kernels, spread_rows(): pl.pallas_call(functools.partial(spread_kernel, exp_dev, capacity, rows,...  7.42 us
    all_to_all x1, waiting for transfers between devices, feature_plan(): lax.all_to_all(turned.reshape(groups, feats, rows), 'dp', split_axis=0, c...  6.8 us
    pallas_call x3, Pallas kernels, project(): pl.pallas_call(functools.partial(project_kernel, exp_dev, capacity, rows,...  6.55 us
  transfers between devices with their start and end apart: 35, of which 20 were waited for; matrix products, arithmetic and copies ran while one was open for 1% of the time, Pallas kernels for 14%

profile of v6, /device:TPU:0, one launch (start us, length us, event | category | flops | bytes accessed | tf_op | source)
XLA Modules:
  0.0 155.4 jit_solution(11078129907871031256)
XLA Ops:
  0.6 2.0 %pack_tokens.1.own = bf16[144,2048]{1,0:T(8,128)(2,1)} custom-call(bf16[128,2048]{1,0:T(8,128)(2,1)} %tokens.1, s32[8,128]{1,0:T(8,128)} %bitcast.19, f32[8,128]{1,0:T(8,128)} %bitcast.20, s32[8,128]{1,0:T(8,128)} %bitcast.21, s32[1,128]{1,0:T(1,128)} %bitcast.22), custom_call_target="tpu_custom_call" | custom-call | flops 1 | bytes 1 | tf_op jit(solution)/shard_map/pack_tokens/pallas_call | solution.py:231
  2.7 3.0 %collective-permute-start.1 = (bf16[144,2048]{1,0:T(8,128)(2,1)}, bf16[144,2048]{1,0:T(8,128)(2,1)S(1)}, u32[]{:S(2)}, u32[]{:S(2)}) collective-permute-start(bf16[144,2048]{1,0:T(8,128)(2,1)} %pack_tokens.1.own), channel_id=1, source_target_pairs={{0,2},{1,3},{2,0},{3,1},{4,6},{5,7},{6,4},{7,5},{8,10},{9,11},{10,... | collective-permute-start | bytes 1769480 | tf_op jit(solution)/shard_map/ppermute | solution.py:149
  7.1 2.0 %copy.13 = bf16[2048,128]{1,0:T(8,128)(2,1)} copy(bf16[2048,128]{0,1:T(8,128)(2,1)} %bitcast.17) | data formatting | bytes 1048576 | tf_op jit(solution)/shard_map/optimization_barrier | solution.py:634
  9.2 4.9 %all-to-all-start = ((bf16[8,256,128]{2,1,0:T(8,128)(2,1)}), bf16[8,256,128]{2,1,0:T(8,128)(2,1)S(1)}, u32[]{:S(2)}, u32[]{:S(2)}) async-start(bf16[8,256,128]{2,1,0:T(8,128)(2,1)} %bitcast.5), calls=%async_computation | async-start | bytes 1048576 | tf_op jit(solution)/shard_map/all_to_all | solution.py:635
  14.0 5.1 %collective-permute-done.1.y_side = bf16[144,2048]{1,0:T(8,128)(2,1)S(1)} collective-permute-done((bf16[144,2048]{1,0:T(8,128)(2,1)}, bf16[144,2048]{1,0:T(8,128)(2,1)S(1)}, u32[]{:S(2)}, u32[]{:S(2)}) %collective-permute-start.1) | collective-permute-done | bytes 589856 | tf_op jit(solution)/shard_map/ppermute | solution.py:149
  19.2 1.8 %collective-permute-start.2 = (bf16[80,2048]{1,0:T(8,128)(2,1)S(1)}, bf16[80,2048]{1,0:T(8,128)(2,1)S(1)}, u32[]{:S(2)}, u32[]{:S(2)}) collective-permute-start(bf16[80,2048]{1,0:T(8,128)(2,1)S(1)} %slice.8), channel_id=1, source_target_pairs={{0,1},{1,0},{2,3},{3,2},{4,5},{5,4},{6,7},{7,6},{8,9},{9,8},{10,11... | collective-permute-start | bytes 983048 | tf_op jit(solution)/shard_map/ppermute | solution.py:149
  21.0 1.6 %collective-permute-start.3 = (bf16[80,2048]{1,0:T(8,128)(2,1)S(1)}, bf16[80,2048]{1,0:T(8,128)(2,1)}, u32[]{:S(2)}, u32[]{:S(2)}) collective-permute-start(bf16[80,2048]{1,0:T(8,128)(2,1)S(1)} %slice.9), channel_id=1, source_target_pairs={{0,2},{1,3},{2,0},{3,1},{4,6},{5,7},{6,4},{7,5},{8,10},{9,11},{10,... | collective-permute-start | bytes 983048 | tf_op jit(solution)/shard_map/ppermute | solution.py:149
  22.6 6.8 %all-to-all-done.refs_5_.refs_10_ = bf16[8,256,128]{2,1,0:T(8,128)(2,1)S(1)} async-done(((bf16[8,256,128]{2,1,0:T(8,128)(2,1)}), bf16[8,256,128]{2,1,0:T(8,128)(2,1)S(1)}, u32[]{:S(2)}, u32[]{:S(2)}) %all-to-all-start) | async-done | bytes 524320 | tf_op jit(solution)/shard_map/all_to_all | solution.py:635
  30.1 8.7 %hidden_rows.1.refs_0_ = bf16[1040,384]{1,0:T(8,128)(2,1)} custom-call(bf16[144,2048]{1,0:T(8,128)(2,1)} %pack_tokens.1.own, bf16[144,2048]{1,0:T(8,128)(2,1)} %copy-done.11, bf16[144,2048]{1,0:T(8,128)(2,1)} %copy-done.10, bf16[80,2048]{1,0:T(8,128)(2,1)} %copy-done.16, bf16[80,2048]{1,0:T(8,128)(2,1)} %collective-permute-done.3.lower, ...), custom_call_target="tpu_custom_call" | custom-call | flops 1 | bytes 1 | tf_op jit(solution)/shard_map/hidden_rows/pallas_call | solution.py:309
  38.9 2.0 %collective-permute-start.6 = (bf16[1040,384]{1,0:T(8,128)(2,1)}, bf16[1040,384]{1,0:T(8,128)(2,1)S(1)}, u32[]{:S(2)}, u32[]{:S(2)}) collective-permute-start(bf16[1040,384]{1,0:T(8,128)(2,1)} %hidden_rows.1.refs_0_), channel_id=1, source_target_pairs={{0,16},{4,20},{8,24},{12,28},{16,0},{20,4},{24,8},{28,12},{1,17},{... | collective-permute-start | bytes 2396168 | tf_op jit(solution)/shard_map/ppermute | solution.py:149
  43.8 1.6 %project.3 = (f32[2,8,128]{2,1,0:T(8,128)S(1)}, bf16[2,256,128]{2,1,0:T(8,128)(2,1)S(1)}, bf16[2,256,128]{2,1,0:T(8,128)(2,1)S(1)}, bf16[2,256,128]{2,1,0:T(8,128)(2,1)S(1)}, bf16[2,256,128]{2,1,0:T(8,128)(2,1)S(1)}) custom-call(bf16[1040,384]{1,0:T(8,128)(2,1)S(1)} %copy-done.3, bf16[1040,384]{1,0:T(8,128)(2,1)S(1)} %collective-permute-done.4.refs_1_, ...), custom_call_target="tpu_custom_call" | custom-call | flops 1 | bytes 1 | tf_op jit(solution)/shard_map/project/pallas_call | solution.py:367
  50.1 1.8 %spread_rows.3.refs_4_ = bf16[2,512,1536]{2,1,0:T(8,128)(2,1)S(1)} custom-call(bf16[1040,384]{1,0:T(8,128)(2,1)S(1)} %copy-done.4, bf16[1040,384]{1,0:T(8,128)(2,1)S(1)} %collective-permute-done.4.refs_1_), custom_call_target="tpu_custom_call" | custom-call | flops 1 | bytes 1 | tf_op jit(solution)/shard_map/spread_rows/pallas_call | solution.py:415
  54.8 1.8 %collective-permute-start.12 = (bf16[512,128]{1,0:T(8,128)(2,1)S(1)}, bf16[512,128]{1,0:T(8,128)(2,1)S(1)}, u32[]{:S(2)}, u32[]{:S(2)}) collective-permute-start(bf16[512,128]{1,0:T(8,128)(2,1)S(1)} %get-tuple-element.80.refs_10_), channel_id=1, source_target_pairs={{0,3},{1,2},{2,1},{3,0},{4,7},{5,6},{6,5},{7,4},{8,11},{9,10},{10,... | collective-permute-start | bytes 393224 | tf_op jit(solution)/shard_map/ppermute | solution.py:149
  58.3 19.1 %collective-permute-done.6.refs_2_ = bf16[1040,384]{1,0:T(8,128)(2,1)S(1)} collective-permute-done((bf16[1040,384]{1,0:T(8,128)(2,1)}, bf16[1040,384]{1,0:T(8,128)(2,1)S(1)}, u32[]{:S(2)}, u32[]{:S(2)}) %collective-permute-start.6) | collective-permute-done | bytes 798752 | tf_op jit(solution)/shard_map/ppermute | solution.py:149
  81.2 3.3 %project.4 = (f32[4,8,128]{2,1,0:T(8,128)S(1)}, bf16[4,256,128]{2,1,0:T(8,128)(2,1)S(1)}, bf16[4,256,128]{2,1,0:T(8,128)(2,1)S(1)}, bf16[4,256,128]{2,1,0:T(8,128)(2,1)S(1)}, bf16[4,256,128]{2,1,0:T(8,128)(2,1)S(1)}) custom-call(bf16[1040,384]{1,0:T(8,128)(2,1)S(1)} %collective-permute-done.5.refs_0_, bf16[1040,384]{1,0:T(8,128)(2,1)S(1)} %collective-permute-done.14.refs_1_, ...), custom_call_target="tpu_custom_call" | custom-call | flops 1 | bytes 1 | tf_op jit(solution)/shard_map/project/pallas_call | solution.py:367
  86.3 1.8 %collective-permute-start.18 = (bf16[4,256,128]{2,1,0:T(8,128)(2,1)S(1)}, bf16[4,256,128]{2,1,0:T(8,128)(2,1)S(1)}, u32[]{:S(2)}, u32[]{:S(2)}) collective-permute-start(bf16[4,256,128]{2,1,0:T(8,128)(2,1)S(1)} %get-tuple-element.86), channel_id=1, source_target_pairs={{0,3},{1,2},{2,1},{3,0},{4,7},{5,6},{6,5},{7,4},{8,11},{9,10},{10,... | collective-permute-start | bytes 786440 | tf_op jit(solution)/shard_map/ppermute | solution.py:149
  88.1 3.7 %spread_rows.4.refs_5_ = bf16[4,512,1536]{2,1,0:T(8,128)(2,1)S(1)} custom-call(bf16[1040,384]{1,0:T(8,128)(2,1)S(1)} %collective-permute-done.5.refs_0_, bf16[1040,384]{1,0:T(8,128)(2,1)S(1)} %collective-permute-done.14.refs_1_, bf16[1040,384]{1,0:T(8,128)(2,1)S(1)} %collective-permute-done.6.refs_2_, bf16[1040,384]{1,0:T(8,128)(2,1)S(1)} %collective-permute-done.15.refs_3_), custom_call_target="tpu_custom_call" | custom-call | flops 1 | bytes 1 | tf_op jit(solution)/shard_map/spread_rows/pallas_call | solution.py:415
  91.9 2.6 %copy-done = bf16[4,512,1536]{2,1,0:T(8,128)(2,1)} copy-done((bf16[4,512,1536]{2,1,0:T(8,128)(2,1)}, bf16[4,512,1536]{2,1,0:T(8,128)(2,1)S(1)}, u32[]{:S(2)}) %copy-start) | copy-done | bytes 6291480
  94.5 4.4 %collective-permute-done.18.refs_3_ = bf16[4,256,128]{2,1,0:T(8,128)(2,1)S(1)} collective-permute-done((bf16[4,256,128]{2,1,0:T(8,128)(2,1)S(1)}, bf16[4,256,128]{2,1,0:T(8,128)(2,1)S(1)}, u32[]{:S(2)}, u32[]{:S(2)}) %collective-permute-start.18) | collective-permute-done | bytes 262176 | tf_op jit(solution)/shard_map/ppermute | solution.py:149
  98.9 2.3 %collective-permute-done.19.refs_1_ = bf16[1040,384]{1,0:T(8,128)(2,1)S(1)} collective-permute-done((bf16[1040,384]{1,0:T(8,128)(2,1)S(1)}, bf16[1040,384]{1,0:T(8,128)(2,1)S(1)}, u32[]{:S(2)}, u32[]{:S(2)}) %collective-permute-start.19) | collective-permute-done | bytes 798752 | tf_op jit(solution)/shard_map/ppermute | solution.py:149
  101.2 1.6 %project.5 = (f32[2,8,128]{2,1,0:T(8,128)S(1)}, bf16[2,256,128]{2,1,0:T(8,128)(2,1)S(1)}, bf16[2,256,128]{2,1,0:T(8,128)(2,1)S(1)}, bf16[2,256,128]{2,1,0:T(8,128)(2,1)S(1)}, bf16[2,256,128]{2,1,0:T(8,128)(2,1)S(1)}) custom-call(bf16[1040,384]{1,0:T(8,128)(2,1)S(1)} %collective-permute-done.13.refs_0_, ...), custom_call_target="tpu_custom_call" | custom-call | flops 1 | bytes 1 | tf_op jit(solution)/shard_map/project/pallas_call | solution.py:367
  106.4 1.9 %spread_rows.5.refs_6_ = bf16[2,512,1536]{2,1,0:T(8,128)(2,1)S(1)} custom-call(bf16[1040,384]{1,0:T(8,128)(2,1)S(1)} %collective-permute-done.13.refs_0_, bf16[1040,384]{1,0:T(8,128)(2,1)S(1)} %collective-permute-done.19.refs_1_), custom_call_target="tpu_custom_call" | custom-call | flops 1 | bytes 1 | tf_op jit(solution)/shard_map/spread_rows/pallas_call | solution.py:415
  108.2 1.7 %copy-done.2 = bf16[2,512,1536]{2,1,0:T(8,128)(2,1)} copy-done((bf16[2,512,1536]{2,1,0:T(8,128)(2,1)}, bf16[2,512,1536]{2,1,0:T(8,128)(2,1)S(1)}, u32[]{:S(2)}) %copy-start.2) | copy-done | bytes 3145752
  110.0 2.4 %collective-permute-done.21.refs_6_ = bf16[2,256,128]{2,1,0:T(8,128)(2,1)S(1)} collective-permute-done((bf16[2,256,128]{2,1,0:T(8,128)(2,1)S(1)}, bf16[2,256,128]{2,1,0:T(8,128)(2,1)S(1)}, u32[]{:S(2)}, u32[]{:S(2)}) %collective-permute-start.21) | collective-permute-done | bytes 131104 | tf_op jit(solution)/shard_map/ppermute | solution.py:149
  113.6 3.8 %all-to-all-start.1 = ((bf16[8,256,128]{2,1,0:T(8,128)(2,1)}), bf16[8,256,128]{2,1,0:T(8,128)(2,1)S(1)}, u32[]{:S(2)}, u32[]{:S(2)}) async-start(bf16[8,256,128]{2,1,0:T(8,128)(2,1)} %get-tuple-element.108), calls=%async_computation.1 | async-start | bytes 1048576 | tf_op jit(solution)/shard_map/all_to_all | solution.py:677
  117.5 1.7 %collective-permute-start.25 = (f32[8,128]{1,0:T(8,128)S(1)}, f32[8,128]{1,0:T(8,128)S(1)}, u32[]{:S(2)}, u32[]{:S(2)}) collective-permute-start(f32[8,128]{1,0:T(8,128)S(1)} %get-tuple-element.109), channel_id=1, source_target_pairs={{0,3},{1,2},{2,1},{3,0},{4,7},{5,6},{6,5},{7,4},{8,11},{9,10},{10,... | collective-permute-start | bytes 12296 | tf_op jit(solution)/shard_map/ppermute | solution.py:149
  123.8 1.8 %collective-permute-start.32 = (bf16[1536,128]{1,0:T(8,128)(2,1)S(1)}, bf16[1536,128]{1,0:T(8,128)(2,1)S(1)}, u32[]{:S(2)}, u32[]{:S(2)}) collective-permute-start(bf16[1536,128]{1,0:T(8,128)(2,1)S(1)} %get-tuple-element.120.refs_14_), channel_id=1, source_target_pairs={{0,3},{1,2},{2,1},{3,0},{4,7},{5,6},{6,5},{7,4},{8,11},{9,10},{10,... | collective-permute-start | bytes 1179656 | tf_op jit(solution)/shard_map/ppermute | solution.py:149
  128.4 3.8 %collective-permute-start.29 = (f32[8,128]{1,0:T(8,128)S(1)}, f32[8,128]{1,0:T(8,128)S(1)}, u32[]{:S(2)}, u32[]{:S(2)}) collective-permute-start(f32[8,128]{1,0:T(8,128)S(1)} %add.15.refs_0_), channel_id=1, source_target_pairs={{0,24},{4,28},{8,16},{12,20},{16,8},{20,12},{24,0},{28,4},{1,25},{... | collective-permute-start | bytes 12296 | tf_op jit(solution)/shard_map/ppermute | solution.py:149
  132.3 1.6 %collective-permute-done.29.refs_3_ = f32[8,128]{1,0:T(8,128)S(1)} collective-permute-done((f32[8,128]{1,0:T(8,128)S(1)}, f32[8,128]{1,0:T(8,128)S(1)}, u32[]{:S(2)}, u32[]{:S(2)}) %collective-permute-start.29) | collective-permute-done | bytes 4128 | tf_op jit(solution)/shard_map/ppermute | solution.py:149
  134.1 2.7 %collective-permute-done.28.refs_2_ = f32[8,128]{1,0:T(8,128)S(1)} collective-permute-done((f32[8,128]{1,0:T(8,128)S(1)}, f32[8,128]{1,0:T(8,128)S(1)}, u32[]{:S(2)}, u32[]{:S(2)}) %collective-permute-start.28) | collective-permute-done | bytes 4128 | tf_op jit(solution)/shard_map/ppermute | solution.py:149
  137.5 5.7 %collective-permute-done.31.refs_16_ = bf16[1536,128]{1,0:T(8,128)(2,1)S(1)} collective-permute-done((bf16[1536,128]{1,0:T(8,128)(2,1)S(1)}, bf16[1536,128]{1,0:T(8,128)(2,1)S(1)}, u32[]{:S(2)}, u32[]{:S(2)}) %collective-permute-start.31) | collective-permute-done | bytes 393248 | tf_op jit(solution)/shard_map/ppermute | solution.py:149
  144.7 9.7 %gradient.1 = (f32[256,4,384]{2,1,0:T(4,128)}, f32[1,64]{1,0:T(1,128)}, f32[1,64]{1,0:T(1,128)}) custom-call(f32[8,128]{1,0:T(8,128)} %copy-done.20, f32[8,128]{1,0:T(8,128)} %copy-done.23, f32[8,128]{1,0:T(8,128)} %copy-done.22, f32[8,128]{1,0:T(8,128)} %copy-done.21, bf16[2,512,1536]{2,1,0:T(8,128)(2,1)} %copy-done.1, bf16[4,512,1536]{2,1,0:T(8,128)(2,1)} %copy-done, ...), custom_call_target="tpu_custom_call" | custom-call | flops 1 | bytes 1 | tf_op jit(solution)/shard_map/gradient/pallas_call | solution.py:582
  (104 shorter events, 35.5 us)
Async XLA Ops:
  2.7 16.5 %collective-permute-start.1 = (bf16[144,2048]{1,0:T(8,128)(2,1)}, bf16[144,2048]{1,0:T(8,128)(2,1)S(1)}, u32[]{:S(2)}, u32[]{:S(2)}) collective-permute-start(bf16[144,2048]{1,0:T(8,128)(2,1)} %pack_tokens.1.own), channel_id=1, source_target_pairs={{0,2},{1,3},{2,0},{3,1},{4,6},{5,7},{6,4},{7,5},{8,10},{9,11},{10,... | collective-permute-start | bytes 1769480 | tf_op jit(solution)/shard_map/ppermute | solution.py:149
  5.6 15.3 %collective-permute-start = (bf16[144,2048]{1,0:T(8,128)(2,1)}, bf16[144,2048]{1,0:T(8,128)(2,1)S(1)}, u32[]{:S(2)}, u32[]{:S(2)}) collective-permute-start(bf16[144,2048]{1,0:T(8,128)(2,1)} %pack_tokens.1.own), channel_id=1, source_target_pairs={{0,1},{1,0},{2,3},{3,2},{4,5},{5,4},{6,7},{7,6},{8,9},{9,8},{10,11... | collective-permute-start | bytes 1769480 | tf_op jit(solution)/shard_map/ppermute | solution.py:149
  9.2 20.2 %all-to-all-start = ((bf16[8,256,128]{2,1,0:T(8,128)(2,1)}), bf16[8,256,128]{2,1,0:T(8,128)(2,1)S(1)}, u32[]{:S(2)}, u32[]{:S(2)}) async-start(bf16[8,256,128]{2,1,0:T(8,128)(2,1)} %bitcast.5), calls=%async_computation | async-start | bytes 1048576 | tf_op jit(solution)/shard_map/all_to_all | solution.py:635
  19.2 10.2 %collective-permute-start.2 = (bf16[80,2048]{1,0:T(8,128)(2,1)S(1)}, bf16[80,2048]{1,0:T(8,128)(2,1)S(1)}, u32[]{:S(2)}, u32[]{:S(2)}) collective-permute-start(bf16[80,2048]{1,0:T(8,128)(2,1)S(1)} %slice.8), channel_id=1, source_target_pairs={{0,1},{1,0},{2,3},{3,2},{4,5},{5,4},{6,7},{7,6},{8,9},{9,8},{10,11... | collective-permute-start | bytes 983048 | tf_op jit(solution)/shard_map/ppermute | solution.py:149
  21.0 8.5 %collective-permute-start.3 = (bf16[80,2048]{1,0:T(8,128)(2,1)S(1)}, bf16[80,2048]{1,0:T(8,128)(2,1)}, u32[]{:S(2)}, u32[]{:S(2)}) collective-permute-start(bf16[80,2048]{1,0:T(8,128)(2,1)S(1)} %slice.9), channel_id=1, source_target_pairs={{0,2},{1,3},{2,0},{3,1},{4,6},{5,7},{6,4},{7,5},{8,10},{9,11},{10,... | collective-permute-start | bytes 983048 | tf_op jit(solution)/shard_map/ppermute | solution.py:149
  38.8 3.8 %collective-permute-start.4 = (bf16[1040,384]{1,0:T(8,128)(2,1)}, bf16[1040,384]{1,0:T(8,128)(2,1)S(1)}, u32[]{:S(2)}, u32[]{:S(2)}) collective-permute-start(bf16[1040,384]{1,0:T(8,128)(2,1)} %hidden_rows.1.refs_0_), channel_id=1, source_target_pairs={{0,4},{4,0},{8,12},{12,8},{16,20},{20,16},{24,28},{28,24},{1,5},{5... | collective-permute-start | bytes 2396168 | tf_op jit(solution)/shard_map/ppermute | solution.py:149
  38.9 38.6 %collective-permute-start.6 = (bf16[1040,384]{1,0:T(8,128)(2,1)}, bf16[1040,384]{1,0:T(8,128)(2,1)S(1)}, u32[]{:S(2)}, u32[]{:S(2)}) collective-permute-start(bf16[1040,384]{1,0:T(8,128)(2,1)} %hidden_rows.1.refs_0_), channel_id=1, source_target_pairs={{0,16},{4,20},{8,24},{12,28},{16,0},{20,4},{24,8},{28,12},{1,17},{... | collective-permute-start | bytes 2396168 | tf_op jit(solution)/shard_map/ppermute | solution.py:149
  41.0 36.7 %collective-permute-start.5 = (bf16[1040,384]{1,0:T(8,128)(2,1)}, bf16[1040,384]{1,0:T(8,128)(2,1)S(1)}, u32[]{:S(2)}, u32[]{:S(2)}) collective-permute-start(bf16[1040,384]{1,0:T(8,128)(2,1)} %hidden_rows.1.refs_0_), channel_id=1, source_target_pairs={{0,8},{4,12},{8,0},{12,4},{16,24},{20,28},{24,16},{28,20},{1,9},{5... | collective-permute-start | bytes 2396168 | tf_op jit(solution)/shard_map/ppermute | solution.py:149
  45.4 6.6 %collective-permute-start.7 = (bf16[2,256,128]{2,1,0:T(8,128)(2,1)S(1)}, bf16[2,256,128]{2,1,0:T(8,128)(2,1)S(1)}, u32[]{:S(2)}, u32[]{:S(2)}) collective-permute-start(bf16[2,256,128]{2,1,0:T(8,128)(2,1)S(1)} %get-tuple-element.71), channel_id=1, source_target_pairs={{0,1},{1,0},{2,3},{3,2},{4,5},{5,4},{6,7},{7,6},{8,9},{9,8},{10,11... | collective-permute-start | bytes 393224 | tf_op jit(solution)/shard_map/ppermute | solution.py:149
  46.6 6.6 %collective-permute-start.8 = (bf16[2,256,128]{2,1,0:T(8,128)(2,1)S(1)}, bf16[2,256,128]{2,1,0:T(8,128)(2,1)S(1)}, u32[]{:S(2)}, u32[]{:S(2)}) collective-permute-start(bf16[2,256,128]{2,1,0:T(8,128)(2,1)S(1)} %get-tuple-element.72), channel_id=1, source_target_pairs={{0,2},{1,3},{2,0},{3,1},{4,6},{5,7},{6,4},{7,5},{8,10},{9,11},{10,... | collective-permute-start | bytes 393224 | tf_op jit(solution)/shard_map/ppermute | solution.py:149
  47.8 6.8 %collective-permute-start.9 = (bf16[2,256,128]{2,1,0:T(8,128)(2,1)S(1)}, bf16[2,256,128]{2,1,0:T(8,128)(2,1)S(1)}, u32[]{:S(2)}, u32[]{:S(2)}) collective-permute-start(bf16[2,256,128]{2,1,0:T(8,128)(2,1)S(1)} %get-tuple-element.73), channel_id=1, source_target_pairs={{0,3},{1,2},{2,1},{3,0},{4,7},{5,6},{6,5},{7,4},{8,11},{9,10},{10,... | collective-permute-start | bytes 393224 | tf_op jit(solution)/shard_map/ppermute | solution.py:149
  54.8 22.9 %collective-permute-start.12 = (bf16[512,128]{1,0:T(8,128)(2,1)S(1)}, bf16[512,128]{1,0:T(8,128)(2,1)S(1)}, u32[]{:S(2)}, u32[]{:S(2)}) collective-permute-start(bf16[512,128]{1,0:T(8,128)(2,1)S(1)} %get-tuple-element.80.refs_10_), channel_id=1, source_target_pairs={{0,3},{1,2},{2,1},{3,0},{4,7},{5,6},{6,5},{7,4},{8,11},{9,10},{10,... | collective-permute-start | bytes 393224 | tf_op jit(solution)/shard_map/ppermute | solution.py:149
  56.6 21.1 %collective-permute-start.11 = (bf16[512,128]{1,0:T(8,128)(2,1)S(1)}, bf16[512,128]{1,0:T(8,128)(2,1)S(1)}, u32[]{:S(2)}, u32[]{:S(2)}) collective-permute-start(bf16[512,128]{1,0:T(8,128)(2,1)S(1)} %get-tuple-element.80.refs_10_), channel_id=1, source_target_pairs={{0,2},{1,3},{2,0},{3,1},{4,6},{5,7},{6,4},{7,5},{8,10},{9,11},{10,... | collective-permute-start | bytes 393224 | tf_op jit(solution)/shard_map/ppermute | solution.py:149
  57.1 20.6 %collective-permute-start.10 = (bf16[512,128]{1,0:T(8,128)(2,1)S(1)}, bf16[512,128]{1,0:T(8,128)(2,1)S(1)}, u32[]{:S(2)}, u32[]{:S(2)}) collective-permute-start(bf16[512,128]{1,0:T(8,128)(2,1)S(1)} %get-tuple-element.80.refs_10_), channel_id=1, source_target_pairs={{0,1},{1,0},{2,3},{3,2},{4,5},{5,4},{6,7},{7,6},{8,9},{9,8},{10,11... | collective-permute-start | bytes 393224 | tf_op jit(solution)/shard_map/ppermute | solution.py:149
  77.8 3.4 %collective-permute-start.15 = (bf16[1040,384]{1,0:T(8,128)(2,1)S(1)}, bf16[1040,384]{1,0:T(8,128)(2,1)S(1)}, u32[]{:S(2)}, u32[]{:S(2)}) collective-permute-start(bf16[1040,384]{1,0:T(8,128)(2,1)S(1)} %collective-permute-done.6.refs_2_), channel_id=1, source_target_pairs={{0,4},{4,0},{8,12},{12,8},{16,20},{20,16},{24,28},{28,24},{1,5},{5... | collective-permute-start | bytes 2396168 | tf_op jit(solution)/shard_map/ppermute | solution.py:149
  78.3 20.6 %collective-permute-start.13 = (bf16[1040,384]{1,0:T(8,128)(2,1)S(1)}, bf16[1040,384]{1,0:T(8,128)(2,1)S(1)}, u32[]{:S(2)}, u32[]{:S(2)}) collective-permute-start(bf16[1040,384]{1,0:T(8,128)(2,1)S(1)} %collective-permute-done.6.refs_2_), channel_id=1, source_target_pairs={{0,8},{4,12},{8,0},{12,4},{16,24},{20,28},{24,16},{28,20},{1,9},{5... | collective-permute-start | bytes 2396168 | tf_op jit(solution)/shard_map/ppermute | solution.py:149
  84.5 10.0 %collective-permute-start.16 = (bf16[4,256,128]{2,1,0:T(8,128)(2,1)S(1)}, bf16[4,256,128]{2,1,0:T(8,128)(2,1)S(1)}, u32[]{:S(2)}, u32[]{:S(2)}) collective-permute-start(bf16[4,256,128]{2,1,0:T(8,128)(2,1)S(1)} %get-tuple-element.84), channel_id=1, source_target_pairs={{0,1},{1,0},{2,3},{3,2},{4,5},{5,4},{6,7},{7,6},{8,9},{9,8},{10,11... | collective-permute-start | bytes 786440 | tf_op jit(solution)/shard_map/ppermute | solution.py:149
  85.1 9.4 %collective-permute-start.17 = (bf16[4,256,128]{2,1,0:T(8,128)(2,1)S(1)}, bf16[4,256,128]{2,1,0:T(8,128)(2,1)S(1)}, u32[]{:S(2)}, u32[]{:S(2)}) collective-permute-start(bf16[4,256,128]{2,1,0:T(8,128)(2,1)S(1)} %get-tuple-element.85), channel_id=1, source_target_pairs={{0,2},{1,3},{2,0},{3,1},{4,6},{5,7},{6,4},{7,5},{8,10},{9,11},{10,... | collective-permute-start | bytes 786440 | tf_op jit(solution)/shard_map/ppermute | solution.py:149
  86.3 12.6 %collective-permute-start.18 = (bf16[4,256,128]{2,1,0:T(8,128)(2,1)S(1)}, bf16[4,256,128]{2,1,0:T(8,128)(2,1)S(1)}, u32[]{:S(2)}, u32[]{:S(2)}) collective-permute-start(bf16[4,256,128]{2,1,0:T(8,128)(2,1)S(1)} %get-tuple-element.86), channel_id=1, source_target_pairs={{0,3},{1,2},{2,1},{3,0},{4,7},{5,6},{6,5},{7,4},{8,11},{9,10},{10,... | collective-permute-start | bytes 786440 | tf_op jit(solution)/shard_map/ppermute | solution.py:149
  102.8 7.2 %collective-permute-start.20 = (bf16[2,256,128]{2,1,0:T(8,128)(2,1)S(1)}, bf16[2,256,128]{2,1,0:T(8,128)(2,1)S(1)}, u32[]{:S(2)}, u32[]{:S(2)}) collective-permute-start(bf16[2,256,128]{2,1,0:T(8,128)(2,1)S(1)} %get-tuple-element.97), channel_id=1, source_target_pairs={{0,1},{1,0},{2,3},{3,2},{4,5},{5,4},{6,7},{7,6},{8,9},{9,8},{10,11... | collective-permute-start | bytes 393224 | tf_op jit(solution)/shard_map/ppermute | solution.py:149
  104.3 8.1 %collective-permute-start.21 = (bf16[2,256,128]{2,1,0:T(8,128)(2,1)S(1)}, bf16[2,256,128]{2,1,0:T(8,128)(2,1)S(1)}, u32[]{:S(2)}, u32[]{:S(2)}) collective-permute-start(bf16[2,256,128]{2,1,0:T(8,128)(2,1)S(1)} %get-tuple-element.98), channel_id=1, source_target_pairs={{0,2},{1,3},{2,0},{3,1},{4,6},{5,7},{6,4},{7,5},{8,10},{9,11},{10,... | collective-permute-start | bytes 393224 | tf_op jit(solution)/shard_map/ppermute | solution.py:149
  105.2 7.2 %collective-permute-start.22 = (bf16[2,256,128]{2,1,0:T(8,128)(2,1)S(1)}, bf16[2,256,128]{2,1,0:T(8,128)(2,1)S(1)}, u32[]{:S(2)}, u32[]{:S(2)}) collective-permute-start(bf16[2,256,128]{2,1,0:T(8,128)(2,1)S(1)} %get-tuple-element.99), channel_id=1, source_target_pairs={{0,3},{1,2},{2,1},{3,0},{4,7},{5,6},{6,5},{7,4},{8,11},{9,10},{10,... | collective-permute-start | bytes 393224 | tf_op jit(solution)/shard_map/ppermute | solution.py:149
  113.6 40.8 %all-to-all-start.1 = ((bf16[8,256,128]{2,1,0:T(8,128)(2,1)}), bf16[8,256,128]{2,1,0:T(8,128)(2,1)S(1)}, u32[]{:S(2)}, u32[]{:S(2)}) async-start(bf16[8,256,128]{2,1,0:T(8,128)(2,1)} %get-tuple-element.108), calls=%async_computation.1 | async-start | bytes 1048576 | tf_op jit(solution)/shard_map/all_to_all | solution.py:677
  117.5 4.5 %collective-permute-start.25 = (f32[8,128]{1,0:T(8,128)S(1)}, f32[8,128]{1,0:T(8,128)S(1)}, u32[]{:S(2)}, u32[]{:S(2)}) collective-permute-start(f32[8,128]{1,0:T(8,128)S(1)} %get-tuple-element.109), channel_id=1, source_target_pairs={{0,3},{1,2},{2,1},{3,0},{4,7},{5,6},{6,5},{7,4},{8,11},{9,10},{10,... | collective-permute-start | bytes 12296 | tf_op jit(solution)/shard_map/ppermute | solution.py:149
  119.2 3.6 %collective-permute-start.24 = (f32[8,128]{1,0:T(8,128)S(1)}, f32[8,128]{1,0:T(8,128)S(1)}, u32[]{:S(2)}, u32[]{:S(2)}) collective-permute-start(f32[8,128]{1,0:T(8,128)S(1)} %get-tuple-element.109), channel_id=1, source_target_pairs={{0,2},{1,3},{2,0},{3,1},{4,6},{5,7},{6,4},{7,5},{8,10},{9,11},{10,... | collective-permute-start | bytes 12296 | tf_op jit(solution)/shard_map/ppermute | solution.py:149
  120.2 3.6 %collective-permute-start.23 = (f32[8,128]{1,0:T(8,128)S(1)}, f32[8,128]{1,0:T(8,128)S(1)}, u32[]{:S(2)}, u32[]{:S(2)}) collective-permute-start(f32[8,128]{1,0:T(8,128)S(1)} %get-tuple-element.109), channel_id=1, source_target_pairs={{0,1},{1,0},{2,3},{3,2},{4,5},{5,4},{6,7},{7,6},{8,9},{9,8},{10,11... | collective-permute-start | bytes 12296 | tf_op jit(solution)/shard_map/ppermute | solution.py:149
  123.8 13.7 %collective-permute-start.32 = (bf16[1536,128]{1,0:T(8,128)(2,1)S(1)}, bf16[1536,128]{1,0:T(8,128)(2,1)S(1)}, u32[]{:S(2)}, u32[]{:S(2)}) collective-permute-start(bf16[1536,128]{1,0:T(8,128)(2,1)S(1)} %get-tuple-element.120.refs_14_), channel_id=1, source_target_pairs={{0,3},{1,2},{2,1},{3,0},{4,7},{5,6},{6,5},{7,4},{8,11},{9,10},{10,... | collective-permute-start | bytes 1179656 | tf_op jit(solution)/shard_map/ppermute | solution.py:149
  125.5 17.7 %collective-permute-start.31 = (bf16[1536,128]{1,0:T(8,128)(2,1)S(1)}, bf16[1536,128]{1,0:T(8,128)(2,1)S(1)}, u32[]{:S(2)}, u32[]{:S(2)}) collective-permute-start(bf16[1536,128]{1,0:T(8,128)(2,1)S(1)} %get-tuple-element.120.refs_14_), channel_id=1, source_target_pairs={{0,2},{1,3},{2,0},{3,1},{4,6},{5,7},{6,4},{7,5},{8,10},{9,11},{10,... | collective-permute-start | bytes 1179656 | tf_op jit(solution)/shard_map/ppermute | solution.py:149
  126.0 17.2 %collective-permute-start.30 = (bf16[1536,128]{1,0:T(8,128)(2,1)S(1)}, bf16[1536,128]{1,0:T(8,128)(2,1)S(1)}, u32[]{:S(2)}, u32[]{:S(2)}) collective-permute-start(bf16[1536,128]{1,0:T(8,128)(2,1)S(1)} %get-tuple-element.120.refs_14_), channel_id=1, source_target_pairs={{0,1},{1,0},{2,3},{3,2},{4,5},{5,4},{6,7},{7,6},{8,9},{9,8},{10,11... | collective-permute-start | bytes 1179656 | tf_op jit(solution)/shard_map/ppermute | solution.py:149
  128.4 5.4 %collective-permute-start.29 = (f32[8,128]{1,0:T(8,128)S(1)}, f32[8,128]{1,0:T(8,128)S(1)}, u32[]{:S(2)}, u32[]{:S(2)}) collective-permute-start(f32[8,128]{1,0:T(8,128)S(1)} %add.15.refs_0_), channel_id=1, source_target_pairs={{0,24},{4,28},{8,16},{12,20},{16,8},{20,12},{24,0},{28,4},{1,25},{... | collective-permute-start | bytes 12296 | tf_op jit(solution)/shard_map/ppermute | solution.py:149
  132.3 4.5 %collective-permute-start.28 = (f32[8,128]{1,0:T(8,128)S(1)}, f32[8,128]{1,0:T(8,128)S(1)}, u32[]{:S(2)}, u32[]{:S(2)}) collective-permute-start(f32[8,128]{1,0:T(8,128)S(1)} %add.15.refs_0_), channel_id=1, source_target_pairs={{0,16},{4,20},{8,24},{12,28},{16,0},{20,4},{24,8},{28,12},{1,17},{... | collective-permute-start | bytes 12296 | tf_op jit(solution)/shard_map/ppermute | solution.py:149
  133.8 3.6 %collective-permute-start.27 = (f32[8,128]{1,0:T(8,128)S(1)}, f32[8,128]{1,0:T(8,128)S(1)}, u32[]{:S(2)}, u32[]{:S(2)}) collective-permute-start(f32[8,128]{1,0:T(8,128)S(1)} %add.15.refs_0_), channel_id=1, source_target_pairs={{0,8},{4,12},{8,0},{12,4},{16,24},{20,28},{24,16},{28,20},{1,9},{5... | collective-permute-start | bytes 12296 | tf_op jit(solution)/shard_map/ppermute | solution.py:149
  (27 other events, 355.4 us)
